TPU v7x, 32 devices: a whole 2x2x4 slice. The times are simulated.
32 devices in a mesh: group: 2 (over y), lon: 4 (over z), lat: 2 (over x), section: 2 (over core).
Axes of the slice: x: 2, y: 2, z: 4, core: 2. Of those that a mesh axis runs over, the one named last changes fastest.
Arguments:
- saved_inputs: bfloat16 [2, 4, 16, 64, 256], P('section', 'group', 'lat', 'lon'), parts along dimension 1, may hold values from -6 to 6
- out_cotangent: bfloat16 [4, 16, 64, 256], P('group', 'lat', 'lon'), parts along dimension 0, may hold values from -6 to 6
- land_mask: int32 [16, 64], P('lat', 'lon'), may hold values 0 or 1
- conv_kernel: bfloat16 [2, 7, 7, 256], P('section'), may hold values from -0.875 to 0.875
- conv_bias: float32 [2, 256], P('section'), may hold values from -3 to 3
- norm_gain: float32 [2, 256], P('section'), may hold values from 0.4 to 2.5
- w_in: bfloat16 [2, 256, 1024], P('section'), may hold values from -0.375 to 0.375
- b_in: float32 [2, 1024], P('section'), may hold values from -4 to 4
- w_out: bfloat16 [2, 1024, 256], P('section'), may hold values from -0.1875 to 0.1875
Outputs:
- input_grads: bfloat16 [2, 4, 16, 64, 256], P('section', 'group', 'lat', 'lon'), parts along dimension 1
- grad_w_in: float32 [2, 512, 1024], P('section', 'group'), parts along dimension 1
- grad_w_out: float32 [2, 2048, 256], P('section', 'group'), parts along dimension 1
- grad_kernel: float32 [2, 98, 256], P('section', 'group'), parts along dimension 1
There are 2 independent parts, one for each index of `group`. A program takes and returns all parts, laid end to end along the dimension named above; an argument that names none is the same for every part. Nothing has to cross between parts.
All inputs are finite; a program needn't handle non-finite values. No bound on the sum of `land_mask` on one device may be relied on, other than what follows from the above.
Results may differ from a plain program's by a relative error of at most 0.01.
Values may be sent and summed in bfloat16 or wider, within the bound.
No kernel may reach another device: no remote copies, remote signals or barrier semaphores. Data moves between devices by JAX's collectives and lax.ppermute only.
A program may use at most 64 MiB of HBM per device.

v0:
```python
import jax
import jax.numpy as jnp
from jax import lax
from jax.sharding import PartitionSpec as P

gelu_k = 0.7978845608028654
gelu_c = 0.044715


def extended(block, sides, width, periodic):
    for axis, dim in sides:
        count = lax.axis_size(axis)
        forward = [(i, i + 1) for i in range(count - 1)]
        if periodic:
            forward.append((count - 1, 0))
        backward = [(target, source) for source, target in forward]
        low = lax.ppermute(
            lax.slice_in_dim(block, block.shape[dim] - width, None, axis=dim), axis, forward
        )
        high = lax.ppermute(lax.slice_in_dim(block, 0, width, axis=dim), axis, backward)
        block = jnp.concatenate([low, block, high], axis=dim)
    return block


def shifted(value, axis, steps):
    count = lax.axis_size(axis)
    initial, last = (max(0, -steps), min(count, count - steps))
    return lax.ppermute(value, axis, [(source, source + steps) for source in range(initial, last)])


def gelu_value(h):
    return 0.5 * h * (1.0 + jnp.tanh(gelu_k * (h + gelu_c * h * h * h)))


def gelu_slope(h):
    tval = jnp.tanh(gelu_k * (h + gelu_c * h * h * h))
    return 0.5 * (1.0 + tval) + 0.5 * h * (1.0 - tval * tval) * gelu_k * (
        1.0 + 3.0 * gelu_c * h * h
    )


def depthwise(padded, kernel, rows, cols):
    kern = kernel.astype(jnp.float32)
    source = padded.astype(jnp.float32)
    total = jnp.zeros((rows, cols, source.shape[2]), jnp.float32)
    for ka in range(7):
        for kb in range(7):
            total = total + source[ka : ka + rows, kb : kb + cols] * kern[ka, kb]
    return total


def widen_input(field):
    rows_wide = extended(field, (("lat", 0),), 3, False)
    return extended(rows_wide, (("lon", 1),), 3, True)


def widen_dz(field):
    rows_wide = extended(field, (("lat", 0),), 3, False)
    return extended(rows_wide, (("lon", 1),), 3, True)


def dense_part(padded, masked, rows, cols, kernel, bias, gain, weight_in, bias_in, weight_out):
    chans = padded.shape[2]
    zval = depthwise(padded, kernel, rows, cols) + bias
    centred = zval - jnp.mean(zval, axis=-1, keepdims=True)
    rscale = lax.rsqrt(jnp.mean(centred * centred, axis=-1, keepdims=True) + 1e-06)
    zhat = centred * rscale
    normed = (zhat * gain).astype(jnp.bfloat16).reshape(-1, chans)
    hidden = jnp.dot(normed, weight_in, preferred_element_type=jnp.float32) + bias_in
    act = gelu_value(hidden).astype(jnp.bfloat16)
    flat_g = masked.reshape(-1, chans)
    dact = jnp.dot(flat_g, weight_out.T, preferred_element_type=jnp.float32)
    dhid = (dact * gelu_slope(hidden)).astype(jnp.bfloat16)
    dnorm = jnp.dot(dhid, weight_in.T, preferred_element_type=jnp.float32).reshape(
        rows, cols, chans
    )
    dzh = dnorm * gain
    dzval = rscale * (
        dzh
        - jnp.mean(dzh, axis=-1, keepdims=True)
        - zhat * jnp.mean(dzh * zhat, axis=-1, keepdims=True)
    )
    return (
        dzval.astype(jnp.bfloat16),
        normed.reshape(rows, cols, chans),
        act.reshape(rows, cols, -1),
        dhid.reshape(rows, cols, -1),
    )


def contract_cells(left, right):
    return lax.dot_general(
        left, right, (((0,), (0,)), ((), ())), preferred_element_type=jnp.float32
    )


def local_backward(field, cot, maskf, kernel, bias, gain, weight_in, bias_in, weight_out):
    rows, cols, chans = field.shape
    masked = (cot.astype(jnp.float32) * maskf).astype(jnp.bfloat16)
    padded = widen_input(field)
    dzval, normed, act, dhid = dense_part(
        padded, masked, rows, cols, kernel, bias, gain, weight_in, bias_in, weight_out
    )
    dz_wide = widen_dz(dzval)
    flat_g = masked.reshape(-1, chans)
    grad_out = contract_cells(act.reshape(rows * cols, -1), flat_g)
    grad_in = contract_cells(normed.reshape(rows * cols, chans), dhid.reshape(rows * cols, -1))
    dz32 = dzval.astype(jnp.float32)
    src32 = padded.astype(jnp.float32)
    kgrads = []
    for ka in range(7):
        for kb in range(7):
            kgrads.append(jnp.sum(dz32 * src32[ka : ka + rows, kb : kb + cols], axis=(0, 1)))
    grad_k = jnp.stack(kgrads)
    back = depthwise(dz_wide, kernel[::-1, ::-1], rows, cols)
    dfield = (masked.astype(jnp.float32) + back).astype(jnp.bfloat16)
    return (dfield, grad_in, grad_out, grad_k)


def run_relay(
    saved_inputs,
    out_cotangent,
    maskf,
    conv_kernel,
    conv_bias,
    norm_gain,
    w_in,
    b_in,
    w_out,
    section_id,
):
    micro_count, rows, cols, chans = out_cotangent.shape
    hidden_width = w_in.shape[2]
    kernel = conv_kernel[0]
    bias = conv_bias[0]
    gain = norm_gain[0]
    weight_in = w_in[0]
    bias_in = b_in[0]
    weight_out = w_out[0]
    saved = saved_inputs[0]
    sum_in = jnp.zeros((chans, hidden_width), jnp.float32)
    sum_out = jnp.zeros((hidden_width, chans), jnp.float32)
    sum_k = jnp.zeros((49, chans), jnp.float32)
    results = jnp.zeros((micro_count, rows, cols, chans), jnp.bfloat16)
    received = jnp.zeros((rows, cols, chans), jnp.bfloat16)
    for rnd in range(micro_count + 1):
        micro = rnd - 1 + section_id
        valid = jnp.logical_and(micro >= 0, micro < micro_count)
        clamped = jnp.clip(micro, 0, micro_count - 1)
        field = lax.dynamic_index_in_dim(saved, clamped, 0, keepdims=False)
        own_cot = lax.dynamic_index_in_dim(out_cotangent, clamped, 0, keepdims=False)
        cot = jnp.where(section_id == 1, own_cot, received)
        dfield, grad_in, grad_out, grad_k = local_backward(
            field, cot, maskf, kernel, bias, gain, weight_in, bias_in, weight_out
        )
        sum_in = sum_in + jnp.where(valid, grad_in, 0.0)
        sum_out = sum_out + jnp.where(valid, grad_out, 0.0)
        sum_k = sum_k + jnp.where(valid, grad_k, 0.0)
        current = lax.dynamic_index_in_dim(results, clamped, 0, keepdims=True)
        update = jnp.where(valid, dfield[None], current)
        results = lax.dynamic_update_slice_in_dim(results, update, clamped, 0)
        if rnd < micro_count:
            received = shifted(dfield, "section", -1)
    total_in, total_out, total_k = lax.psum((sum_in, sum_out, sum_k), ("lon", "lat"))
    return (results[None], total_in, total_out, total_k)


def shards(
    saved_inputs, out_cotangent, land_mask, conv_kernel, conv_bias, norm_gain, w_in, b_in, w_out
):
    micro_count, rows, cols, chans = out_cotangent.shape
    section_id = lax.axis_index("section")
    maskf = land_mask.astype(jnp.float32)[:, :, None]
    results, total_in, total_out, total_k = run_relay(
        saved_inputs,
        out_cotangent,
        maskf,
        conv_kernel,
        conv_bias,
        norm_gain,
        w_in,
        b_in,
        w_out,
        section_id,
    )
    factor = 1.0 / (micro_count * rows * lax.axis_size("lat") * cols * lax.axis_size("lon")) ** 0.5
    return (
        results,
        (total_in * factor)[None],
        (total_out * factor)[None],
        (total_k * factor)[None],
    )


def solution(mesh):
    in_specs = (
        P("section", "group", "lat", "lon", None),
        P("group", "lat", "lon", None),
        P("lat", "lon"),
        P("section", None, None, None),
        P("section", None),
        P("section", None),
        P("section", None, None),
        P("section", None),
        P("section", None, None),
    )
    out_specs = (
        P("section", "group", "lat", "lon", None),
        P("section", "group", None),
        P("section", "group", None),
        P("section", "group", None),
    )
    return jax.shard_map(shards, mesh=mesh, in_specs=in_specs, out_specs=out_specs, check_vma=False)
```

profile of v0, /device:TPU:0, one launch (start us, length us, event | category | flops | bytes accessed | tf_op | source)
XLA Modules:
  0.0 224.7 jit_solution(6471024829686266573)
XLA Ops:
  8.1 4.8 %collective-permute-start.18 = (bf16[3,16,256]{2,1,0:T(8,128)(2,1)S(1)}, bf16[3,16,256]{2,1,0:T(8,128)(2,1)S(1)}, u32[]{:S(2)}, u32[]{:S(2)}) collective-permute-start(bf16[3,16,256]{2,1,0:T(8,128)(2,1)S(1)} %get-tuple-element.172), channel_id=1, source_target_pairs={{0,2},{1,3},{4,6},{5,7},{8,10},{9,11},{12,14},{13,15},{16,18},{17,... | collective-permute-start | bytes 73736 | tf_op jit(solution)/shard_map/ppermute | solution.py:17
  13.0 1.3 collective-permute-start.19
  14.3 1.3 collective-permute-start.10
  15.6 4.5 %collective-permute-start.9 = (bf16[3,16,256]{2,1,0:T(8,128)(2,1)S(1)}, bf16[3,16,256]{2,1,0:T(8,128)(2,1)S(1)}, u32[]{:S(2)}, u32[]{:S(2)}) collective-permute-start(bf16[3,16,256]{2,1,0:T(8,128)(2,1)S(1)} %get-tuple-element.175), channel_id=1, source_target_pairs={{0,2},{1,3},{4,6},{5,7},{8,10},{9,11},{12,14},{13,15},{16,18},{17,... | collective-permute-start | bytes 73736 | tf_op jit(solution)/shard_map/ppermute | solution.py:17
  20.1 1.3 collective-permute-start.1
  25.3 4.5 %collective-permute-start = (bf16[3,16,256]{2,1,0:T(8,128)(2,1)S(1)}, bf16[3,16,256]{2,1,0:T(8,128)(2,1)S(1)}, u32[]{:S(2)}, u32[]{:S(2)}) collective-permute-start(bf16[3,16,256]{2,1,0:T(8,128)(2,1)S(1)} %get-tuple-element.177), channel_id=1, source_target_pairs={{0,2},{1,3},{4,6},{5,7},{8,10},{9,11},{12,14},{13,15},{16,18},{17,... | collective-permute-start | bytes 73736 | tf_op jit(solution)/shard_map/ppermute | solution.py:17
  29.9 1.6 collective-permute-start.20
  31.6 2.2 %collective-permute-start.21 = (bf16[14,3,256]{2,1,0:T(4,128)(2,1)S(1)}, bf16[14,3,256]{2,1,0:T(4,128)(2,1)S(1)}, u32[]{:S(2)}, u32[]{:S(2)}) collective-permute-start(bf16[14,3,256]{2,1,0:T(4,128)(2,1)S(1)} %get-tuple-element.184), channel_id=1, source_target_pairs={{4,0},{8,4},{12,8},{0,12},{5,1},{9,5},{13,9},{1,13},{6,2},{10,6},{... | collective-permute-start | bytes 64520 | tf_op jit(solution)/shard_map/ppermute | solution.py:20
  33.9 3.8 %collective-permute-start.12 = (bf16[14,3,256]{2,1,0:T(4,128)(2,1)S(1)}, bf16[14,3,256]{2,1,0:T(4,128)(2,1)S(1)}, u32[]{:S(2)}, u32[]{:S(2)}) collective-permute-start(bf16[14,3,256]{2,1,0:T(4,128)(2,1)S(1)} %get-tuple-element.188), channel_id=1, source_target_pairs={{4,0},{8,4},{12,8},{0,12},{5,1},{9,5},{13,9},{1,13},{6,2},{10,6},{... | collective-permute-start | bytes 64520 | tf_op jit(solution)/shard_map/ppermute | solution.py:20
  37.8 1.8 collective-permute-done.11
  39.7 2.0 collective-permute-start.3
  43.8 0.9 fusion.362
  45.1 0.9 fusion.358
  48.5 1.0 copy-done.201
  50.4 1.0 fusion.90
  51.4 1.3 collective-permute-start.4
  52.7 1.4 collective-permute-start.5
  54.5 1.4 convolution_select_fusion.2
  55.8 1.0 convolution_add_fusion
  56.9 1.7 collective-permute-done.5
  58.7 3.8 %collective-permute-start.7 = (bf16[14,3,256]{2,1,0:T(4,128)(2,1)S(1)}, bf16[14,3,256]{2,1,0:T(4,128)(2,1)S(1)}, u32[]{:S(2)}, u32[]{:S(2)}) collective-permute-start(bf16[14,3,256]{2,1,0:T(4,128)(2,1)S(1)} %get-tuple-element.190), channel_id=1, source_target_pairs={{4,0},{8,4},{12,8},{0,12},{5,1},{9,5},{13,9},{1,13},{6,2},{10,6},{... | collective-permute-start | bytes 64520 | tf_op jit(solution)/shard_map/ppermute | solution.py:20
  63.4 0.9 collective-permute-done.6
  65.5 1.5 bitcast_dynamic-update-slice_fusion.1
  67.0 1.3 collective-permute-start.8
  70.2 6.3 %stack.499 = f32[49,256]{1,0:T(8,128)} concatenate(f32[1,256]{1,0:T(1,128)} %bitcast.780, f32[1,256]{1,0:T(1,128)S(1)} %bitcast.715, f32[1,256]{1,0:T(1,128)S(1)} %bitcast.716, f32[1,256]{1,0:T(1,128)S(1)} %bitcast.717, f32[1,256]{1,0:T(1,128)S(1)} %bitcast.718, f32[1,256]{1,0:T(1,128)S(1)} %bitcast.719, f32[1,256]{1,0:T(1,128)S(1)} %bitcast.720, f32[1,256]{1,0:T(1,128)S(1)} %bitcast.721, ...), dimensions={0} | concatenate | bytes 100352 | tf_op jit(solution)/shard_map/stack | solution.py:114
  76.5 0.9 multiply_convert_fusion.11
  77.5 1.5 fusion.5
  79.4 1.0 fusion.139
  80.4 2.8 %collective-permute-start.13 = (bf16[3,16,256]{2,1,0:T(8,128)(2,1)S(1)}, bf16[3,16,256]{2,1,0:T(8,128)(2,1)S(1)}, u32[]{:S(2)}, u32[]{:S(2)}) collective-permute-start(bf16[3,16,256]{2,1,0:T(8,128)(2,1)S(1)} %get-tuple-element.195), channel_id=1, source_target_pairs={{0,2},{1,3},{4,6},{5,7},{8,10},{9,11},{12,14},{13,15},{16,18},{17,... | collective-permute-start | bytes 73736 | tf_op jit(solution)/shard_map/ppermute | solution.py:17
  83.3 1.6 collective-permute-start.14
  85.3 1.3 fusion.3
  86.6 2.5 %collective-permute-done.14 = bf16[3,16,256]{2,1,0:T(8,128)(2,1)S(1)} collective-permute-done((bf16[3,16,256]{2,1,0:T(8,128)(2,1)S(1)}, bf16[3,16,256]{2,1,0:T(8,128)(2,1)S(1)}, u32[]{:S(2)}, u32[]{:S(2)}) %collective-permute-start.14) | collective-permute-done | bytes 24608 | tf_op jit(solution)/shard_map/ppermute | solution.py:20
  90.1 3.0 %collective-permute-start.16 = (bf16[14,3,256]{2,1,0:T(4,128)(2,1)S(1)}, bf16[14,3,256]{2,1,0:T(4,128)(2,1)S(1)}, u32[]{:S(2)}, u32[]{:S(2)}) collective-permute-start(bf16[14,3,256]{2,1,0:T(4,128)(2,1)S(1)} %get-tuple-element.186), channel_id=1, source_target_pairs={{4,0},{8,4},{12,8},{0,12},{5,1},{9,5},{13,9},{1,13},{6,2},{10,6},{... | collective-permute-start | bytes 64520 | tf_op jit(solution)/shard_map/ppermute | solution.py:20
  93.8 1.2 collective-permute-done.15
  95.7 1.5 fusion.342
  97.2 1.3 collective-permute-start.17
  99.3 4.3 %stack.549 = f32[49,256]{1,0:T(8,128)} concatenate(f32[1,256]{1,0:T(1,128)S(1)} %bitcast.793, f32[1,256]{1,0:T(1,128)S(1)} %bitcast.733, f32[1,256]{1,0:T(1,128)S(1)} %bitcast.734, f32[1,256]{1,0:T(1,128)S(1)} %bitcast.735, f32[1,256]{1,0:T(1,128)S(1)} %bitcast.736, f32[1,256]{1,0:T(1,128)S(1)} %bitcast.737, f32[1,256]{1,0:T(1,128)S(1)} %bitcast.738, f32[1,256]{1,0:T(1,128)S(1)} %bitcast.739, ...), dimensions={0} | concatenate | bytes 100352 | tf_op jit(solution)/shard_map/stack | solution.py:114
  104.3 1.5 fusion.6
  106.9 1.4 fusion
  108.3 1.3 fusion.2
  110.0 2.0 collective-permute-start.22
  112.0 1.3 collective-permute-start.23
  114.7 40.8 %psum.23 = f32[49,256]{1,0:T(8,128)S(1)} all-reduce(f32[49,256]{1,0:T(8,128)S(1)} %select_add_fusion), channel_id=1, replica_groups=mesh['group'=2,'lon'=4,'lat'=2,'section'=2] {'lon','lat'}, use_global_device_ids=true, to_apply=%region_161.162 | all-reduce | flops 12544 | bytes 100352 | tf_op jit(solution)/shard_map/psum | solution.py:164
  155.6 3.8 %collective-permute-start.25 = (bf16[14,3,256]{2,1,0:T(4,128)(2,1)S(1)}, bf16[14,3,256]{2,1,0:T(4,128)(2,1)S(1)}, u32[]{:S(2)}, u32[]{:S(2)}) collective-permute-start(bf16[14,3,256]{2,1,0:T(4,128)(2,1)S(1)} %get-tuple-element.182), channel_id=1, source_target_pairs={{4,0},{8,4},{12,8},{0,12},{5,1},{9,5},{13,9},{1,13},{6,2},{10,6},{... | collective-permute-start | bytes 64520 | tf_op jit(solution)/shard_map/ppermute | solution.py:20
  160.4 1.0 collective-permute-done.24
  162.8 51.5 %all-reduce.3.cloned.1.call-done = (f32[256,1024]{1,0:T(8,128)}, f32[1024,256]{1,0:T(8,128)}) async-done(((f32[256,1024]{1,0:T(8,128)}, f32[1024,256]{1,0:T(8,128)}), (f32[256,1024]{1,0:T(8,128)}, f32[1024,256]{1,0:T(8,128)})) %all-reduce.3.cloned.1.call-update) | async-done | bytes 2097168 | tf_op jit(solution)/shard_map/psum | solution.py:164
  214.3 2.4 %multiply_bitcast_fusion.1 = f32[1,256,1024]{2,1,0:T(8,128)} fusion(f32[256,1024]{1,0:T(8,128)} %get-tuple-element.157), kind=kLoop, calls=%fused_computation.170 | loop fusion | flops 262144 | bytes 2097152 | tf_op jit(solution)/shard_map/broadcast_in_dim | solution.py:189
  216.8 1.1 multiply_bitcast_fusion
  (498 shorter events, 23.0 us)
Async XLA Ops:
  7.2 40.1 %copy-start = (bf16[1,256,1024]{2,1,0:T(8,128)(2,1)S(1)}, bf16[1,256,1024]{2,1,0:T(8,128)(2,1)}, u32[]{:S(2)}) copy-start(bf16[1,256,1024]{2,1,0:T(8,128)(2,1)} %param.15) | copy-start | bytes 1572868
  7.2 207.1 %all-reduce.3.cloned.1.call-start = ((), (), s32[]{:S(2)}) async-start(), calls=%async_computation | async-start | bytes 4194304 | tf_op jit(solution)/shard_map/psum | solution.py:164
  7.2 14.2 %copy-start.19 = (bf16[1,7,7,256]{3,2,1,0:T(8,128)(2,1)S(1)}, bf16[1,7,7,256]{3,2,1,0:T(8,128)(2,1)}, u32[]{:S(2)}) copy-start(bf16[1,7,7,256]{3,2,1,0:T(8,128)(2,1)} %param.12) | copy-start | bytes 75268
  8.1 17.2 %collective-permute-start.18 = (bf16[3,16,256]{2,1,0:T(8,128)(2,1)S(1)}, bf16[3,16,256]{2,1,0:T(8,128)(2,1)S(1)}, u32[]{:S(2)}, u32[]{:S(2)}) collective-permute-start(bf16[3,16,256]{2,1,0:T(8,128)(2,1)S(1)} %get-tuple-element.172), channel_id=1, source_target_pairs={{0,2},{1,3},{4,6},{5,7},{8,10},{9,11},{12,14},{13,15},{16,18},{17,... | collective-permute-start | bytes 73736 | tf_op jit(solution)/shard_map/ppermute | solution.py:17
  13.0 16.9 %collective-permute-start.19 = (bf16[3,16,256]{2,1,0:T(8,128)(2,1)S(1)}, bf16[3,16,256]{2,1,0:T(8,128)(2,1)S(1)}, u32[]{:S(2)}, u32[]{:S(2)}) collective-permute-start(bf16[3,16,256]{2,1,0:T(8,128)(2,1)S(1)} %get-tuple-element.173), channel_id=1, source_target_pairs={{2,0},{3,1},{6,4},{7,5},{10,8},{11,9},{14,12},{15,13},{18,16},{19,... | collective-permute-start | bytes 73736 | tf_op jit(solution)/shard_map/ppermute | solution.py:20
  14.3 17.3 %collective-permute-start.10 = (bf16[3,16,256]{2,1,0:T(8,128)(2,1)S(1)}, bf16[3,16,256]{2,1,0:T(8,128)(2,1)S(1)}, u32[]{:S(2)}, u32[]{:S(2)}) collective-permute-start(bf16[3,16,256]{2,1,0:T(8,128)(2,1)S(1)} %get-tuple-element.174), channel_id=1, source_target_pairs={{2,0},{3,1},{6,4},{7,5},{10,8},{11,9},{14,12},{15,13},{18,16},{19,... | collective-permute-start | bytes 73736 | tf_op jit(solution)/shard_map/ppermute | solution.py:20
  15.6 18.2 %collective-permute-start.9 = (bf16[3,16,256]{2,1,0:T(8,128)(2,1)S(1)}, bf16[3,16,256]{2,1,0:T(8,128)(2,1)S(1)}, u32[]{:S(2)}, u32[]{:S(2)}) collective-permute-start(bf16[3,16,256]{2,1,0:T(8,128)(2,1)S(1)} %get-tuple-element.175), channel_id=1, source_target_pairs={{0,2},{1,3},{4,6},{5,7},{8,10},{9,11},{12,14},{13,15},{16,18},{17,... | collective-permute-start | bytes 73736 | tf_op jit(solution)/shard_map/ppermute | solution.py:17
  20.1 13.8 %collective-permute-start.1 = (bf16[3,16,256]{2,1,0:T(8,128)(2,1)S(1)}, bf16[3,16,256]{2,1,0:T(8,128)(2,1)S(1)}, u32[]{:S(2)}, u32[]{:S(2)}) collective-permute-start(bf16[3,16,256]{2,1,0:T(8,128)(2,1)S(1)} %get-tuple-element.176), channel_id=1, source_target_pairs={{2,0},{3,1},{6,4},{7,5},{10,8},{11,9},{14,12},{15,13},{18,16},{19,... | collective-permute-start | bytes 73736 | tf_op jit(solution)/shard_map/ppermute | solution.py:20
  22.2 2.2 copy-start.11
  25.3 12.4 %collective-permute-start = (bf16[3,16,256]{2,1,0:T(8,128)(2,1)S(1)}, bf16[3,16,256]{2,1,0:T(8,128)(2,1)S(1)}, u32[]{:S(2)}, u32[]{:S(2)}) collective-permute-start(bf16[3,16,256]{2,1,0:T(8,128)(2,1)S(1)} %get-tuple-element.177), channel_id=1, source_target_pairs={{0,2},{1,3},{4,6},{5,7},{8,10},{9,11},{12,14},{13,15},{16,18},{17,... | collective-permute-start | bytes 73736 | tf_op jit(solution)/shard_map/ppermute | solution.py:17
  29.9 15.1 %collective-permute-start.20 = (bf16[14,3,256]{2,1,0:T(4,128)(2,1)S(1)}, bf16[14,3,256]{2,1,0:T(4,128)(2,1)S(1)}, u32[]{:S(2)}, u32[]{:S(2)}) collective-permute-start(bf16[14,3,256]{2,1,0:T(4,128)(2,1)S(1)} %get-tuple-element.183), channel_id=1, source_target_pairs={{0,4},{4,8},{8,12},{12,0},{1,5},{5,9},{9,13},{13,1},{2,6},{6,10},{... | collective-permute-start | bytes 64520 | tf_op jit(solution)/shard_map/ppermute | solution.py:17
  31.6 13.5 %collective-permute-start.21 = (bf16[14,3,256]{2,1,0:T(4,128)(2,1)S(1)}, bf16[14,3,256]{2,1,0:T(4,128)(2,1)S(1)}, u32[]{:S(2)}, u32[]{:S(2)}) collective-permute-start(bf16[14,3,256]{2,1,0:T(4,128)(2,1)S(1)} %get-tuple-element.184), channel_id=1, source_target_pairs={{4,0},{8,4},{12,8},{0,12},{5,1},{9,5},{13,9},{1,13},{6,2},{10,6},{... | collective-permute-start | bytes 64520 | tf_op jit(solution)/shard_map/ppermute | solution.py:20
  33.8 5.8 %collective-permute-start.11 = (bf16[14,3,256]{2,1,0:T(4,128)(2,1)S(1)}, bf16[14,3,256]{2,1,0:T(4,128)(2,1)S(1)}, u32[]{:S(2)}, u32[]{:S(2)}) collective-permute-start(bf16[14,3,256]{2,1,0:T(4,128)(2,1)S(1)} %get-tuple-element.187), channel_id=1, source_target_pairs={{0,4},{4,8},{8,12},{12,0},{1,5},{5,9},{9,13},{13,1},{2,6},{6,10},{... | collective-permute-start | bytes 64520 | tf_op jit(solution)/shard_map/ppermute | solution.py:17
  33.9 7.7 %collective-permute-start.12 = (bf16[14,3,256]{2,1,0:T(4,128)(2,1)S(1)}, bf16[14,3,256]{2,1,0:T(4,128)(2,1)S(1)}, u32[]{:S(2)}, u32[]{:S(2)}) collective-permute-start(bf16[14,3,256]{2,1,0:T(4,128)(2,1)S(1)} %get-tuple-element.188), channel_id=1, source_target_pairs={{4,0},{8,4},{12,8},{0,12},{5,1},{9,5},{13,9},{1,13},{6,2},{10,6},{... | collective-permute-start | bytes 64520 | tf_op jit(solution)/shard_map/ppermute | solution.py:20
  37.7 5.7 %collective-permute-start.2 = (bf16[14,3,256]{2,1,0:T(4,128)(2,1)S(1)}, bf16[14,3,256]{2,1,0:T(4,128)(2,1)S(1)}, u32[]{:S(2)}, u32[]{:S(2)}) collective-permute-start(bf16[14,3,256]{2,1,0:T(4,128)(2,1)S(1)} %get-tuple-element.191), channel_id=1, source_target_pairs={{0,4},{4,8},{8,12},{12,0},{1,5},{5,9},{9,13},{13,1},{2,6},{6,10},{... | collective-permute-start | bytes 64520 | tf_op jit(solution)/shard_map/ppermute | solution.py:17
  39.7 4.1 %collective-permute-start.3 = (bf16[14,3,256]{2,1,0:T(4,128)(2,1)S(1)}, bf16[14,3,256]{2,1,0:T(4,128)(2,1)S(1)}, u32[]{:S(2)}, u32[]{:S(2)}) collective-permute-start(bf16[14,3,256]{2,1,0:T(4,128)(2,1)S(1)} %get-tuple-element.192), channel_id=1, source_target_pairs={{4,0},{8,4},{12,8},{0,12},{5,1},{9,5},{13,9},{1,13},{6,2},{10,6},{... | collective-permute-start | bytes 64520 | tf_op jit(solution)/shard_map/ppermute | solution.py:20
  48.2 29.2 %copy-start.4 = (f32[128,1024]{1,0:T(8,128)}, f32[128,1024]{1,0:T(8,128)S(1)}, u32[]{:S(2)}) copy-start(f32[128,1024]{1,0:T(8,128)S(1)} %convolution_add_fusion.1) | copy-start | bytes 1572868
  51.4 5.4 %collective-permute-start.4 = (bf16[3,16,256]{2,1,0:T(8,128)(2,1)S(1)}, bf16[3,16,256]{2,1,0:T(8,128)(2,1)S(1)}, u32[]{:S(2)}, u32[]{:S(2)}) collective-permute-start(bf16[3,16,256]{2,1,0:T(8,128)(2,1)S(1)} %get-tuple-element.197), channel_id=1, source_target_pairs={{0,2},{1,3},{4,6},{5,7},{8,10},{9,11},{12,14},{13,15},{16,18},{17,... | collective-permute-start | bytes 73736 | tf_op jit(solution)/shard_map/ppermute | solution.py:17
  52.7 5.9 %collective-permute-start.5 = (bf16[3,16,256]{2,1,0:T(8,128)(2,1)S(1)}, bf16[3,16,256]{2,1,0:T(8,128)(2,1)S(1)}, u32[]{:S(2)}, u32[]{:S(2)}) collective-permute-start(bf16[3,16,256]{2,1,0:T(8,128)(2,1)S(1)} %get-tuple-element.198), channel_id=1, source_target_pairs={{2,0},{3,1},{6,4},{7,5},{10,8},{11,9},{14,12},{15,13},{18,16},{19,... | collective-permute-start | bytes 73736 | tf_op jit(solution)/shard_map/ppermute | solution.py:20
  58.6 5.7 %collective-permute-start.6 = (bf16[14,3,256]{2,1,0:T(4,128)(2,1)S(1)}, bf16[14,3,256]{2,1,0:T(4,128)(2,1)S(1)}, u32[]{:S(2)}, u32[]{:S(2)}) collective-permute-start(bf16[14,3,256]{2,1,0:T(4,128)(2,1)S(1)} %get-tuple-element.189), channel_id=1, source_target_pairs={{0,4},{4,8},{8,12},{12,0},{1,5},{5,9},{9,13},{13,1},{2,6},{6,10},{... | collective-permute-start | bytes 64520 | tf_op jit(solution)/shard_map/ppermute | solution.py:17
  58.7 5.7 %collective-permute-start.7 = (bf16[14,3,256]{2,1,0:T(4,128)(2,1)S(1)}, bf16[14,3,256]{2,1,0:T(4,128)(2,1)S(1)}, u32[]{:S(2)}, u32[]{:S(2)}) collective-permute-start(bf16[14,3,256]{2,1,0:T(4,128)(2,1)S(1)} %get-tuple-element.190), channel_id=1, source_target_pairs={{4,0},{8,4},{12,8},{0,12},{5,1},{9,5},{13,9},{1,13},{6,2},{10,6},{... | collective-permute-start | bytes 64520 | tf_op jit(solution)/shard_map/ppermute | solution.py:20
  67.0 2.1 copy-start.6
  67.0 9.5 %collective-permute-start.8 = (bf16[8,16,256]{2,1,0:T(8,128)(2,1)S(1)}, bf16[8,16,256]{2,1,0:T(8,128)(2,1)}, u32[]{:S(2)}, u32[]{:S(2)}) collective-permute-start(bf16[8,16,256]{2,1,0:T(8,128)(2,1)S(1)} %get-tuple-element.169), channel_id=1, source_target_pairs={{1,0},{3,2},{5,4},{7,6},{9,8},{11,10},{13,12},{15,14},{17,16},{19,... | collective-permute-start | bytes 196616 | tf_op jit(solution)/shard_map/ppermute | solution.py:28
  79.4 5.5 %copy-start.5 = (f32[128,1024]{1,0:T(8,128)S(1)}, f32[128,1024]{1,0:T(8,128)}, u32[]{:S(2)}) copy-start(f32[128,1024]{1,0:T(8,128)} %copy-done.4) | copy-start | bytes 1572868
  79.4 5.5 %copy-start.9 = (f32[1024,256]{1,0:T(8,128)S(1)}, f32[1024,256]{1,0:T(8,128)}, u32[]{:S(2)}) copy-start(f32[1024,256]{1,0:T(8,128)} %convolution_select_fusion.2) | copy-start | bytes 3145732
  80.4 6.2 %collective-permute-start.13 = (bf16[3,16,256]{2,1,0:T(8,128)(2,1)S(1)}, bf16[3,16,256]{2,1,0:T(8,128)(2,1)S(1)}, u32[]{:S(2)}, u32[]{:S(2)}) collective-permute-start(bf16[3,16,256]{2,1,0:T(8,128)(2,1)S(1)} %get-tuple-element.195), channel_id=1, source_target_pairs={{0,2},{1,3},{4,6},{5,7},{8,10},{9,11},{12,14},{13,15},{16,18},{17,... | collective-permute-start | bytes 73736 | tf_op jit(solution)/shard_map/ppermute | solution.py:17
  83.3 2.0 copy-start.14
  83.3 5.9 %collective-permute-start.14 = (bf16[3,16,256]{2,1,0:T(8,128)(2,1)S(1)}, bf16[3,16,256]{2,1,0:T(8,128)(2,1)S(1)}, u32[]{:S(2)}, u32[]{:S(2)}) collective-permute-start(bf16[3,16,256]{2,1,0:T(8,128)(2,1)S(1)} %get-tuple-element.196), channel_id=1, source_target_pairs={{2,0},{3,1},{6,4},{7,5},{10,8},{11,9},{14,12},{15,13},{18,16},{19,... | collective-permute-start | bytes 73736 | tf_op jit(solution)/shard_map/ppermute | solution.py:20
  89.2 5.8 %collective-permute-start.15 = (bf16[14,3,256]{2,1,0:T(4,128)(2,1)S(1)}, bf16[14,3,256]{2,1,0:T(4,128)(2,1)S(1)}, u32[]{:S(2)}, u32[]{:S(2)}) collective-permute-start(bf16[14,3,256]{2,1,0:T(4,128)(2,1)S(1)} %get-tuple-element.185), channel_id=1, source_target_pairs={{0,4},{4,8},{8,12},{12,0},{1,5},{5,9},{9,13},{13,1},{2,6},{6,10},{... | collective-permute-start | bytes 64520 | tf_op jit(solution)/shard_map/ppermute | solution.py:17
  90.1 4.9 %collective-permute-start.16 = (bf16[14,3,256]{2,1,0:T(4,128)(2,1)S(1)}, bf16[14,3,256]{2,1,0:T(4,128)(2,1)S(1)}, u32[]{:S(2)}, u32[]{:S(2)}) collective-permute-start(bf16[14,3,256]{2,1,0:T(4,128)(2,1)S(1)} %get-tuple-element.186), channel_id=1, source_target_pairs={{4,0},{8,4},{12,8},{0,12},{5,1},{9,5},{13,9},{1,13},{6,2},{10,6},{... | collective-permute-start | bytes 64520 | tf_op jit(solution)/shard_map/ppermute | solution.py:20
  93.1 2.0 copy-start.35
  93.1 2.0 copy-start.38
  93.1 2.0 copy-start.41
  93.2 2.0 copy-start.44
  93.2 2.0 copy-start.47
  93.2 2.0 copy-start.50
  93.2 2.0 copy-start.53
  93.2 2.0 copy-start.56
  93.2 2.0 copy-start.59
  97.2 7.1 %collective-permute-start.17 = (bf16[8,16,256]{2,1,0:T(8,128)(2,1)S(1)}, bf16[8,16,256]{2,1,0:T(8,128)(2,1)S(1)}, u32[]{:S(2)}, u32[]{:S(2)}) collective-permute-start(bf16[8,16,256]{2,1,0:T(8,128)(2,1)S(1)} %get-tuple-element.165), channel_id=1, source_target_pairs={{1,0},{3,2},{5,4},{7,6},{9,8},{11,10},{13,12},{15,14},{17,16},{19,... | collective-permute-start | bytes 196616 | tf_op jit(solution)/shard_map/ppermute | solution.py:28
  98.7 5.6 %copy-start.12 = (bf16[2,8,16,256]{3,2,1,0:T(8,128)(2,1)S(1)}, bf16[2,8,16,256]{3,2,1,0:T(8,128)(2,1)}, u32[]{:S(2)}) copy-start(bf16[2,8,16,256]{3,2,1,0:T(8,128)(2,1)} %param.10) | copy-start | bytes 393220
  98.9 5.4 %copy-start.2 = (f32[128,1024]{1,0:T(8,128)S(1)}, f32[128,1024]{1,0:T(8,128)}, u32[]{:S(2)}) copy-start(f32[128,1024]{1,0:T(8,128)} %convolution_add_fusion) | copy-start | bytes 1572868
  110.0 45.5 %collective-permute-start.22 = (bf16[3,16,256]{2,1,0:T(8,128)(2,1)S(1)}, bf16[3,16,256]{2,1,0:T(8,128)(2,1)S(1)}, u32[]{:S(2)}, u32[]{:S(2)}) collective-permute-start(bf16[3,16,256]{2,1,0:T(8,128)(2,1)S(1)} %get-tuple-element.193), channel_id=1, source_target_pairs={{0,2},{1,3},{4,6},{5,7},{8,10},{9,11},{12,14},{13,15},{16,18},{17,... | collective-permute-start | bytes 73736 | tf_op jit(solution)/shard_map/ppermute | solution.py:17
  112.0 43.5 %collective-permute-start.23 = (bf16[3,16,256]{2,1,0:T(8,128)(2,1)S(1)}, bf16[3,16,256]{2,1,0:T(8,128)(2,1)S(1)}, u32[]{:S(2)}, u32[]{:S(2)}) collective-permute-start(bf16[3,16,256]{2,1,0:T(8,128)(2,1)S(1)} %get-tuple-element.194), channel_id=1, source_target_pairs={{2,0},{3,1},{6,4},{7,5},{10,8},{11,9},{14,12},{15,13},{18,16},{19,... | collective-permute-start | bytes 73736 | tf_op jit(solution)/shard_map/ppermute | solution.py:20
  155.5 5.9 %collective-permute-start.24 = (bf16[14,3,256]{2,1,0:T(4,128)(2,1)S(1)}, bf16[14,3,256]{2,1,0:T(4,128)(2,1)S(1)}, u32[]{:S(2)}, u32[]{:S(2)}) collective-permute-start(bf16[14,3,256]{2,1,0:T(4,128)(2,1)S(1)} %get-tuple-element.181), channel_id=1, source_target_pairs={{0,4},{4,8},{8,12},{12,0},{1,5},{5,9},{9,13},{13,1},{2,6},{6,10},{... | collective-permute-start | bytes 64520 | tf_op jit(solution)/shard_map/ppermute | solution.py:17
  155.6 5.8 %collective-permute-start.25 = (bf16[14,3,256]{2,1,0:T(4,128)(2,1)S(1)}, bf16[14,3,256]{2,1,0:T(4,128)(2,1)S(1)}, u32[]{:S(2)}, u32[]{:S(2)}) collective-permute-start(bf16[14,3,256]{2,1,0:T(4,128)(2,1)S(1)} %get-tuple-element.182), channel_id=1, source_target_pairs={{4,0},{8,4},{12,8},{0,12},{5,1},{9,5},{13,9},{1,13},{6,2},{10,6},{... | collective-permute-start | bytes 64520 | tf_op jit(solution)/shard_map/ppermute | solution.py:20
  162.8 54.0 %copy-start.18 = (bf16[1,2,8,16,256]{4,3,2,1,0:T(8,128)(2,1)}, bf16[1,2,8,16,256]{4,3,2,1,0:T(8,128)(2,1)S(1)}, u32[]{:S(2)}) copy-start(bf16[1,2,8,16,256]{4,3,2,1,0:T(8,128)(2,1)S(1)} %bitcast_dynamic-update-slice_fusion) | copy-start | bytes 393220
  214.3 2.4 %copy-start.8 = (f32[1024,256]{1,0:T(8,128)S(1)}, f32[1024,256]{1,0:T(8,128)}, u32[]{:S(2)}) copy-start(f32[1024,256]{1,0:T(8,128)} %get-tuple-element.158) | copy-start | bytes 3145732
  (181 other events, 193.7 us)
Sparse Core Ops, SparseCore 0:
  109.7 104.5 all-reduce.2
where the time goes:
time: 226 us; the launch traced here: 225 us
  waiting for transfers between devices  61.3 us (27%)
  starting transfers between devices  52.3 us (23%)
  blocking collectives  40.8 us (18%)
  local copies, waits for them, and re-layouts  22.8 us (10%)
  other arithmetic  18.5 us (8%)
  between operations  16.8 us (7%)
  matrix products  12.2 us (5%)
    psum x1, waiting for transfers between devices, run_relay(): lax.psum((sum_in, sum_out, sum_k), ('lon', 'lat'))  51.5 us
    psum x1, blocking collectives, run_relay(): lax.psum((sum_in, sum_out, sum_k), ('lon', 'lat'))  40.8 us
    ppermute x12, starting transfers between devices, extended(): lax.ppermute(lax.slice_in_dim(block, 0, width, axis=dim), axis, backward)  26.9 us
    ppermute x12, starting transfers between devices, extended(): lax.ppermute(lax.slice_in_dim(block, block.shape[dim] - width, None, axis...  22.8 us
    another operation x3, local copies, waits for them, and re-layouts, local_backward(): grad_k = jnp.stack(kgrads)  10.8 us
    unnamed x405, local copies, waits for them, and re-layouts  8.26 us
    dot_general x6, matrix products, contract_cells(): lax.dot_general(left, right, (((0,), (0,)), ((), ())), preferred_element_...  5.99 us
    ppermute x12, waiting for transfers between devices, extended(): lax.ppermute(lax.slice_in_dim(block, block.shape[dim] - width, None, axis...  5.16 us
  transfers between devices with their start and end apart: 27, of which 9 were waited for; matrix products, arithmetic and copies ran while one was open for 12% of the time, Pallas kernels for 0%

commit v1 on v0

v1 whole, which is shorter than its diff:
```python
import functools
import jax
import jax.numpy as jnp
from jax import lax
from jax.experimental import pallas as pl
from jax.experimental.pallas import tpu as pltpu
from jax.sharding import PartitionSpec as P

gelu_k = 0.7978845608028654
gelu_c = 0.044715
LANES = 128
HALO = 3
SIDE = 8
F32 = jnp.float32
BF16 = jnp.bfloat16
VMEM_LIMIT = 48 * 1024 * 1024
GATHER_TILES = 8


def call(body, outs, scratch, *args, flops=0):
    moved = sum(a.size * a.dtype.itemsize for a in args)
    moved += sum(o.size * o.dtype.itemsize for o in outs)
    return pl.pallas_call(
        body,
        out_shape=outs,
        in_specs=[pl.BlockSpec(memory_space=pltpu.VMEM)] * len(args),
        out_specs=[pl.BlockSpec(memory_space=pltpu.VMEM)] * len(outs),
        scratch_shapes=scratch,
        compiler_params=pltpu.CompilerParams(vmem_limit_bytes=VMEM_LIMIT),
        cost_estimate=pl.CostEstimate(flops=flops, bytes_accessed=moved, transcendentals=0),
    )(*args)


def like(shape, dtype):
    return jax.ShapeDtypeStruct(shape, dtype)


def nt_dot(left, right):
    return lax.dot_general(left, right, (((1,), (1,)), ((), ())), preferred_element_type=F32)


def tn_dot(left, right):
    return lax.dot_general(left, right, (((0,), (0,)), ((), ())), preferred_element_type=F32)


def gelu_both(h):
    h2 = h * h
    tval = jnp.tanh(h * (gelu_k + (gelu_k * gelu_c) * h2))
    half = 0.5 + 0.5 * tval
    slope = half + (0.5 * h) * (1.0 - tval * tval) * (gelu_k + (3.0 * gelu_k * gelu_c) * h2)
    return h * half, slope


def widen(dst, own, low, high, left, right):
    rows, cols = own.shape[1], own.shape[2]
    dst[:, :HALO, SIDE : SIDE + cols, :] = low[...].astype(F32)
    dst[:, HALO : HALO + rows, SIDE : SIDE + cols, :] = own[...].astype(F32)
    dst[:, HALO + rows :, SIDE : SIDE + cols, :] = high[...].astype(F32)
    dst[:, :, SIDE - HALO : SIDE, :] = left[...].astype(F32)
    dst[:, :, SIDE + cols : SIDE + cols + HALO, :] = right[...].astype(F32)


def depthwise(src, kern, rows, cols, flip, emit):
    micros, chans = src.shape[0], src.shape[3]
    for part in range(chans // LANES):
        lanes = slice(part * LANES, (part + 1) * LANES)
        for micro in range(micros):
            total = jnp.zeros((rows, cols, LANES), F32)
            for kb in range(7):
                begin = SIDE - HALO + kb
                slab = src[micro, :, begin : begin + cols, lanes]
                for ka in range(7):
                    tap = (6 - ka) * 7 + (6 - kb) if flip else ka * 7 + kb
                    total = total + slab[ka : ka + rows] * kern[tap : tap + 1, lanes]
            emit(micro, lanes, total)


def dense_back(masked, slope, zhat, rscale, gain, w_in, w_out):
    dact = nt_dot(masked, w_out)
    dhid = (dact * slope).astype(BF16)
    dzh = nt_dot(dhid, w_in) * gain
    return rscale * (
        dzh
        - jnp.mean(dzh, axis=-1, keepdims=True)
        - zhat * jnp.mean(dzh * zhat, axis=-1, keepdims=True)
    )


def forward_body(
    x, low, high, left, right, masked, kern, bias, gain, w_in, b_in, w_out,
    wide, normed, zhat, rscale, slope, dz, zval,
):
    rows, cols = x.shape[1], x.shape[2]
    widen(wide, x, low, high, left, right)

    def emit(micro, lanes, total):
        cells = rows * cols
        zval[micro * cells : (micro + 1) * cells, lanes] = total.reshape(cells, LANES)

    depthwise(wide, kern, rows, cols, False, emit)
    z = zval[...] + bias[...]
    centred = z - jnp.mean(z, axis=-1, keepdims=True)
    rs = lax.rsqrt(jnp.mean(centred * centred, axis=-1, keepdims=True) + 1e-06)
    zh = centred * rs
    n = (zh * gain[...]).astype(BF16)
    normed[...] = n
    zhat[...] = zh
    rscale[...] = rs
    h = jnp.dot(n, w_in[...], preferred_element_type=F32) + b_in[...]
    _, sl = gelu_both(h)
    slope[...] = sl
    dz[...] = dense_back(masked[...], sl, zh, rs, gain[...], w_in[...], w_out[...]).astype(BF16)


def back_body(masked, slope, zhat, rscale, gain, w_in, w_out, dz):
    dz[...] = dense_back(
        masked[...], slope[...], zhat[...], rscale[...], gain[...], w_in[...], w_out[...]
    ).astype(BF16)


def kernel_grad_body(wide, dz, grad):
    micros, rows, cols, chans = dz.shape
    for part in range(chans // LANES):
        lanes = slice(part * LANES, (part + 1) * LANES)
        for kb in range(7):
            begin = SIDE - HALO + kb
            sums = [None] * 7
            for micro in range(micros):
                own = dz[micro, :, :, lanes].astype(F32)
                slab = wide[micro, :, begin : begin + cols, lanes]
                for ka in range(7):
                    prod = jnp.sum(slab[ka : ka + rows] * own, axis=0)
                    sums[ka] = prod if sums[ka] is None else sums[ka] + prod
            for ka in range(7):
                tap = ka * 7 + kb
                grad[tap : tap + 1, lanes] = jnp.sum(sums[ka], axis=0, keepdims=True)


def input_grad_body(own, low, high, left, right, masked, maskb, kern, dx, dxm, wide):
    rows, cols = own.shape[1], own.shape[2]
    widen(wide, own, low, high, left, right)

    def emit(micro, lanes, total):
        value = (total + masked[micro, :, :, lanes].astype(F32)).astype(BF16)
        dx[micro, :, :, lanes] = value
        dxm[micro, :, :, lanes] = (value.astype(F32) * maskb[...]).astype(BF16)

    depthwise(wide, kern, rows, cols, True, emit)


def weight_grad_body(parts, factor, *refs):
    normed, masked = refs[:parts], refs[parts : 2 * parts]
    w_in, b_in, w_out, grad_in, grad_out = refs[2 * parts :]
    grad_in[...] = jnp.zeros_like(grad_in)
    grad_out[...] = jnp.zeros_like(grad_out)
    for part in range(parts):
        cells = normed[part].shape[0]
        step = min(cells, 256)

        @pl.loop(0, cells // step)
        def _(index):
            at = pl.ds(pl.multiple_of(index * step, step), step)
            n = normed[part][at, :]
            gm = masked[part][at, :]
            h = jnp.dot(n, w_in[...], preferred_element_type=F32) + b_in[...]
            act, slope = gelu_both(h)
            dhid = (nt_dot(gm, w_out[...]) * slope).astype(BF16)
            grad_in[...] += tn_dot(n, dhid)
            grad_out[...] += tn_dot(act.astype(BF16), gm)

    grad_in[...] = grad_in[...] * factor
    grad_out[...] = grad_out[...] * factor


def lat_edges(first, last):
    count = lax.axis_size("lat")
    if count == 1:
        return jnp.zeros_like(last), jnp.zeros_like(first)
    if count == 2:
        index = lax.axis_index("lat")
        got = lax.ppermute(jnp.where(index == 0, last, first), "lat", [(0, 1), (1, 0)])
        none = jnp.zeros_like(got)
        return jnp.where(index == 0, none, got), jnp.where(index == 0, got, none)
    up = [(i, i + 1) for i in range(count - 1)]
    low = lax.ppermute(last, "lat", up)
    return low, lax.ppermute(first, "lat", [(b, a) for a, b in up])


def halo(own):
    low, high = lat_edges(own[:, :HALO], own[:, -HALO:])
    count = lax.axis_size("lon")
    firsts = jnp.concatenate([v[:, :, :HALO] for v in (low, own, high)], axis=1)
    lasts = jnp.concatenate([v[:, :, -HALO:] for v in (low, own, high)], axis=1)
    ring = [(i, (i + 1) % count) for i in range(count)]
    left = lax.ppermute(lasts, "lon", ring)
    right = lax.ppermute(firsts, "lon", [(b, a) for a, b in ring])
    return low, high, left, right


def ring_pieces(value, axis):
    count = lax.axis_size(axis)
    return [value] + [
        lax.ppermute(value, axis, [(i, (i + d) % count) for i in range(count)])
        for d in range(1, count)
    ]


def crossing_pieces(value):
    count = lax.axis_size("lon")
    pieces = []
    for d in range(count):
        pairs = []
        for i in range(count):
            for s in range(2):
                pairs.append((i * 2 + s, ((i + d) % count) * 2 + 1 - s))
        pieces.append(lax.ppermute(value, ("lon", "section"), pairs))
    return pieces


def summed(value):
    for axis in ("lat", "lon"):
        count = lax.axis_size(axis)
        if count & (count - 1):
            value = lax.psum(value, axis)
            continue
        step = 1
        while step < count:
            value = value + lax.ppermute(value, axis, [(i, i ^ step) for i in range(count)])
            step *= 2
    return value


def shards(
    saved_inputs, out_cotangent, land_mask, conv_kernel, conv_bias, norm_gain, w_in, b_in, w_out
):
    micros, rows, cols, chans = out_cotangent.shape
    hidden = w_in.shape[2]
    cells = micros * rows * cols
    shape = (micros, rows, cols, chans)
    wide_shape = (micros, rows + 2 * HALO, SIDE + cols + SIDE, chans)
    flat = (cells, chans)
    tiles = lax.axis_size("lat") * lax.axis_size("lon")
    factor = 1.0 / (cells * tiles) ** 0.5
    section = lax.axis_index("section")
    gather = tiles <= GATHER_TILES

    kern = conv_kernel[0].reshape(49, chans).astype(F32)
    weight_in, weight_out = w_in[0], w_out[0]
    maskf = land_mask.astype(F32)
    maskb = jnp.broadcast_to(maskf[:, :, None], (rows, cols, LANES))
    masked1 = (out_cotangent.astype(F32) * maskf[None, :, :, None]).astype(BF16)

    x = saved_inputs[0]
    wide, normed, zhat, rscale, slope, dz = call(
        forward_body,
        [
            like(wide_shape, F32),
            like(flat, BF16),
            like(flat, F32),
            like((cells, 1), F32),
            like((cells, hidden), F32),
            like(flat, BF16),
        ],
        [pltpu.VMEM(flat, F32)],
        x, *halo(x), masked1.reshape(flat), kern, conv_bias, norm_gain, weight_in, b_in, weight_out,
        flops=6 * cells * chans * hidden + 98 * cells * chans,
    )
    if gather:
        normed_row = jnp.concatenate(ring_pieces(normed, "lon"))
        normed_all = ring_pieces(normed_row, "lat")

    def input_grad(dz, masked):
        dz = dz.reshape(shape)
        edges = halo(dz)
        (grad_k,) = call(
            kernel_grad_body, [like((49, chans), F32)], [], wide, dz, flops=98 * cells * chans
        )
        dx, dxm = call(
            input_grad_body,
            [like(shape, BF16), like(shape, BF16)],
            [pltpu.VMEM(wide_shape, F32)],
            dz, *edges, masked, maskb, kern,
            flops=98 * cells * chans,
        )
        return grad_k, dx, dxm

    grad_k1, dx1, dxm1 = input_grad(dz, masked1)
    cross = jnp.where(section == 1, dxm1, masked1).reshape(flat)
    if gather:
        pieces = crossing_pieces(cross)
        masked0 = pieces[0]
        masked_all = ring_pieces(jnp.concatenate(pieces), "lat")
    else:
        masked0 = lax.ppermute(cross, "section", [(0, 1), (1, 0)])
        normed_all, masked_all = [normed], [masked0]
    (dz0,) = call(
        back_body, [like(flat, BF16)], [],
        masked0, slope, zhat, rscale, norm_gain, weight_in, weight_out,
        flops=4 * cells * chans * hidden,
    )
    grad_k0, dx0, _ = input_grad(dz0, masked0.reshape(shape))
    grad_k = summed(jnp.where(section == 1, grad_k1, grad_k0)) * factor
    grad_in, grad_out = call(
        functools.partial(weight_grad_body, len(normed_all), factor),
        [like((chans, hidden), F32), like((hidden, chans), F32)],
        [],
        *normed_all, *masked_all, weight_in, b_in, weight_out,
        flops=8 * sum(v.shape[0] for v in normed_all) * chans * hidden,
    )
    if not gather:
        grad_in, grad_out = lax.psum((grad_in, grad_out), ("lon", "lat"))
    results = jnp.where(section == 1, dx1, dx0)
    return results[None], grad_in[None], grad_out[None], grad_k[None]


def solution(mesh):
    in_specs = (
        P("section", "group", "lat", "lon", None),
        P("group", "lat", "lon", None),
        P("lat", "lon"),
        P("section", None, None, None),
        P("section", None),
        P("section", None),
        P("section", None, None),
        P("section", None),
        P("section", None, None),
    )
    out_specs = (
        P("section", "group", "lat", "lon", None),
        P("section", "group", None),
        P("section", "group", None),
        P("section", "group", None),
    )
    return jax.shard_map(shards, mesh=mesh, in_specs=in_specs, out_specs=out_specs, check_vma=False)
```

time: 226 us -> 85.9 us (0.38)
  blocking collectives: 40.8 us -> 0 us
  waiting for transfers between devices: 61.3 us -> 21.6 us
  Pallas kernels: 0 us -> 25.3 us
  starting transfers between devices: 52.3 us -> 31.3 us
  local copies, waits for them, and re-layouts: 22.8 us -> 3.48 us
  between operations: 16.8 us -> 0.99 us
  other arithmetic: 18.5 us -> 3.04 us
  matrix products: 12.2 us -> 0 us
    psum x1 -> x0, waiting for transfers between devices: 51.5 us -> none  [run_relay(): lax.psum((sum_in, sum_out, sum_k), ('lon', 'lat'))]
    psum x1 -> x0, blocking collectives: 40.8 us -> none  [run_relay(): lax.psum((sum_in, sum_out, sum_k), ('lon', 'lat'))]
    pallas_call x0 -> x7, Pallas kernels: none -> 25.3 us  [call(): pl.pallas_call(body, out_shape=outs, in_specs=[pl.BlockSpec(memory_space=...]
    ppermute x26 -> x21, starting transfers between devices: 52.3 us -> 31.3 us  [the longest x3 5.87 us: lat_edges(): lax.ppermute(jnp.where(index == 0, last, first), 'lat', [(0, 1), (1, 0)])]
    dot_general x15 -> x0, matrix products: 12.2 us -> none  [the longest x6 5.99 us: contract_cells(): lax.dot_general(left, right, (((0,), (0,)), ((), ())), preferred_element_...]
    ppermute x26 -> x21, waiting for transfers between devices: 9.71 us -> 21.6 us  [the longest x3 6.4 us: lat_edges(): lax.ppermute(jnp.where(index == 0, last, first), 'lat', [(0, 1), (1, 0)])]
    another operation x3 -> x0, local copies, waits for them, and re-layouts: 10.8 us -> none  [local_backward(): grad_k = jnp.stack(kgrads)]
    reduce_sum x15 -> x0, other arithmetic: 8.43 us -> none  [the longest x9 5.14 us: local_backward(): jnp.sum(dz32 * src32[ka:ka + rows, kb:kb + cols], axis=(0, 1))]
  transfers between devices with their start and end apart: 27 -> 21, of which waited for: 9 -> 13; matrix products, arithmetic and copies ran while one was open for 12% -> 5% of each run, Pallas kernels for 0% -> 12%
where the time goes in v1:
time: 85.9 us; the launch traced here: 85.7 us
  starting transfers between devices  31.3 us (36%)
  Pallas kernels  25.3 us (29%)
  waiting for transfers between devices  21.6 us (25%)
  local copies, waits for them, and re-layouts  3.48 us (4%)
  other arithmetic  3.04 us (4%)
  between operations  0.99 us (1%)
    pallas_call x7, Pallas kernels, call(): pl.pallas_call(body, out_shape=outs, in_specs=[pl.BlockSpec(memory_space=...  25.3 us
    ppermute x3, waiting for transfers between devices, lat_edges(): lax.ppermute(jnp.where(index == 0, last, first), 'lat', [(0, 1), (1, 0)])  6.4 us
    ppermute x3, starting transfers between devices, lat_edges(): lax.ppermute(jnp.where(index == 0, last, first), 'lat', [(0, 1), (1, 0)])  5.87 us
    ppermute x4, starting transfers between devices, crossing_pieces(): pieces.append(lax.ppermute(value, ('lon', 'section'), pairs))  5.65 us
    ppermute x3, starting transfers between devices, halo(): right = lax.ppermute(firsts, 'lon', [(b, a) for a, b in ring])  5.59 us
    ppermute x3, starting transfers between devices, halo(): left = lax.ppermute(lasts, 'lon', ring)  5.59 us
    ppermute x3, waiting for transfers between devices, halo(): left = lax.ppermute(lasts, 'lon', ring)  5.48 us
    ppermute x5, starting transfers between devices, ring_pieces(): lax.ppermute(value, axis, [(i, (i + d) % count) for i in range(count)])  5.31 us
  transfers between devices with their start and end apart: 21, of which 13 were waited for; matrix products, arithmetic and copies ran while one was open for 5% of the time, Pallas kernels for 12%

profile of v1, /device:TPU:0, one launch (start us, length us, event | category | flops | bytes accessed | tf_op | source)
XLA Modules:
  0.0 85.7 jit_solution(4227859715374463284)
XLA Ops:
  0.7 0.9 %slice_select_fusion.2 = bf16[2,3,16,256]{3,2,1,0:T(8,128)(2,1)S(1)} fusion(bf16[2,8,16,256]{3,2,1,0:T(8,128)(2,1)} %bitcast.30, pred[]{:T(512)S(6)} %eq.5), kind=kLoop, calls=%fused_computation.12 | loop fusion | flops 24576 | bytes 147457 | tf_op jit(solution)/shard_map/jit(_where)/select_n | solution.py:181
  1.6 3.0 %collective-permute-start = (bf16[2,3,16,256]{3,2,1,0:T(8,128)(2,1)S(1)}, bf16[2,3,16,256]{3,2,1,0:T(8,128)(2,1)S(1)}, u32[]{:S(2)}, u32[]{:S(2)}) collective-permute-start(bf16[2,3,16,256]{3,2,1,0:T(8,128)(2,1)S(1)} %slice_select_fusion.2), channel_id=1, source_target_pairs={{0,2},{2,0},{1,3},{3,1},{4,6},{6,4},{5,7},{7,5},{8,10},{10,8},{9,1... | collective-permute-start | bytes 147464 | tf_op jit(solution)/shard_map/ppermute | solution.py:181
  4.6 0.9 %fusion.2 = (bf16[2,8,3,256]{3,2,1,0:T(4,128)(2,1)S(1)}, bf16[2,8,3,256]{3,2,1,0:T(4,128)(2,1)S(1)}) fusion(bf16[2,8,16,256]{3,2,1,0:T(8,128)(2,1)} %bitcast.31), kind=kLoop, calls=%fused_computation.30 | loop fusion | bytes 98304 | tf_op jit(solution)/shard_map/slice | solution.py:192
  5.5 1.1 %collective-permute-done = bf16[2,3,16,256]{3,2,1,0:T(8,128)(2,1)S(1)} collective-permute-done((bf16[2,3,16,256]{3,2,1,0:T(8,128)(2,1)S(1)}, bf16[2,3,16,256]{3,2,1,0:T(8,128)(2,1)S(1)}, u32[]{:S(2)}, u32[]{:S(2)}) %collective-permute-start) | collective-permute-done | bytes 49184 | tf_op jit(solution)/shard_map/ppermute | solution.py:181
  6.7 2.2 %collective-permute-start.1 = (bf16[2,14,3,256]{3,2,1,0:T(4,128)(2,1)S(1)}, bf16[2,14,3,256]{3,2,1,0:T(4,128)(2,1)S(1)}, u32[]{:S(2)}, u32[]{:S(2)}) collective-permute-start(bf16[2,14,3,256]{3,2,1,0:T(4,128)(2,1)S(1)} %pad_maximum_fusion), channel_id=1, source_target_pairs={{0,4},{4,8},{8,12},{12,0},{1,5},{5,9},{9,13},{13,1},{2,6},{6,10},{... | collective-permute-start | bytes 129032 | tf_op jit(solution)/shard_map/ppermute | solution.py:195
  8.9 2.1 %collective-permute-start.2 = (bf16[2,14,3,256]{3,2,1,0:T(4,128)(2,1)S(1)}, bf16[2,14,3,256]{3,2,1,0:T(4,128)(2,1)S(1)}, u32[]{:S(2)}, u32[]{:S(2)}) collective-permute-start(bf16[2,14,3,256]{3,2,1,0:T(4,128)(2,1)S(1)} %pad_maximum_fusion.1), channel_id=1, source_target_pairs={{4,0},{8,4},{12,8},{0,12},{5,1},{9,5},{13,9},{1,13},{6,2},{10,6},{... | collective-permute-start | bytes 129032 | tf_op jit(solution)/shard_map/ppermute | solution.py:196
  11.0 1.0 %multiply_convert_fusion.masked = bf16[2,8,16,256]{3,2,1,0:T(8,128)(2,1)S(1)} fusion(bf16[2,8,16,256]{3,2,1,0:T(8,128)(2,1)} %param.10, f32[8,16]{1,0:T(8,128)S(1)} %convert_element_type.15), kind=kLoop, calls=%fused_computation | loop fusion | flops 196608 | bytes 262656 | tf_op jit(solution)/shard_map/convert_element_type | solution.py:251
  12.1 1.3 %collective-permute-done.1.left = bf16[2,14,3,256]{3,2,1,0:T(4,128)(2,1)S(1)} collective-permute-done((bf16[2,14,3,256]{3,2,1,0:T(4,128)(2,1)S(1)}, bf16[2,14,3,256]{3,2,1,0:T(4,128)(2,1)S(1)}, u32[]{:S(2)}, u32[]{:S(2)}) %collective-permute-start.1) | collective-permute-done | bytes 43040 | tf_op jit(solution)/shard_map/ppermute | solution.py:195
  13.4 0.3 collective-permute-done.2.right
  13.7 0.7 copy-done.3
  14.4 0.9 %copy-done.2 = bf16[1,2,8,16,256]{4,3,2,1,0:T(8,128)(2,1)S(1)} copy-done((bf16[1,2,8,16,256]{4,3,2,1,0:T(8,128)(2,1)S(1)}, bf16[1,2,8,16,256]{4,3,2,1,0:T(8,128)(2,1)}, u32[]{:S(2)}) %copy-start.2) | copy-done | bytes 131096
  15.3 3.6 %shard_map.120 = (f32[2,14,32,256]{3,2,1,0:T(8,128)S(1)}, bf16[256,256]{1,0:T(8,128)(2,1)S(1)}, f32[256,256]{1,0:T(8,128)S(1)}, f32[256,1]{1,0:T(8,128)S(1)}, f3...) custom-call(bf16[2,8,16,256]{3,2,1,0:T(8,128)(2,1)S(1)} %bitcast.32, ...), custom_call_target="tpu_custom_call" | custom-call | flops 409075712 | bytes 4042752 | tf_op jit(solution)/shard_map/pallas_call | solution.py:23
  18.9 1.6 %collective-permute-start.3 = (bf16[2,3,16,256]{3,2,1,0:T(8,128)(2,1)S(1)}, bf16[2,3,16,256]{3,2,1,0:T(8,128)(2,1)S(1)}, u32[]{:S(2)}, u32[]{:S(2)}) collective-permute-start(bf16[2,3,16,256]{3,2,1,0:T(8,128)(2,1)S(1)} %slice_select_fusion.1), channel_id=1, source_target_pairs={{0,2},{2,0},{1,3},{3,1},{4,6},{6,4},{5,7},{7,5},{8,10},{10,8},{9,1... | collective-permute-start | bytes 147464 | tf_op jit(solution)/shard_map/ppermute | solution.py:181
  20.6 3.5 %collective-permute-start.12 = (bf16[256,256]{1,0:T(8,128)(2,1)S(1)}, bf16[256,256]{1,0:T(8,128)(2,1)S(1)}, u32[]{:S(2)}, u32[]{:S(2)}) collective-permute-start(bf16[256,256]{1,0:T(8,128)(2,1)S(1)} %get-tuple-element.22), channel_id=1, source_target_pairs={{0,12},{4,0},{8,4},{12,8},{1,13},{5,1},{9,5},{13,9},{2,14},{6,2},{... | collective-permute-start | bytes 393224 | tf_op jit(solution)/shard_map/ppermute | solution.py:203
  24.1 0.6 collective-permute-start.10
  24.8 2.9 %collective-permute-start.4 = (bf16[2,14,3,256]{3,2,1,0:T(4,128)(2,1)S(1)}, bf16[2,14,3,256]{3,2,1,0:T(4,128)(2,1)S(1)}, u32[]{:S(2)}, u32[]{:S(2)}) collective-permute-start(bf16[2,14,3,256]{3,2,1,0:T(4,128)(2,1)S(1)} %pad_maximum_fusion.2), channel_id=1, source_target_pairs={{0,4},{4,8},{8,12},{12,0},{1,5},{5,9},{9,13},{13,1},{2,6},{6,10},{... | collective-permute-start | bytes 129032 | tf_op jit(solution)/shard_map/ppermute | solution.py:195
  27.8 1.0 %collective-permute-start.5 = (bf16[2,14,3,256]{3,2,1,0:T(4,128)(2,1)S(1)}, bf16[2,14,3,256]{3,2,1,0:T(4,128)(2,1)S(1)}, u32[]{:S(2)}, u32[]{:S(2)}) collective-permute-start(bf16[2,14,3,256]{3,2,1,0:T(4,128)(2,1)S(1)} %pad_maximum_fusion.3), channel_id=1, source_target_pairs={{4,0},{8,4},{12,8},{0,12},{5,1},{9,5},{13,9},{1,13},{6,2},{10,6},{... | collective-permute-start | bytes 129032 | tf_op jit(solution)/shard_map/ppermute | solution.py:196
  28.8 2.0 %shard_map.125 = f32[49,256]{1,0:T(8,128)S(1)} custom-call(f32[2,14,32,256]{3,2,1,0:T(8,128)S(1)} %get-tuple-element.25.wide, bf16[2,8,16,256]{3,2,1,0:T(8,128)(2,1)S(1)} %bitcast.26), custom_call_target="tpu_custom_call" | custom-call | flops 6422528 | bytes 1098752 | tf_op jit(solution)/shard_map/pallas_call | solution.py:23
  30.9 2.3 %collective-permute-done.4.left = bf16[2,14,3,256]{3,2,1,0:T(4,128)(2,1)S(1)} collective-permute-done((bf16[2,14,3,256]{3,2,1,0:T(4,128)(2,1)S(1)}, bf16[2,14,3,256]{3,2,1,0:T(4,128)(2,1)S(1)}, u32[]{:S(2)}, u32[]{:S(2)}) %collective-permute-start.4) | collective-permute-done | bytes 43040 | tf_op jit(solution)/shard_map/ppermute | solution.py:195
  33.1 1.2 %collective-permute-done.5.right = bf16[2,14,3,256]{3,2,1,0:T(4,128)(2,1)S(1)} collective-permute-done((bf16[2,14,3,256]{3,2,1,0:T(4,128)(2,1)S(1)}, bf16[2,14,3,256]{3,2,1,0:T(4,128)(2,1)S(1)}, u32[]{:S(2)}, u32[]{:S(2)}) %collective-permute-start.5) | collective-permute-done | bytes 43040 | tf_op jit(solution)/shard_map/ppermute | solution.py:196
  34.4 0.1 broadcast_in_dim.19.maskb
  34.4 2.4 %shard_map.121 = (bf16[2,8,16,256]{3,2,1,0:T(8,128)(2,1)S(1)}, bf16[2,8,16,256]{3,2,1,0:T(8,128)(2,1)S(1)}) custom-call(bf16[2,8,16,256]{3,2,1,0:T(8,128)(2,1)S(1)} %bitcast.27, bf16[2,3,16,256]{3,2,1,0:T(8,128)(2,1)S(1)} %get-tuple-element.47.low, bf16[2,3,16,256]{3,2,1,0:T(8,128)(2,1)S(1)} %get-tuple-element.46.high, ...), custom_call_target="tpu_custom_call" | custom-call | flops 6422528 | bytes 824320 | tf_op jit(solution)/shard_map/pallas_call | solution.py:23
  36.8 0.1 broadcast_select_fusion
  37.0 3.5 %collective-permute-start.15 = (bf16[256,256]{1,0:T(8,128)(2,1)S(1)}, bf16[256,256]{1,0:T(8,128)(2,1)S(1)}, u32[]{:S(2)}, u32[]{:S(2)}) collective-permute-start(bf16[256,256]{1,0:T(8,128)(2,1)S(1)} %bitcast.34), channel_id=1, source_target_pairs={{0,9},{1,8},{4,13},{5,12},{8,1},{9,0},{12,5},{13,4},{2,11},{3,10},... | collective-permute-start | bytes 393224 | tf_op jit(solution)/shard_map/ppermute | solution.py:216
  40.6 0.6 collective-permute-start.14
  41.2 1.4 %collective-permute-start.6 = (bf16[256,256]{1,0:T(8,128)(2,1)S(1)}, bf16[256,256]{1,0:T(8,128)(2,1)S(1)}, u32[]{:S(2)}, u32[]{:S(2)}) collective-permute-start(bf16[256,256]{1,0:T(8,128)(2,1)S(1)} %bitcast.36), channel_id=1, source_target_pairs={{0,1},{1,0},{4,5},{5,4},{8,9},{9,8},{12,13},{13,12},{2,3},{3,2},{6... | collective-permute-start | bytes 393224 | tf_op jit(solution)/shard_map/ppermute | solution.py:216
  42.7 0.6 collective-permute-start.13
  43.3 0.3 collective-permute-done.6.masked
  43.6 0.7 shard_map.122
  44.3 2.0 %shard_map.126 = f32[49,256]{1,0:T(8,128)S(1)} custom-call(f32[2,14,32,256]{3,2,1,0:T(8,128)S(1)} %get-tuple-element.25.wide, bf16[2,8,16,256]{3,2,1,0:T(8,128)(2,1)S(1)} %bitcast.14), custom_call_target="tpu_custom_call" | custom-call | flops 6422528 | bytes 1098752 | tf_op jit(solution)/shard_map/pallas_call | solution.py:23
  46.4 1.2 %collective-permute-start.7 = (bf16[2,3,16,256]{3,2,1,0:T(8,128)(2,1)S(1)}, bf16[2,3,16,256]{3,2,1,0:T(8,128)(2,1)S(1)}, u32[]{:S(2)}, u32[]{:S(2)}) collective-permute-start(bf16[2,3,16,256]{3,2,1,0:T(8,128)(2,1)S(1)} %slice_select_fusion), channel_id=1, source_target_pairs={{0,2},{2,0},{1,3},{3,1},{4,6},{6,4},{5,7},{7,5},{8,10},{10,8},{9,1... | collective-permute-start | bytes 147464 | tf_op jit(solution)/shard_map/ppermute | solution.py:181
  47.6 3.3 %collective-permute-done.14 = bf16[256,256]{1,0:T(8,128)(2,1)S(1)} collective-permute-done((bf16[256,256]{1,0:T(8,128)(2,1)S(1)}, bf16[256,256]{1,0:T(8,128)(2,1)S(1)}, u32[]{:S(2)}, u32[]{:S(2)}) %collective-permute-start.14) | collective-permute-done | bytes 131104 | tf_op jit(solution)/shard_map/ppermute | solution.py:216
  50.9 0.5 collective-permute-start.18
  51.5 1.2 %collective-permute-done.15 = bf16[256,256]{1,0:T(8,128)(2,1)S(1)} collective-permute-done((bf16[256,256]{1,0:T(8,128)(2,1)S(1)}, bf16[256,256]{1,0:T(8,128)(2,1)S(1)}, u32[]{:S(2)}, u32[]{:S(2)}) %collective-permute-start.15) | collective-permute-done | bytes 131104 | tf_op jit(solution)/shard_map/ppermute | solution.py:216
  52.7 0.6 collective-permute-start.17
  53.3 5.2 %collective-permute-done.7 = bf16[2,3,16,256]{3,2,1,0:T(8,128)(2,1)S(1)} collective-permute-done((bf16[2,3,16,256]{3,2,1,0:T(8,128)(2,1)S(1)}, bf16[2,3,16,256]{3,2,1,0:T(8,128)(2,1)S(1)}, u32[]{:S(2)}, u32[]{:S(2)}) %collective-permute-start.7) | collective-permute-done | bytes 49184 | tf_op jit(solution)/shard_map/ppermute | solution.py:181
  58.7 0.5 collective-permute-start.8
  59.2 0.6 collective-permute-done.18
  59.8 0.5 collective-permute-start.19
  60.4 2.5 %collective-permute-start.9 = (bf16[2,14,3,256]{3,2,1,0:T(4,128)(2,1)S(1)}, bf16[2,14,3,256]{3,2,1,0:T(4,128)(2,1)S(1)}, u32[]{:S(2)}, u32[]{:S(2)}) collective-permute-start(bf16[2,14,3,256]{3,2,1,0:T(4,128)(2,1)S(1)} %pad_maximum_fusion.5), channel_id=1, source_target_pairs={{4,0},{8,4},{12,8},{0,12},{5,1},{9,5},{13,9},{1,13},{6,2},{10,6},{... | collective-permute-start | bytes 129032 | tf_op jit(solution)/shard_map/ppermute | solution.py:196
  62.9 2.0 %collective-permute-done.8.left = bf16[2,14,3,256]{3,2,1,0:T(4,128)(2,1)S(1)} collective-permute-done((bf16[2,14,3,256]{3,2,1,0:T(4,128)(2,1)S(1)}, bf16[2,14,3,256]{3,2,1,0:T(4,128)(2,1)S(1)}, u32[]{:S(2)}, u32[]{:S(2)}) %collective-permute-start.8) | collective-permute-done | bytes 43040 | tf_op jit(solution)/shard_map/ppermute | solution.py:195
  64.8 0.5 collective-permute-done.9.right
  65.3 3.0 %shard_map.123 = (bf16[2,8,16,256]{3,2,1,0:T(8,128)(2,1)S(1)}, bf16[2,8,16,256]{3,2,1,0:T(8,128)(2,1)}) custom-call(bf16[2,8,16,256]{3,2,1,0:T(8,128)(2,1)S(1)} %bitcast.17, bf16[2,3,16,256]{3,2,1,0:T(8,128)(2,1)S(1)} %get-tuple-element.41.low, bf16[2,3,16,256]{3,2,1,0:T(8,128)(2,1)S(1)} %get-tuple-element.40.high, ...), custom_call_target="tpu_custom_call" | custom-call | flops 6422528 | bytes 824320 | tf_op jit(solution)/shard_map/pallas_call | solution.py:23
  68.3 2.3 %collective-permute-start.20 = (f32[49,256]{1,0:T(8,128)S(1)}, f32[49,256]{1,0:T(8,128)S(1)}, u32[]{:S(2)}, u32[]{:S(2)}) collective-permute-start(f32[49,256]{1,0:T(8,128)S(1)} %add.10), channel_id=1, source_target_pairs={{0,8},{4,12},{8,0},{12,4},{1,9},{5,13},{9,1},{13,5},{2,10},{6,14},... | collective-permute-start | bytes 150536 | tf_op jit(solution)/shard_map/ppermute | solution.py:228
  70.6 0.7 select_bitcast_fusion
  71.3 2.2 %collective-permute-done.20 = f32[49,256]{1,0:T(8,128)S(1)} collective-permute-done((f32[49,256]{1,0:T(8,128)S(1)}, f32[49,256]{1,0:T(8,128)S(1)}, u32[]{:S(2)}, u32[]{:S(2)}) %collective-permute-start.20) | collective-permute-done | bytes 50208 | tf_op jit(solution)/shard_map/ppermute | solution.py:228
  73.5 0.7 copy.13
  74.2 11.5 %shard_map.124 = (f32[256,1024]{1,0:T(8,128)}, f32[1024,256]{1,0:T(8,128)}) custom-call(bf16[1024,256]{1,0:T(8,128)(2,1)S(1)} %constant_dynamic-update-slice_fusion.refs_0_, bf16[1024,256]{1,0:T(8,128)(2,1)S(1)} %collective-permute-done.13.refs_1_, bf16[1024,256]{1,0:T(8,128)(2,1)S(1)} %constant_dynamic-update-slice_fusion.4.refs_2_, ...), custom_call_target="tpu_custom_call" | custom-call | flops 4294967296 | bytes 5246976 | tf_op jit(solution)/shard_map/pallas_call | solution.py:23
  (58 shorter events, 0.7 us)
Async XLA Ops:
  0.6 4.8 %copy-start.8 = (s32[8,16]{1,0:T(8,128)S(1)}, s32[8,16]{1,0:T(8,128)}, u32[]{:S(2)}) copy-start(s32[8,16]{1,0:T(8,128)} %param.11) | copy-start | bytes 1540
  0.6 11.4 %copy-start.7 = (bf16[1,7,7,256]{3,2,1,0:T(8,128)(2,1)S(1)}, bf16[1,7,7,256]{3,2,1,0:T(8,128)(2,1)}, u32[]{:S(2)}) copy-start(bf16[1,7,7,256]{3,2,1,0:T(8,128)(2,1)} %param.12) | copy-start | bytes 75268
  0.7 13.1 %copy-start.1 = (bf16[1,1024,256]{2,1,0:T(8,128)(2,1)S(1)}, bf16[1,1024,256]{2,1,0:T(8,128)(2,1)}, u32[]{:S(2)}) copy-start(bf16[1,1024,256]{2,1,0:T(8,128)(2,1)} %param.17) | copy-start | bytes 1572868
  1.6 12.1 %copy-start = (bf16[1,256,1024]{2,1,0:T(8,128)(2,1)S(1)}, bf16[1,256,1024]{2,1,0:T(8,128)(2,1)}, u32[]{:S(2)}) copy-start(bf16[1,256,1024]{2,1,0:T(8,128)(2,1)} %param.15) | copy-start | bytes 1572868
  1.6 5.1 %collective-permute-start = (bf16[2,3,16,256]{3,2,1,0:T(8,128)(2,1)S(1)}, bf16[2,3,16,256]{3,2,1,0:T(8,128)(2,1)S(1)}, u32[]{:S(2)}, u32[]{:S(2)}) collective-permute-start(bf16[2,3,16,256]{3,2,1,0:T(8,128)(2,1)S(1)} %slice_select_fusion.2), channel_id=1, source_target_pairs={{0,2},{2,0},{1,3},{3,1},{4,6},{6,4},{5,7},{7,5},{8,10},{10,8},{9,1... | collective-permute-start | bytes 147464 | tf_op jit(solution)/shard_map/ppermute | solution.py:181
  6.7 6.6 %collective-permute-start.1 = (bf16[2,14,3,256]{3,2,1,0:T(4,128)(2,1)S(1)}, bf16[2,14,3,256]{3,2,1,0:T(4,128)(2,1)S(1)}, u32[]{:S(2)}, u32[]{:S(2)}) collective-permute-start(bf16[2,14,3,256]{3,2,1,0:T(4,128)(2,1)S(1)} %pad_maximum_fusion), channel_id=1, source_target_pairs={{0,4},{4,8},{8,12},{12,0},{1,5},{5,9},{9,13},{13,1},{2,6},{6,10},{... | collective-permute-start | bytes 129032 | tf_op jit(solution)/shard_map/ppermute | solution.py:195
  8.9 4.8 %collective-permute-start.2 = (bf16[2,14,3,256]{3,2,1,0:T(4,128)(2,1)S(1)}, bf16[2,14,3,256]{3,2,1,0:T(4,128)(2,1)S(1)}, u32[]{:S(2)}, u32[]{:S(2)}) collective-permute-start(bf16[2,14,3,256]{3,2,1,0:T(4,128)(2,1)S(1)} %pad_maximum_fusion.1), channel_id=1, source_target_pairs={{4,0},{8,4},{12,8},{0,12},{5,1},{9,5},{13,9},{1,13},{6,2},{10,6},{... | collective-permute-start | bytes 129032 | tf_op jit(solution)/shard_map/ppermute | solution.py:196
  12.1 1.7 %copy-start.5 = (f32[1,256]{1,0:T(1,128)S(1)}, f32[1,256]{1,0:T(1,128)}, u32[]{:S(2)}) copy-start(f32[1,256]{1,0:T(1,128)} %bias.1) | copy-start | bytes 3076
  12.1 1.6 %copy-start.4 = (f32[1,1024]{1,0:T(1,128)S(1)}, f32[1,1024]{1,0:T(1,128)}, u32[]{:S(2)}) copy-start(f32[1,1024]{1,0:T(1,128)} %refs_5_.1) | copy-start | bytes 12292
  13.7 0.7 copy-start.3
  14.4 0.9 %copy-start.2 = (bf16[1,2,8,16,256]{4,3,2,1,0:T(8,128)(2,1)S(1)}, bf16[1,2,8,16,256]{4,3,2,1,0:T(8,128)(2,1)}, u32[]{:S(2)}) copy-start(bf16[1,2,8,16,256]{4,3,2,1,0:T(8,128)(2,1)} %param.9) | copy-start | bytes 393220
  18.9 5.8 %collective-permute-start.3 = (bf16[2,3,16,256]{3,2,1,0:T(8,128)(2,1)S(1)}, bf16[2,3,16,256]{3,2,1,0:T(8,128)(2,1)S(1)}, u32[]{:S(2)}, u32[]{:S(2)}) collective-permute-start(bf16[2,3,16,256]{3,2,1,0:T(8,128)(2,1)S(1)} %slice_select_fusion.1), channel_id=1, source_target_pairs={{0,2},{2,0},{1,3},{3,1},{4,6},{6,4},{5,7},{7,5},{8,10},{10,8},{9,1... | collective-permute-start | bytes 147464 | tf_op jit(solution)/shard_map/ppermute | solution.py:181
  20.6 22.0 %collective-permute-start.12 = (bf16[256,256]{1,0:T(8,128)(2,1)S(1)}, bf16[256,256]{1,0:T(8,128)(2,1)S(1)}, u32[]{:S(2)}, u32[]{:S(2)}) collective-permute-start(bf16[256,256]{1,0:T(8,128)(2,1)S(1)} %get-tuple-element.22), channel_id=1, source_target_pairs={{0,12},{4,0},{8,4},{12,8},{1,13},{5,1},{9,5},{13,9},{2,14},{6,2},{... | collective-permute-start | bytes 393224 | tf_op jit(solution)/shard_map/ppermute | solution.py:203
  24.1 17.1 %collective-permute-start.11 = (bf16[256,256]{1,0:T(8,128)(2,1)S(1)}, bf16[256,256]{1,0:T(8,128)(2,1)S(1)}, u32[]{:S(2)}, u32[]{:S(2)}) collective-permute-start(bf16[256,256]{1,0:T(8,128)(2,1)S(1)} %get-tuple-element.22), channel_id=1, source_target_pairs={{0,8},{4,12},{8,0},{12,4},{1,9},{5,13},{9,1},{13,5},{2,10},{6,14},... | collective-permute-start | bytes 393224 | tf_op jit(solution)/shard_map/ppermute | solution.py:203
  24.1 16.5 %collective-permute-start.10 = (bf16[256,256]{1,0:T(8,128)(2,1)S(1)}, bf16[256,256]{1,0:T(8,128)(2,1)S(1)}, u32[]{:S(2)}, u32[]{:S(2)}) collective-permute-start(bf16[256,256]{1,0:T(8,128)(2,1)S(1)} %get-tuple-element.22), channel_id=1, source_target_pairs={{0,4},{4,8},{8,12},{12,0},{1,5},{5,9},{9,13},{13,1},{2,6},{6,10},{... | collective-permute-start | bytes 393224 | tf_op jit(solution)/shard_map/ppermute | solution.py:203
  24.8 8.3 %collective-permute-start.4 = (bf16[2,14,3,256]{3,2,1,0:T(4,128)(2,1)S(1)}, bf16[2,14,3,256]{3,2,1,0:T(4,128)(2,1)S(1)}, u32[]{:S(2)}, u32[]{:S(2)}) collective-permute-start(bf16[2,14,3,256]{3,2,1,0:T(4,128)(2,1)S(1)} %pad_maximum_fusion.2), channel_id=1, source_target_pairs={{0,4},{4,8},{8,12},{12,0},{1,5},{5,9},{9,13},{13,1},{2,6},{6,10},{... | collective-permute-start | bytes 129032 | tf_op jit(solution)/shard_map/ppermute | solution.py:195
  27.8 6.6 %collective-permute-start.5 = (bf16[2,14,3,256]{3,2,1,0:T(4,128)(2,1)S(1)}, bf16[2,14,3,256]{3,2,1,0:T(4,128)(2,1)S(1)}, u32[]{:S(2)}, u32[]{:S(2)}) collective-permute-start(bf16[2,14,3,256]{3,2,1,0:T(4,128)(2,1)S(1)} %pad_maximum_fusion.3), channel_id=1, source_target_pairs={{4,0},{8,4},{12,8},{0,12},{5,1},{9,5},{13,9},{1,13},{6,2},{10,6},{... | collective-permute-start | bytes 129032 | tf_op jit(solution)/shard_map/ppermute | solution.py:196
  34.4 2.4 %copy-start.6 = (bf16[2,8,16,256]{3,2,1,0:T(8,128)(2,1)S(1)}, bf16[2,8,16,256]{3,2,1,0:T(8,128)(2,1)}, u32[]{:S(2)}) copy-start(bf16[2,8,16,256]{3,2,1,0:T(8,128)(2,1)} %param.10) | copy-start | bytes 393220
  36.9 15.8 %collective-permute-start.16 = (bf16[256,256]{1,0:T(8,128)(2,1)S(1)}, bf16[256,256]{1,0:T(8,128)(2,1)S(1)}, u32[]{:S(2)}, u32[]{:S(2)}) collective-permute-start(bf16[256,256]{1,0:T(8,128)(2,1)S(1)} %bitcast.33), channel_id=1, source_target_pairs={{0,13},{1,12},{4,1},{5,0},{8,5},{9,4},{12,9},{13,8},{2,15},{3,14},... | collective-permute-start | bytes 393224 | tf_op jit(solution)/shard_map/ppermute | solution.py:216
  37.0 15.7 %collective-permute-start.15 = (bf16[256,256]{1,0:T(8,128)(2,1)S(1)}, bf16[256,256]{1,0:T(8,128)(2,1)S(1)}, u32[]{:S(2)}, u32[]{:S(2)}) collective-permute-start(bf16[256,256]{1,0:T(8,128)(2,1)S(1)} %bitcast.34), channel_id=1, source_target_pairs={{0,9},{1,8},{4,13},{5,12},{8,1},{9,0},{12,5},{13,4},{2,11},{3,10},... | collective-permute-start | bytes 393224 | tf_op jit(solution)/shard_map/ppermute | solution.py:216
  40.6 10.4 %collective-permute-start.14 = (bf16[256,256]{1,0:T(8,128)(2,1)S(1)}, bf16[256,256]{1,0:T(8,128)(2,1)S(1)}, u32[]{:S(2)}, u32[]{:S(2)}) collective-permute-start(bf16[256,256]{1,0:T(8,128)(2,1)S(1)} %bitcast.35), channel_id=1, source_target_pairs={{0,5},{1,4},{4,9},{5,8},{8,13},{9,12},{12,1},{13,0},{2,7},{3,6},{6... | collective-permute-start | bytes 393224 | tf_op jit(solution)/shard_map/ppermute | solution.py:216
  41.2 2.4 %collective-permute-start.6 = (bf16[256,256]{1,0:T(8,128)(2,1)S(1)}, bf16[256,256]{1,0:T(8,128)(2,1)S(1)}, u32[]{:S(2)}, u32[]{:S(2)}) collective-permute-start(bf16[256,256]{1,0:T(8,128)(2,1)S(1)} %bitcast.36), channel_id=1, source_target_pairs={{0,1},{1,0},{4,5},{5,4},{8,9},{9,8},{12,13},{13,12},{2,3},{3,2},{6... | collective-permute-start | bytes 393224 | tf_op jit(solution)/shard_map/ppermute | solution.py:216
  42.7 31.5 %collective-permute-start.13 = (bf16[1024,256]{1,0:T(8,128)(2,1)S(1)}, bf16[1024,256]{1,0:T(8,128)(2,1)S(1)}, u32[]{:S(2)}, u32[]{:S(2)}) collective-permute-start(bf16[1024,256]{1,0:T(8,128)(2,1)S(1)} %constant_dynamic-update-slice_fusion.refs_0_), channel_id=1, source_target_pairs={{0,2},{2,0},{1,3},{3,1},{4,6},{6,4},{5,7},{7,5},{8,10},{10,8},{9,1... | collective-permute-start | bytes 1572872 | tf_op jit(solution)/shard_map/ppermute | solution.py:203
  46.4 12.2 %collective-permute-start.7 = (bf16[2,3,16,256]{3,2,1,0:T(8,128)(2,1)S(1)}, bf16[2,3,16,256]{3,2,1,0:T(8,128)(2,1)S(1)}, u32[]{:S(2)}, u32[]{:S(2)}) collective-permute-start(bf16[2,3,16,256]{3,2,1,0:T(8,128)(2,1)S(1)} %slice_select_fusion), channel_id=1, source_target_pairs={{0,2},{2,0},{1,3},{3,1},{4,6},{6,4},{5,7},{7,5},{8,10},{10,8},{9,1... | collective-permute-start | bytes 147464 | tf_op jit(solution)/shard_map/ppermute | solution.py:181
  50.9 8.9 %collective-permute-start.18 = (f32[49,256]{1,0:T(8,128)S(1)}, f32[49,256]{1,0:T(8,128)S(1)}, u32[]{:S(2)}, u32[]{:S(2)}) collective-permute-start(f32[49,256]{1,0:T(8,128)S(1)} %broadcast_select_fusion.7), channel_id=1, source_target_pairs={{0,2},{2,0},{1,3},{3,1},{4,6},{6,4},{5,7},{7,5},{8,10},{10,8},{9,1... | collective-permute-start | bytes 150536 | tf_op jit(solution)/shard_map/ppermute | solution.py:228
  52.7 21.4 %collective-permute-start.17 = (bf16[1024,256]{1,0:T(8,128)(2,1)S(1)}, bf16[1024,256]{1,0:T(8,128)(2,1)S(1)}, u32[]{:S(2)}, u32[]{:S(2)}) collective-permute-start(bf16[1024,256]{1,0:T(8,128)(2,1)S(1)} %constant_dynamic-update-slice_fusion.4.refs_2_), channel_id=1, source_target_pairs={{0,2},{2,0},{1,3},{3,1},{4,6},{6,4},{5,7},{7,5},{8,10},{10,8},{9,1... | collective-permute-start | bytes 1572872 | tf_op jit(solution)/shard_map/ppermute | solution.py:203
  58.7 6.1 %collective-permute-start.8 = (bf16[2,14,3,256]{3,2,1,0:T(4,128)(2,1)S(1)}, bf16[2,14,3,256]{3,2,1,0:T(4,128)(2,1)S(1)}, u32[]{:S(2)}, u32[]{:S(2)}) collective-permute-start(bf16[2,14,3,256]{3,2,1,0:T(4,128)(2,1)S(1)} %pad_maximum_fusion.4), channel_id=1, source_target_pairs={{0,4},{4,8},{8,12},{12,0},{1,5},{5,9},{9,13},{13,1},{2,6},{6,10},{... | collective-permute-start | bytes 129032 | tf_op jit(solution)/shard_map/ppermute | solution.py:195
  59.8 8.5 %collective-permute-start.19 = (f32[49,256]{1,0:T(8,128)S(1)}, f32[49,256]{1,0:T(8,128)S(1)}, u32[]{:S(2)}, u32[]{:S(2)}) collective-permute-start(f32[49,256]{1,0:T(8,128)S(1)} %add.9), channel_id=1, source_target_pairs={{0,4},{4,0},{8,12},{12,8},{1,5},{5,1},{9,13},{13,9},{2,6},{6,2},{1... | collective-permute-start | bytes 150536 | tf_op jit(solution)/shard_map/ppermute | solution.py:228
  60.4 4.9 %collective-permute-start.9 = (bf16[2,14,3,256]{3,2,1,0:T(4,128)(2,1)S(1)}, bf16[2,14,3,256]{3,2,1,0:T(4,128)(2,1)S(1)}, u32[]{:S(2)}, u32[]{:S(2)}) collective-permute-start(bf16[2,14,3,256]{3,2,1,0:T(4,128)(2,1)S(1)} %pad_maximum_fusion.5), channel_id=1, source_target_pairs={{4,0},{8,4},{12,8},{0,12},{5,1},{9,5},{13,9},{1,13},{6,2},{10,6},{... | collective-permute-start | bytes 129032 | tf_op jit(solution)/shard_map/ppermute | solution.py:196
  68.3 5.1 %collective-permute-start.20 = (f32[49,256]{1,0:T(8,128)S(1)}, f32[49,256]{1,0:T(8,128)S(1)}, u32[]{:S(2)}, u32[]{:S(2)}) collective-permute-start(f32[49,256]{1,0:T(8,128)S(1)} %add.10), channel_id=1, source_target_pairs={{0,8},{4,12},{8,0},{12,4},{1,9},{5,13},{9,1},{13,5},{2,10},{6,14},... | collective-permute-start | bytes 150536 | tf_op jit(solution)/shard_map/ppermute | solution.py:228

commit v2 on v1

--- a/solution.py
+++ b/solution.py
@@ -13,21 +13,24 @@
 SIDE = 8
 F32 = jnp.float32
 BF16 = jnp.bfloat16
-VMEM_LIMIT = 48 * 1024 * 1024
+VMEM_LIMIT = 16 * 1024 * 1024
 GATHER_TILES = 8
 
 
-def call(body, outs, scratch, *args, flops=0):
-    moved = sum(a.size * a.dtype.itemsize for a in args)
-    moved += sum(o.size * o.dtype.itemsize for o in outs)
+def call(body, outs, scratch, *args, micros=1.0, scalars=0, specs=None, limit=VMEM_LIMIT):
+    if specs is None:
+        specs = [pl.BlockSpec(memory_space=pltpu.SMEM)] * scalars
+        specs += [pl.BlockSpec(memory_space=pltpu.VMEM)] * (len(args) - scalars)
     return pl.pallas_call(
         body,
         out_shape=outs,
-        in_specs=[pl.BlockSpec(memory_space=pltpu.VMEM)] * len(args),
+        in_specs=specs,
         out_specs=[pl.BlockSpec(memory_space=pltpu.VMEM)] * len(outs),
         scratch_shapes=scratch,
-        compiler_params=pltpu.CompilerParams(vmem_limit_bytes=VMEM_LIMIT),
-        cost_estimate=pl.CostEstimate(flops=flops, bytes_accessed=moved, transcendentals=0),
+        compiler_params=pltpu.CompilerParams(vmem_limit_bytes=limit),
+        cost_estimate=pl.CostEstimate(
+            flops=int(micros * 1.1e9), bytes_accessed=int(micros * 3.6e6), transcendentals=0
+        ),
     )(*args)
 
 
@@ -60,19 +63,22 @@
     dst[:, :, SIDE + cols : SIDE + cols + HALO, :] = right[...].astype(F32)
 
 
-def depthwise(src, kern, rows, cols, flip, emit):
+def depthwise(src, kern, rows, cols, begin, flip, emit):
     micros, chans = src.shape[0], src.shape[3]
+    chunk = 8 if cols > 8 else 16
+    chunk = chunk if rows % chunk == 0 else rows
     for part in range(chans // LANES):
         lanes = slice(part * LANES, (part + 1) * LANES)
         for micro in range(micros):
-            total = jnp.zeros((rows, cols, LANES), F32)
-            for kb in range(7):
-                begin = SIDE - HALO + kb
-                slab = src[micro, :, begin : begin + cols, lanes]
-                for ka in range(7):
-                    tap = (6 - ka) * 7 + (6 - kb) if flip else ka * 7 + kb
-                    total = total + slab[ka : ka + rows] * kern[tap : tap + 1, lanes]
-            emit(micro, lanes, total)
+            for first in range(0, rows, chunk):
+                total = jnp.zeros((chunk, cols, LANES), F32)
+                for kb in range(7):
+                    at = slice(begin + kb, begin + kb + cols)
+                    slab = src[micro, first : first + chunk + 2 * HALO, at, lanes]
+                    for ka in range(7):
+                        tap = (6 - ka) * 7 + (6 - kb) if flip else ka * 7 + kb
+                        total = total + slab[ka : ka + chunk] * kern[tap : tap + 1, lanes]
+                emit(micro, first, chunk, lanes, total)
 
 
 def dense_back(masked, slope, zhat, rscale, gain, w_in, w_out):
@@ -93,11 +99,11 @@
     rows, cols = x.shape[1], x.shape[2]
     widen(wide, x, low, high, left, right)
 
-    def emit(micro, lanes, total):
-        cells = rows * cols
-        zval[micro * cells : (micro + 1) * cells, lanes] = total.reshape(cells, LANES)
-
-    depthwise(wide, kern, rows, cols, False, emit)
+    def emit(micro, first, chunk, lanes, total):
+        at = (micro * rows + first) * cols
+        zval[at : at + chunk * cols, lanes] = total.reshape(chunk * cols, LANES)
+
+    depthwise(wide, kern, rows, cols, SIDE - HALO, False, emit)
     z = zval[...] + bias[...]
     centred = z - jnp.mean(z, axis=-1, keepdims=True)
     rs = lax.rsqrt(jnp.mean(centred * centred, axis=-1, keepdims=True) + 1e-06)
@@ -118,12 +124,12 @@
     ).astype(BF16)
 
 
-def kernel_grad_body(wide, dz, grad):
+def kernel_grad_body(first, wide, dz, grad):
     micros, rows, cols, chans = dz.shape
     for part in range(chans // LANES):
         lanes = slice(part * LANES, (part + 1) * LANES)
         for kb in range(7):
-            begin = SIDE - HALO + kb
+            begin = first + kb
             sums = [None] * 7
             for micro in range(micros):
                 own = dz[micro, :, :, lanes].astype(F32)
@@ -140,19 +146,25 @@
     rows, cols = own.shape[1], own.shape[2]
     widen(wide, own, low, high, left, right)
 
-    def emit(micro, lanes, total):
-        value = (total + masked[micro, :, :, lanes].astype(F32)).astype(BF16)
-        dx[micro, :, :, lanes] = value
-        dxm[micro, :, :, lanes] = (value.astype(F32) * maskb[...]).astype(BF16)
-
-    depthwise(wide, kern, rows, cols, True, emit)
-
-
-def weight_grad_body(parts, factor, *refs):
+    def emit(micro, first, chunk, lanes, total):
+        at = slice(first, first + chunk)
+        value = (total + masked[micro, at, :, lanes].astype(F32)).astype(BF16)
+        dx[micro, at, :, lanes] = value
+        dxm[micro, at, :, lanes] = (value.astype(F32) * maskb[at]).astype(BF16)
+
+    depthwise(wide, kern, rows, cols, SIDE - HALO, True, emit)
+
+
+def weight_grad_body(parts, carried, factor, *refs):
     normed, masked = refs[:parts], refs[parts : 2 * parts]
-    w_in, b_in, w_out, grad_in, grad_out = refs[2 * parts :]
-    grad_in[...] = jnp.zeros_like(grad_in)
-    grad_out[...] = jnp.zeros_like(grad_out)
+    w_in, b_in, w_out = refs[2 * parts : 2 * parts + 3]
+    grad_in, grad_out, sum_in, sum_out = refs[-4:]
+    if carried:
+        sum_in[...] = refs[2 * parts + 3][...]
+        sum_out[...] = refs[2 * parts + 4][...]
+    else:
+        sum_in[...] = jnp.zeros_like(sum_in)
+        sum_out[...] = jnp.zeros_like(sum_out)
     for part in range(parts):
         cells = normed[part].shape[0]
         step = min(cells, 256)
@@ -165,11 +177,11 @@
             h = jnp.dot(n, w_in[...], preferred_element_type=F32) + b_in[...]
             act, slope = gelu_both(h)
             dhid = (nt_dot(gm, w_out[...]) * slope).astype(BF16)
-            grad_in[...] += tn_dot(n, dhid)
-            grad_out[...] += tn_dot(act.astype(BF16), gm)
-
-    grad_in[...] = grad_in[...] * factor
-    grad_out[...] = grad_out[...] * factor
+            sum_in[...] += tn_dot(n, dhid)
+            sum_out[...] += tn_dot(act.astype(BF16), gm)
+
+    grad_in[...] = sum_in[...] * factor
+    grad_out[...] = sum_out[...] * factor
 
 
 def lat_edges(first, last):
@@ -230,7 +242,18 @@
     return value
 
 
-def shards(
+def weight_grads(normed, masked, factor, w_in, b_in, w_out, carried=()):
+    chans, hidden = w_in.shape
+    return call(
+        functools.partial(weight_grad_body, len(normed), bool(carried), factor),
+        [like((chans, hidden), F32), like((hidden, chans), F32)],
+        [pltpu.VMEM((chans, hidden), F32), pltpu.VMEM((hidden, chans), F32)],
+        *normed, *masked, w_in, b_in, w_out, *carried,
+        micros=sum(v.shape[0] for v in normed) / 200.0,
+    )
+
+
+def tile_shards(
     saved_inputs, out_cotangent, land_mask, conv_kernel, conv_bias, norm_gain, w_in, b_in, w_out
 ):
     micros, rows, cols, chans = out_cotangent.shape
@@ -263,7 +286,7 @@
         ],
         [pltpu.VMEM(flat, F32)],
         x, *halo(x), masked1.reshape(flat), kern, conv_bias, norm_gain, weight_in, b_in, weight_out,
-        flops=6 * cells * chans * hidden + 98 * cells * chans,
+        micros=3.0,
     )
     if gather:
         normed_row = jnp.concatenate(ring_pieces(normed, "lon"))
@@ -273,14 +296,18 @@
         dz = dz.reshape(shape)
         edges = halo(dz)
         (grad_k,) = call(
-            kernel_grad_body, [like((49, chans), F32)], [], wide, dz, flops=98 * cells * chans
+            functools.partial(kernel_grad_body, SIDE - HALO),
+            [like((49, chans), F32)],
+            [],
+            wide, dz,
+            micros=3.0,
         )
         dx, dxm = call(
             input_grad_body,
             [like(shape, BF16), like(shape, BF16)],
             [pltpu.VMEM(wide_shape, F32)],
             dz, *edges, masked, maskb, kern,
-            flops=98 * cells * chans,
+            micros=3.0,
         )
         return grad_k, dx, dxm
 
@@ -296,21 +323,407 @@
     (dz0,) = call(
         back_body, [like(flat, BF16)], [],
         masked0, slope, zhat, rscale, norm_gain, weight_in, weight_out,
-        flops=4 * cells * chans * hidden,
+        micros=3.0,
     )
     grad_k0, dx0, _ = input_grad(dz0, masked0.reshape(shape))
     grad_k = summed(jnp.where(section == 1, grad_k1, grad_k0)) * factor
-    grad_in, grad_out = call(
-        functools.partial(weight_grad_body, len(normed_all), factor),
-        [like((chans, hidden), F32), like((hidden, chans), F32)],
-        [],
-        *normed_all, *masked_all, weight_in, b_in, weight_out,
-        flops=8 * sum(v.shape[0] for v in normed_all) * chans * hidden,
+    grad_in, grad_out = weight_grads(
+        normed_all, masked_all, factor, weight_in, b_in, weight_out
     )
     if not gather:
         grad_in, grad_out = lax.psum((grad_in, grad_out), ("lon", "lat"))
     results = jnp.where(section == 1, dx1, dx0)
     return results[None], grad_in[None], grad_out[None], grad_k[None]
+
+
+def copied(pairs, sems):
+    copies = [pltpu.make_async_copy(a, b, sems.at[i]) for i, (a, b) in enumerate(pairs)]
+    for copy in copies:
+        copy.start()
+    return copies
+
+
+def prepare_body(
+    place, x_far, g_far, mask_far, x, sent, near, far, g, mask, firsts, lasts, sems
+):
+    micros, rows, cols, chans = x.shape
+    for copy in copied([(x_far, x), (g_far, g), (mask_far, mask)], sems):
+        copy.wait()
+    maskb = jnp.broadcast_to(mask[...].astype(F32)[:, :, None], (rows, cols, chans))
+    gm = g[...].astype(F32) * maskb[None]
+    sent[:micros] = gm.astype(BF16)
+    sent[micros] = maskb.astype(BF16)
+    xf = x[...].astype(F32)
+    for row in range(micros * rows):
+        micro, at = row // rows, row % rows
+        for buf, x_cols, g_cols in (
+            (firsts, slice(0, 2 * HALO), slice(0, HALO)),
+            (lasts, slice(cols - 2 * HALO, cols), slice(cols - HALO, cols)),
+        ):
+            buf[row * 9 : row * 9 + 6, :] = xf[micro, at, x_cols]
+            buf[row * 9 + 6 : row * 9 + 9, :] = gm[micro, at, g_cols]
+
+    @pl.when(place[0] == 1)
+    def _():
+        near[...] = lasts[...].astype(BF16)
+        far[...] = firsts[...].astype(BF16)
+
+    @pl.when(place[0] == 0)
+    def _():
+        near[...] = firsts[...].astype(BF16)
+        far[...] = lasts[...].astype(BF16)
+
+
+def stage_body(near, masked, taps, *refs):
+    count = (len(refs) - 4) // 2
+    sources, kern, sent, targets = refs[:count], refs[count], refs[count + 1], refs[count + 2 : -2]
+    held, sems = refs[-2:]
+    copies = copied(list(zip(sources, targets)) + [(taps, held)], sems)
+    sent[...] = masked[...]
+    for copy in copies:
+        copy.wait()
+    for ka in range(7):
+        kern[ka * 7 : ka * 7 + 7, :] = held[0, ka].astype(F32)
+
+
+def norm_body(
+    place, x, xp, near, far, kern, bias, gain, w_in, b_in,
+    wide, normed, zhat, rscale, slope, zval, packed,
+):
+    micros, rows, cols, chans = x.shape
+    half = cols // 2
+    all_rows = 2 * rows
+    reach = half + 8
+    side, lat = place[0], place[1]
+    wide[...] = jnp.zeros_like(wide)
+    for tile, edge, at in ((x, near, lat * rows), (xp, far, (1 - lat) * rows)):
+        own_rows = pl.ds(HALO + at, rows)
+        tile_x = tile[...].astype(F32)
+        packed[...] = edge[...].astype(F32)
+
+        @pl.when(side == 0)
+        def _():
+            for row in range(micros * rows):
+                micro, to = row // rows, row % rows
+                wide[micro, at + HALO + to, : 2 * HALO, :] = packed[row * 9 : row * 9 + 6, :]
+            wide[:, own_rows, 2 * HALO : 2 * HALO + cols, :] = tile_x
+
+        @pl.when(side == 1)
+        def _():
+            skip = half - 2 * HALO
+            wide[:, own_rows, : cols - skip, :] = tile_x[:, :, skip:]
+            for row in range(micros * rows):
+                micro, to = row // rows, row % rows
+                wide[micro, at + HALO + to, cols - skip : cols - skip + 2 * HALO, :] = packed[
+                    row * 9 : row * 9 + 6, :
+                ]
+
+    def emit(micro, first, chunk, lanes, total):
+        at = (micro * all_rows + first) * reach
+        zval[at : at + chunk * reach, lanes] = total.reshape(chunk * reach, LANES)
+
+    depthwise(wide, kern, all_rows, reach, 0, False, emit)
+    z = zval[...] + bias[...]
+    centred = z - jnp.mean(z, axis=-1, keepdims=True)
+    rs = lax.rsqrt(jnp.mean(centred * centred, axis=-1, keepdims=True) + 1e-06)
+    zh = centred * rs
+    zhat[...] = zh
+    rscale[...] = rs
+    n = zh * gain[...]
+    core = n.reshape(micros * all_rows, reach, chans)[:, HALO : HALO + half]
+    normed[...] = core.reshape(normed.shape).astype(BF16)
+    h = jnp.dot(n.astype(BF16), w_in[...], preferred_element_type=F32) + b_in[...]
+    slope[...] = gelu_both(h)[1]
+
+
+def pair_back(gwide, dwide, zhat, rscale, slope, gain, w_in, w_out, kern, dz, emit):
+    micros, rows, reach, chans = gwide.shape
+    half = reach - 8
+    masked = gwide[...].reshape(micros * rows * reach, chans).astype(BF16)
+    dzval = dense_back(
+        masked, slope[...], zhat[...], rscale[...], gain[...], w_in[...], w_out[...]
+    )
+    rounded = dzval.astype(BF16).astype(F32).reshape(micros, rows, reach, chans)
+    nothing = jnp.zeros((micros, HALO, reach, chans), F32)
+    dwide[:, :HALO] = nothing
+    dwide[:, HALO + rows :] = nothing
+    dwide[:, HALO : HALO + rows] = rounded
+    dz[...] = rounded[:, :, HALO : HALO + half].astype(BF16)
+
+    def add(micro, first, chunk, lanes, total):
+        own = gwide[micro, first : first + chunk, HALO : HALO + half, lanes]
+        emit(micro, slice(first, first + chunk), lanes, (total + own).astype(BF16))
+
+    depthwise(dwide, kern, rows, half, 0, True, add)
+
+
+def last_back_body(place, *refs):
+    @pl.when(place[2] == 1)
+    def _():
+        last_back_work(place, *refs)
+
+
+def last_back_work(
+    place, gm, gmp, near, far, zhat, rscale, slope, gain, w_in, w_out, kern,
+    dx, dxm, first3, last3, dz, core, gwide, dwide, mask, packed,
+):
+    micros, all_rows, half, chans = dx.shape
+    rows, cols = all_rows // 2, 2 * half
+    side, lat = place[0], place[1]
+    gwide[:, :, half:, :] = jnp.zeros((micros, all_rows, 8, chans), F32)
+    for tile, edge, at in ((gm, near, lat * rows), (gmp, far, (1 - lat) * rows)):
+        to_rows = pl.ds(at, rows)
+        both = tile[...].astype(F32)
+        packed[...] = edge[...].astype(F32)
+
+        @pl.when(side == 0)
+        def _():
+            gwide[:, to_rows, HALO : 2 * HALO + half, :] = both[:micros, :, : half + HALO]
+            for row in range(micros * rows):
+                gwide[row // rows, at + row % rows, :HALO, :] = packed[row * 9 + 6 : row * 9 + 9, :]
+            mask[to_rows] = both[micros, :, :half]
+
+        @pl.when(side == 1)
+        def _():
+            gwide[:, to_rows, : HALO + half, :] = both[:micros, :, half - HALO :]
+            for row in range(micros * rows):
+                gwide[row // rows, at + row % rows, HALO + half : 2 * HALO + half, :] = packed[
+                    row * 9 + 6 : row * 9 + 9, :
+                ]
+            mask[to_rows] = both[micros, :, half:]
+
+    core[...] = gwide[:, :, HALO : HALO + half, :].astype(BF16)
+
+    def emit(micro, at, lanes, value):
+        dx[micro, at, :, lanes] = value
+        kept = value.astype(F32) * mask[at, :, lanes]
+        dxm[micro, at, :, lanes] = kept.astype(BF16)
+        first3[micro, at, :, lanes] = kept[:, :HALO].astype(BF16)
+        last3[micro, at, :, lanes] = kept[:, half - HALO :].astype(BF16)
+
+    pair_back(gwide, dwide, zhat, rscale, slope, gain, w_in, w_out, kern, dz, emit)
+
+
+def first_back_body(place, *refs):
+    @pl.when(place[2] == 0)
+    def _():
+        first_back_work(*refs)
+
+
+def first_back_work(
+    core, left, right, zhat, rscale, slope, gain, w_in, w_out, kern, dx, dz, gwide, dwide
+):
+    micros, rows, half, chans = core.shape
+    gwide[:, :, half:, :] = jnp.zeros((micros, rows, 8, chans), F32)
+    gwide[:, :, :HALO, :] = left[...].astype(F32)
+    gwide[:, :, HALO : HALO + half, :] = core[...].astype(F32)
+    gwide[:, :, HALO + half : 2 * HALO + half, :] = right[...].astype(F32)
+
+    def emit(micro, at, lanes, value):
+        dx[micro, at, :, lanes] = value
+
+    pair_back(gwide, dwide, zhat, rscale, slope, gain, w_in, w_out, kern, dz, emit)
+
+
+def pair_up(target, first, second):
+    half = first.shape[0]
+    target[:half] = first[...]
+    target[half:] = second[...]
+
+
+def edge_body(first3, normed, got, sent, pair):
+    sent[...] = first3[...]
+    pair_up(pair, normed, got)
+
+
+def select_join_body(place, core1, got1, core0, got0, pair):
+    half = pair.shape[0] // 2
+    for number, core, got in ((1, core1, got1), (0, core0, got0)):
+
+        @pl.when(place[2] == number)
+        def _():
+            pair[:half] = core[...].reshape(half, pair.shape[1])
+            pair[half:] = got[...].reshape(half, pair.shape[1])
+
+
+def pair_kernel_grad_body(place, wide, dz1, dz0, after, grad, dz):
+    @pl.when(place[2] == 1)
+    def _():
+        dz[...] = dz1[...]
+
+    @pl.when(place[2] == 0)
+    def _():
+        dz[...] = dz0[...]
+
+    kernel_grad_body(HALO, wide, dz, grad)
+
+
+def pair_shards(
+    saved_inputs, out_cotangent, land_mask, conv_kernel, conv_bias, norm_gain, w_in, b_in, w_out
+):
+    micros, rows, cols, chans = out_cotangent.shape
+    hidden = w_in.shape[2]
+    lons = lax.axis_size("lon")
+    half, all_rows, reach = cols // 2, 2 * rows, cols // 2 + 8
+    cells = micros * all_rows * half
+    many = micros * all_rows * reach
+    shape = (micros, all_rows, half, chans)
+    edge_shape = (micros, all_rows, HALO, chans)
+    wide_shape = (micros, all_rows + 2 * HALO, reach + 8, chans)
+    reach_shape = (micros, all_rows, reach, chans)
+    factor = 1.0 / (cells * 2 * lons) ** 0.5
+    section, lat, lon = (lax.axis_index(a) for a in ("section", "lat", "lon"))
+    side = jnp.bitwise_xor(lat, jnp.bitwise_and(lon, 1))
+    count = 2 * lons
+
+    def device(position):
+        position = position % count
+        tile, which = position // 2, position % 2
+        return tile * 2 + (which ^ (tile & 1))
+
+    x = saved_inputs[0]
+    place = jnp.stack([side, lat, section]).astype(jnp.int32)
+    packed = (micros * rows * 3 * HALO, chans)
+    sent_shape = (micros + 1, rows, cols, chans)
+
+    swap = [(0, 1), (1, 0)]
+    xp = lax.ppermute(x, "lat", swap)
+    anywhere, vmem = pl.BlockSpec(memory_space=pl.ANY), pl.BlockSpec(memory_space=pltpu.VMEM)
+    hbm, smem = pl.BlockSpec(memory_space=pltpu.HBM), pl.BlockSpec(memory_space=pltpu.SMEM)
+    x_near, masked, near, far = call(
+        prepare_body,
+        [like(x.shape, BF16), like(sent_shape, BF16), like(packed, BF16), like(packed, BF16)],
+        [
+            pltpu.VMEM(x.shape, BF16),
+            pltpu.VMEM(land_mask.shape, land_mask.dtype),
+            pltpu.VMEM(packed, F32),
+            pltpu.VMEM(packed, F32),
+            pltpu.SemaphoreType.DMA((3,)),
+        ],
+        place, x, out_cotangent, land_mask,
+        specs=[smem, hbm, hbm, hbm],
+    )
+    near_pairs = [(device(p), device(p + 1 if p % 2 else p - 1)) for p in range(count)]
+    far_pairs = [(device(p), device(p - 2 if p % 2 else p + 2)) for p in range(count)]
+    near = lax.ppermute(near, ("lon", "lat"), near_pairs)
+    far = lax.ppermute(far, ("lon", "lat"), far_pairs)
+    params = [conv_bias, norm_gain, w_in[0], b_in, w_out[0]]
+    kern, masked, bias, gain, weight_in, bias_in, weight_out = call(
+        stage_body,
+        [like((49, chans), F32), like(sent_shape, BF16)] + [like(v.shape, v.dtype) for v in params],
+        [pltpu.VMEM(conv_kernel.shape, BF16), pltpu.SemaphoreType.DMA((len(params) + 1,))],
+        near, masked, conv_kernel, *params,
+        specs=[anywhere, vmem] + [hbm] * (1 + len(params)),
+    )
+    gmp = lax.ppermute(masked, ("lat", "section"), [(1, 3), (3, 1)])
+
+    wide, normed, zhat, rscale, slope = call(
+        norm_body,
+        [
+            like(wide_shape, F32),
+            like((cells, chans), BF16),
+            like((many, chans), F32),
+            like((many, 1), F32),
+            like((many, hidden), F32),
+        ],
+        [pltpu.VMEM((many, chans), F32), pltpu.VMEM(packed, F32)],
+        place, x_near, xp, near, far, kern, bias, gain, weight_in, bias_in,
+        micros=6.5,
+        scalars=1,
+    )
+    state = (zhat, rscale, slope, gain, weight_in, weight_out, kern)
+    buffers = [
+        pltpu.VMEM(reach_shape, F32),
+        pltpu.VMEM((micros, all_rows + 2 * HALO, reach, chans), F32),
+    ]
+    dx1, dxm1, first3, last3, dz1, core1 = call(
+        last_back_body,
+        [like(shape, BF16), like(shape, BF16), like(edge_shape, BF16), like(edge_shape, BF16)]
+        + [like(shape, BF16), like(shape, BF16)],
+        buffers + [pltpu.VMEM(shape[1:], F32), pltpu.VMEM(packed, F32)],
+        place, masked, gmp, near, far, *state,
+        micros=4.5,
+        scalars=1,
+    )
+    far_step = lons // 2
+
+    def exchanged(value, axis, step):
+        return lax.ppermute(value, axis, [(i, i ^ step) for i in range(lax.axis_size(axis))])
+
+    def across(value, to):
+        pairs = [(i * 2 + 1, (i ^ far_step) * 2 + to) for i in range(lons)]
+        return lax.ppermute(value, ("lon", "section"), pairs)
+
+    axes = ("lon", "lat", "section")
+    core0 = lax.ppermute(dxm1, "section", [(1, 0)])
+    left0 = lax.ppermute(
+        last3, axes, [(device(p) * 2 + 1, device(p + 1) * 2) for p in range(count)]
+    )
+    first3, normed_pair = call(
+        edge_body,
+        [like(edge_shape, BF16), like((2 * cells, chans), BF16)],
+        [],
+        first3, normed, exchanged(normed, "lon", far_step),
+        micros=0.5,
+    )
+    right0 = lax.ppermute(
+        first3, axes, [(device(p) * 2 + 1, device(p - 1) * 2) for p in range(count)]
+    )
+    (masked_pair,) = call(
+        select_join_body,
+        [like((2 * cells, chans), BF16)],
+        [],
+        place, core1, across(core1, 1), core0, across(dxm1, 0),
+        micros=0.5,
+        scalars=1,
+    )
+    dx0, dz0 = call(
+        first_back_body,
+        [like(shape, BF16), like(shape, BF16)],
+        buffers,
+        place, core0, left0, right0, *state,
+        micros=4.5,
+        scalars=1,
+    )
+    parts = [(normed_pair, masked_pair)]
+    if lons == 4:
+        parts.append((exchanged(normed_pair, "lon", 1), exchanged(masked_pair, "lon", 1)))
+    parts += [tuple(lax.ppermute(v, "lat", swap) for v in part) for part in parts]
+
+    (grad_k,) = call(
+        pair_kernel_grad_body,
+        [like((49, chans), F32)],
+        [pltpu.VMEM(shape, BF16)],
+        place, wide, dz1, dz0, parts[1][1],
+        micros=3.0,
+        specs=[smem] + [vmem] * 3 + [anywhere],
+    )
+    grad_k = summed(grad_k) * factor
+    sums = ()
+    for index, part in enumerate(parts):
+        scale = factor if index == len(parts) - 1 else 1.0
+        sums = weight_grads(
+            [part[0]], [part[1]], scale, weight_in, bias_in, weight_out, sums
+        )
+    grad_in, grad_out = sums
+
+    result = jnp.where(section == 1, dx1, dx0)
+    kept = lax.dynamic_slice_in_dim(result, lat * rows, rows, 1)
+    given = lax.dynamic_slice_in_dim(result, (1 - lat) * rows, rows, 1)
+    got = lax.ppermute(given, "lat", swap)
+    low = jnp.where(side == 0, kept, got)
+    high = jnp.where(side == 0, got, kept)
+    result = jnp.concatenate([low, high], axis=2)
+    return result[None], grad_in[None], grad_out[None], grad_k[None]
+
+
+def shards(saved_inputs, out_cotangent, *rest):
+    lats, lons = lax.axis_size("lat"), lax.axis_size("lon")
+    paired = lats == 2 and lons in (2, 4) and lats * lons <= GATHER_TILES
+    rows, cols = out_cotangent.shape[1:3]
+    paired = paired and rows % 8 == 0 and cols == 16
+    body = pair_shards if paired else tile_shards
+    return body(saved_inputs, out_cotangent, *rest)
 
 
 def solution(mesh):

time: 85.9 us -> 76.9 us (0.90)
  starting transfers between devices: 31.3 us -> 22.4 us
  Pallas kernels: 25.3 us -> 29.5 us
  other arithmetic: 3.04 us -> 0.8 us
  waiting for transfers between devices: 21.6 us -> 19.8 us
    ppermute x18 -> x17, starting transfers between devices: 28 us -> 19.9 us  [the longest x1 5.12 us: pair_shards(): near = lax.ppermute(near, ('lon', 'lat'), near_pairs)]
    pallas_call x7 -> x12, Pallas kernels: 25.3 us -> 29.5 us  [call(): pl.pallas_call(body, out_shape=outs, in_specs=specs, out_specs=[pl.BlockS...]
    ppermute x18 -> x17, waiting for transfers between devices: 18.8 us -> 15.3 us  [the longest x2 4.03 us: across(): return lax.ppermute(value, ('lon', 'section'), pairs)]
    ppermute x3, waiting for transfers between devices: 2.79 us -> 4.53 us  [summed(): lax.ppermute(value, axis, [(i, i ^ step) for i in range(count)])]
    slice x8 -> x0, local copies, waits for them, and re-layouts: 1.04 us -> none  [halo(): firsts = jnp.concatenate([v[:, :, :HALO] for v in (low, own, high)], axis=1)]
    select_n x8 -> x2, other arithmetic: 1.07 us -> 0.03 us  [the longest x1 0.02 us: pair_shards(): result = jnp.where(section == 1, dx1, dx0)]
    convert_element_type x2 -> x0, other arithmetic: 0.99 us -> none  [the longest x1 0.99 us: shards(): masked1 = (out_cotangent.astype(F32) * maskf[None, :, :, None]).astype(BF16)]
    unnamed x25 -> x29, local copies, waits for them, and re-layouts: 2.33 us -> 3.09 us
  transfers between devices with their start and end apart: 21 -> 20, of which waited for: 13 -> 8; matrix products, arithmetic and copies ran while one was open for 5% -> 2% of each run, Pallas kernels for 12% -> 31%
where the time goes in v2:
time: 76.9 us; the launch traced here: 76.6 us
  Pallas kernels  29.5 us (38%)
  starting transfers between devices  22.4 us (29%)
  waiting for transfers between devices  19.8 us (26%)
  local copies, waits for them, and re-layouts  3.1 us (4%)
  between operations  0.94 us (1%)
  other arithmetic  0.8 us (1%)
    pallas_call x12, Pallas kernels, call(): pl.pallas_call(body, out_shape=outs, in_specs=specs, out_specs=[pl.BlockS...  29.5 us
    ppermute x1, starting transfers between devices, pair_shards(): near = lax.ppermute(near, ('lon', 'lat'), near_pairs)  5.12 us
    ppermute x3, waiting for transfers between devices, summed(): lax.ppermute(value, axis, [(i, i ^ step) for i in range(count)])  4.53 us
    ppermute x4, starting transfers between devices, pair_shards(): lax.ppermute(v, 'lat', swap)  4.37 us
    ppermute x2, waiting for transfers between devices, across(): return lax.ppermute(value, ('lon', 'section'), pairs)  4.03 us
    ppermute x1, waiting for transfers between devices, pair_shards(): lax.ppermute(last3, axes, [(device(p) * 2 + 1, device(p + 1) * 2) for p i...  3.95 us
    ppermute x1, waiting for transfers between devices, pair_shards(): far = lax.ppermute(far, ('lon', 'lat'), far_pairs)  3.84 us
    unnamed x29, local copies, waits for them, and re-layouts  3.09 us
  transfers between devices with their start and end apart: 20, of which 8 were waited for; matrix products, arithmetic and copies ran while one was open for 2% of the time, Pallas kernels for 31%

profile of v2, /device:TPU:0, one launch (start us, length us, event | category | flops | bytes accessed | tf_op | source)
XLA Modules:
  0.0 76.6 jit_solution(15625285237823226008)
XLA Ops:
  0.7 0.1 pad_add_fusion.place
  0.7 1.0 %copy-done.2 = bf16[2,8,16,256]{3,2,1,0:T(8,128)(2,1)S(1)} copy-done((bf16[2,8,16,256]{3,2,1,0:T(8,128)(2,1)S(1)}, bf16[2,8,16,256]{3,2,1,0:T(8,128)(2,1)}, u32[]{:S(2)}) %copy-start.2) | copy-done | bytes 131096
  1.7 0.7 copy-done.4
  2.4 1.6 %shard_map.120 = (bf16[2,8,16,256]{3,2,1,0:T(8,128)(2,1)S(1)}, bf16[3,8,16,256]{3,2,1,0:T(8,128)(2,1)S(1)}, bf16[144,256]{1,0:T(8,128)(2,1)S(1)}, bf16[144,256]{1,0:T(8,128)(2,1)S(1)}) custom-call(s32[3]{0:T(128)S(1)} %pad_add_fusion.place, bf16[2,8,16,256]{3,2,1,0:T(8,128)(2,1)} %bitcast.3.x_far, bf16[2,8,16,256]{3,2,1,0:T(8,128)(2,1)S(1)} %copy-done.2, ...), custom_call_target="tpu_custom_call" | custom-call | flops 1100000000 | bytes 3600000 | tf_op jit(solution)/shard_map/pallas_call | solution.py:24
  4.0 5.1 %collective-permute-start = (bf16[144,256]{1,0:T(8,128)(2,1)S(1)}, bf16[144,256]{1,0:T(8,128)(2,1)S(1)}, u32[]{:S(2)}, u32[]{:S(2)}) collective-permute-start(bf16[144,256]{1,0:T(8,128)(2,1)S(1)} %get-tuple-element.38), channel_id=1, source_target_pairs={{0,12},{2,6},{6,2},{4,8},{8,4},{10,14},{14,10},{12,0},{1,13},{3,7}... | collective-permute-start | bytes 221192 | tf_op jit(solution)/shard_map/ppermute | solution.py:608
  9.2 1.0 %collective-permute-start.2 = (bf16[144,256]{1,0:T(8,128)(2,1)S(1)}, bf16[144,256]{1,0:T(8,128)(2,1)S(1)}, u32[]{:S(2)}, u32[]{:S(2)}) collective-permute-start(bf16[144,256]{1,0:T(8,128)(2,1)S(1)} %get-tuple-element.41), channel_id=1, source_target_pairs={{0,6},{2,12},{6,8},{4,2},{8,14},{10,4},{14,0},{12,10},{1,7},{3,13}... | collective-permute-start | bytes 221192 | tf_op jit(solution)/shard_map/ppermute | solution.py:609
  10.2 1.4 %collective-permute-done.near.refs_2_ = bf16[144,256]{1,0:T(8,128)(2,1)S(1)} collective-permute-done((bf16[144,256]{1,0:T(8,128)(2,1)S(1)}, bf16[144,256]{1,0:T(8,128)(2,1)S(1)}, u32[]{:S(2)}, u32[]{:S(2)}) %collective-permute-start) | collective-permute-done | bytes 73760 | tf_op jit(solution)/shard_map/ppermute | solution.py:608
  11.6 0.2 shard_map.121
  11.8 0.7 collective-permute-start.1
  12.5 3.8 %collective-permute-done.2.far.refs_3_ = bf16[144,256]{1,0:T(8,128)(2,1)S(1)} collective-permute-done((bf16[144,256]{1,0:T(8,128)(2,1)S(1)}, bf16[144,256]{1,0:T(8,128)(2,1)S(1)}, u32[]{:S(2)}, u32[]{:S(2)}) %collective-permute-start.2) | collective-permute-done | bytes 73760 | tf_op jit(solution)/shard_map/ppermute | solution.py:609
  16.3 6.7 %shard_map.122 = (f32[2,22,24,256]{3,2,1,0:T(8,128)S(1)}, bf16[256,256]{1,0:T(8,128)(2,1)S(1)}, f32[512,256]{1,0:T(8,128)S(1)}, f32[512,1]{1,0:T(8,128)S(1)}, f32[512,1024]{1,0:T(8,128)S(1)}) custom-call(s32[3]{0:T(128)S(1)} %pad_add_fusion.place, bf16[2,8,16,256]{3,2,1,0:T(8,128)(2,1)S(1)} %get-tuple-element.42.x, ...), custom_call_target="tpu_custom_call" | custom-call | flops 7150000128 | bytes 23400000 | tf_op jit(solution)/shard_map/pallas_call | solution.py:24
  23.1 0.0 copy-start.10
  23.1 0.0 copy-start.12
  23.1 0.3 collective-permute-start.6
  23.3 0.5 shard_map.123
  23.9 0.5 copy-done.8
  24.4 0.1 copy-done.10
  24.5 0.1 copy-done.12
  24.6 0.7 collective-permute-start.11
  25.3 1.3 %collective-permute-start.12 = (bf16[2,16,8,256]{3,2,1,0:T(8,128)(2,1)S(1)}, bf16[2,16,8,256]{3,2,1,0:T(8,128)(2,1)S(1)}, u32[]{:S(2)}, u32[]{:S(2)}) collective-permute-start(bf16[2,16,8,256]{3,2,1,0:T(8,128)(2,1)S(1)} %get-tuple-element.53), channel_id=1, source_target_pairs={{1,8},{5,12},{9,0},{13,4},{3,10},{7,14},{11,2},{15,6},{17,24},{21,... | collective-permute-start | bytes 393224 | tf_op jit(solution)/shard_map/ppermute | solution.py:655
  26.6 1.3 %collective-permute-start.4 = (bf16[2,16,8,256]{3,2,1,0:T(8,128)(2,1)S(1)}, bf16[2,16,8,256]{3,2,1,0:T(8,128)(2,1)S(1)}, u32[]{:S(2)}, u32[]{:S(2)}) collective-permute-start(bf16[2,16,8,256]{3,2,1,0:T(8,128)(2,1)S(1)} %get-tuple-element.53), channel_id=1, source_target_pairs={{1,0},{3,2},{5,4},{7,6},{9,8},{11,10},{13,12},{15,14},{17,16},{19,... | collective-permute-start | bytes 393224 | tf_op jit(solution)/shard_map/ppermute | solution.py:658
  27.9 2.1 %collective-permute-done.6.got = bf16[256,256]{1,0:T(8,128)(2,1)S(1)} collective-permute-done((bf16[256,256]{1,0:T(8,128)(2,1)S(1)}, bf16[256,256]{1,0:T(8,128)(2,1)S(1)}, u32[]{:S(2)}, u32[]{:S(2)}) %collective-permute-start.6) | collective-permute-done | bytes 131104 | tf_op jit(solution)/shard_map/ppermute | solution.py:651
  30.0 0.1 collective-permute-start.9
  30.1 1.1 %collective-permute-start.15 = (bf16[512,256]{1,0:T(8,128)(2,1)S(1)}, bf16[512,256]{1,0:T(8,128)(2,1)S(1)}, u32[]{:S(2)}, u32[]{:S(2)}) collective-permute-start(bf16[512,256]{1,0:T(8,128)(2,1)S(1)} %get-tuple-element.59.refs_0_), channel_id=1, source_target_pairs={{0,2},{2,0},{1,3},{3,1},{4,6},{6,4},{5,7},{7,5},{8,10},{10,8},{9,1... | collective-permute-start | bytes 786440 | tf_op jit(solution)/shard_map/ppermute | solution.py:691
  31.3 1.3 %collective-permute-start.7 = (bf16[2,16,3,256]{3,2,1,0:T(4,128)(2,1)S(1)}, bf16[2,16,3,256]{3,2,1,0:T(4,128)(2,1)S(1)}, u32[]{:S(2)}, u32[]{:S(2)}) collective-permute-start(bf16[2,16,3,256]{3,2,1,0:T(4,128)(2,1)S(1)} %get-tuple-element.57), channel_id=1, source_target_pairs={{1,12},{3,0},{7,2},{5,6},{9,4},{11,8},{15,10},{13,14},{17,28},{19,... | collective-permute-start | bytes 147464 | tf_op jit(solution)/shard_map/ppermute | solution.py:669
  32.5 4.0 %collective-permute-done.12.got0 = bf16[2,16,8,256]{3,2,1,0:T(8,128)(2,1)S(1)} collective-permute-done((bf16[2,16,8,256]{3,2,1,0:T(8,128)(2,1)S(1)}, bf16[2,16,8,256]{3,2,1,0:T(8,128)(2,1)S(1)}, u32[]{:S(2)}, u32[]{:S(2)}) %collective-permute-start.12) | collective-permute-done | bytes 131104 | tf_op jit(solution)/shard_map/ppermute | solution.py:655
  36.6 1.3 %collective-permute-start.5 = (bf16[2,16,3,256]{3,2,1,0:T(4,128)(2,1)S(1)}, bf16[2,16,3,256]{3,2,1,0:T(4,128)(2,1)S(1)}, u32[]{:S(2)}, u32[]{:S(2)}) collective-permute-start(bf16[2,16,3,256]{3,2,1,0:T(4,128)(2,1)S(1)} %get-tuple-element.54), channel_id=1, source_target_pairs={{1,2},{3,6},{7,4},{5,8},{9,10},{11,14},{15,12},{13,0},{17,18},{19,... | collective-permute-start | bytes 147464 | tf_op jit(solution)/shard_map/ppermute | solution.py:659
  37.9 0.6 shard_map.126.refs_1_
  38.4 1.6 %collective-permute-start.13 = (bf16[512,256]{1,0:T(8,128)(2,1)S(1)}, bf16[512,256]{1,0:T(8,128)(2,1)S(1)}, u32[]{:S(2)}, u32[]{:S(2)}) collective-permute-start(bf16[512,256]{1,0:T(8,128)(2,1)S(1)} %shard_map.126.refs_1_), channel_id=1, source_target_pairs={{0,4},{4,0},{8,12},{12,8},{1,5},{5,1},{9,13},{13,9},{2,6},{6,2},{1... | collective-permute-start | bytes 786440 | tf_op jit(solution)/shard_map/ppermute | solution.py:651
  40.1 4.0 %collective-permute-done.5.refs_1_ = bf16[2,16,3,256]{3,2,1,0:T(4,128)(2,1)S(1)} collective-permute-done((bf16[2,16,3,256]{3,2,1,0:T(4,128)(2,1)S(1)}, bf16[2,16,3,256]{3,2,1,0:T(4,128)(2,1)S(1)}, u32[]{:S(2)}, u32[]{:S(2)}) %collective-permute-start.5) | collective-permute-done | bytes 49184 | tf_op jit(solution)/shard_map/ppermute | solution.py:659
  44.1 4.4 %shard_map.125 = (bf16[2,16,8,256]{3,2,1,0:T(8,128)(2,1)S(1)}, bf16[2,16,8,256]{3,2,1,0:T(8,128)(2,1)S(1)}) custom-call(s32[3]{0:T(128)S(1)} %pad_add_fusion.place, bf16[2,16,8,256]{3,2,1,0:T(8,128)(2,1)S(1)} %collective-permute-done.4.refs_0_.core0, bf16[2,16,3,256]{3,2,1,0:T(4,128)(2,1)S(1)} %collective-permute-done.5.refs_1_, ...), custom_call_target="tpu_custom_call" | custom-call | flops 4950000128 | bytes 16200000 | tf_op jit(solution)/shard_map/pallas_call | solution.py:24
  48.5 1.0 %collective-permute-start.8 = (bf16[2,8,8,256]{3,2,1,0:T(8,128)(2,1)S(1)}, bf16[2,8,8,256]{3,2,1,0:T(8,128)(2,1)S(1)}, u32[]{:S(2)}, u32[]{:S(2)}) collective-permute-start(bf16[2,8,8,256]{3,2,1,0:T(8,128)(2,1)S(1)} %constant_dynamic-slice_fusion), channel_id=1, source_target_pairs={{0,2},{2,0},{1,3},{3,1},{4,6},{6,4},{5,7},{7,5},{8,10},{10,8},{9,1... | collective-permute-start | bytes 196616 | tf_op jit(solution)/shard_map/ppermute | solution.py:713
  49.5 2.7 %shard_map.127 = (f32[256,1024]{1,0:T(8,128)S(1)}, f32[1024,256]{1,0:T(8,128)S(1)}) custom-call(bf16[512,256]{1,0:T(8,128)(2,1)S(1)} %get-tuple-element.59.refs_0_, bf16[512,256]{1,0:T(8,128)(2,1)S(1)} %shard_map.126.refs_1_, bf16[256,1024]{1,0:T(8,128)(2,1)S(1)} %get-tuple-element.46.w_in.refs_8_.refs_7_.refs_2_, ...), custom_call_target="tpu_custom_call" | custom-call | flops 2816000000 | bytes 9216000 | tf_op jit(solution)/shard_map/pallas_call | solution.py:24
  52.2 1.2 %collective-permute-start.16 = (bf16[512,256]{1,0:T(8,128)(2,1)S(1)}, bf16[512,256]{1,0:T(8,128)(2,1)S(1)}, u32[]{:S(2)}, u32[]{:S(2)}) collective-permute-start(bf16[512,256]{1,0:T(8,128)(2,1)S(1)} %shard_map.126.refs_1_), channel_id=1, source_target_pairs={{0,2},{2,0},{1,3},{3,1},{4,6},{6,4},{5,7},{7,5},{8,10},{10,8},{9,1... | collective-permute-start | bytes 786440 | tf_op jit(solution)/shard_map/ppermute | solution.py:691
  53.4 3.1 %shard_map.131 = f32[49,256]{1,0:T(8,128)S(1)} custom-call(s32[3]{0:T(128)S(1)} %pad_add_fusion.place, f32[2,22,24,256]{3,2,1,0:T(8,128)S(1)} %get-tuple-element.69.wide, bf16[2,16,8,256]{3,2,1,0:T(8,128)(2,1)S(1)} %get-tuple-element.70.dz1, bf16[2,16,8,256]{3,2,1,0:T(8,128)(2,1)S(1)} %get-tuple-element.71.dz0, ...), custom_call_target="tpu_custom_call" | custom-call | flops 3300000000 | bytes 10800000 | tf_op jit(solution)/shard_map/pallas_call | solution.py:24
  56.6 1.0 %collective-permute-start.17 = (f32[49,256]{1,0:T(8,128)S(1)}, f32[49,256]{1,0:T(8,128)S(1)}, u32[]{:S(2)}, u32[]{:S(2)}) collective-permute-start(f32[49,256]{1,0:T(8,128)S(1)} %shard_map.131), channel_id=1, source_target_pairs={{0,2},{2,0},{1,3},{3,1},{4,6},{6,4},{5,7},{7,5},{8,10},{10,8},{9,1... | collective-permute-start | bytes 150536 | tf_op jit(solution)/shard_map/ppermute | solution.py:240
  57.5 0.7 maximum_bitcast_fusion
  58.2 1.1 %collective-permute-start.10 = (bf16[512,256]{1,0:T(8,128)(2,1)S(1)}, bf16[512,256]{1,0:T(8,128)(2,1)S(1)}, u32[]{:S(2)}, u32[]{:S(2)}) collective-permute-start(bf16[512,256]{1,0:T(8,128)(2,1)S(1)} %collective-permute-done.9.refs_0_), channel_id=1, source_target_pairs={{0,2},{2,0},{1,3},{3,1},{4,6},{6,4},{5,7},{7,5},{8,10},{10,8},{9,1... | collective-permute-start | bytes 786440 | tf_op jit(solution)/shard_map/ppermute | solution.py:691
  59.3 0.9 %collective-permute-start.14 = (bf16[512,256]{1,0:T(8,128)(2,1)S(1)}, bf16[512,256]{1,0:T(8,128)(2,1)S(1)}, u32[]{:S(2)}, u32[]{:S(2)}) collective-permute-start(bf16[512,256]{1,0:T(8,128)(2,1)S(1)} %collective-permute-done.13.refs_1_.after), channel_id=1, source_target_pairs={{0,2},{2,0},{1,3},{3,1},{4,6},{6,4},{5,7},{7,5},{8,10},{10,8},{9,1... | collective-permute-start | bytes 786440 | tf_op jit(solution)/shard_map/ppermute | solution.py:691
  60.2 1.6 %collective-permute-done.17 = f32[49,256]{1,0:T(8,128)S(1)} collective-permute-done((f32[49,256]{1,0:T(8,128)S(1)}, f32[49,256]{1,0:T(8,128)S(1)}, u32[]{:S(2)}, u32[]{:S(2)}) %collective-permute-start.17) | collective-permute-done | bytes 50208 | tf_op jit(solution)/shard_map/ppermute | solution.py:240
  61.8 0.7 collective-permute-start.18
  62.5 2.7 %shard_map.128 = (f32[256,1024]{1,0:T(8,128)S(1)}, f32[1024,256]{1,0:T(8,128)S(1)}) custom-call(bf16[512,256]{1,0:T(8,128)(2,1)S(1)} %collective-permute-done.9.refs_0_, bf16[512,256]{1,0:T(8,128)(2,1)S(1)} %collective-permute-done.13.refs_1_.after, bf16[256,1024]{1,0:T(8,128)(2,1)S(1)} %get-tuple-element.46.w_in.refs_8_.refs_7_.refs_2_, ...), custom_call_target="tpu_custom_call" | custom-call | flops 2816000000 | bytes 9216000 | tf_op jit(solution)/shard_map/pallas_call | solution.py:24
  65.3 0.8 %collective-permute-done.18 = f32[49,256]{1,0:T(8,128)S(1)} collective-permute-done((f32[49,256]{1,0:T(8,128)S(1)}, f32[49,256]{1,0:T(8,128)S(1)}, u32[]{:S(2)}, u32[]{:S(2)}) %collective-permute-start.18) | collective-permute-done | bytes 50208 | tf_op jit(solution)/shard_map/ppermute | solution.py:240
  66.1 0.8 %collective-permute-start.19 = (f32[49,256]{1,0:T(8,128)S(1)}, f32[49,256]{1,0:T(8,128)S(1)}, u32[]{:S(2)}, u32[]{:S(2)}) collective-permute-start(f32[49,256]{1,0:T(8,128)S(1)} %add.18), channel_id=1, source_target_pairs={{0,8},{4,12},{8,0},{12,4},{1,9},{5,13},{9,1},{13,5},{2,10},{6,14},... | collective-permute-start | bytes 150536 | tf_op jit(solution)/shard_map/ppermute | solution.py:240
  66.9 2.8 %shard_map.129 = (f32[256,1024]{1,0:T(8,128)S(1)}, f32[1024,256]{1,0:T(8,128)S(1)}) custom-call(bf16[512,256]{1,0:T(8,128)(2,1)S(1)} %collective-permute-done.15.refs_0_, bf16[512,256]{1,0:T(8,128)(2,1)S(1)} %collective-permute-done.16.refs_1_, bf16[256,1024]{1,0:T(8,128)(2,1)S(1)} %get-tuple-element.46.w_in.refs_8_.refs_7_.refs_2_, ...), custom_call_target="tpu_custom_call" | custom-call | flops 2816000000 | bytes 9216000 | tf_op jit(solution)/shard_map/pallas_call | solution.py:24
  69.7 2.1 %collective-permute-done.19 = f32[49,256]{1,0:T(8,128)S(1)} collective-permute-done((f32[49,256]{1,0:T(8,128)S(1)}, f32[49,256]{1,0:T(8,128)S(1)}, u32[]{:S(2)}, u32[]{:S(2)}) %collective-permute-start.19) | collective-permute-done | bytes 50208 | tf_op jit(solution)/shard_map/ppermute | solution.py:240
  71.9 0.7 copy.13
  72.6 4.0 %shard_map.130 = (f32[256,1024]{1,0:T(8,128)}, f32[1024,256]{1,0:T(8,128)}) custom-call(bf16[512,256]{1,0:T(8,128)(2,1)S(1)} %collective-permute-done.10.refs_0_, bf16[512,256]{1,0:T(8,128)(2,1)S(1)} %collective-permute-done.14.refs_1_, bf16[256,1024]{1,0:T(8,128)(2,1)S(1)} %get-tuple-element.46.w_in.refs_8_.refs_7_.refs_2_, ...), custom_call_target="tpu_custom_call" | custom-call | flops 2816000000 | bytes 9216000 | tf_op jit(solution)/shard_map/pallas_call | solution.py:24
  (41 shorter events, 0.2 us)
Async XLA Ops:
  0.6 10.9 %copy-start = (bf16[1,256,1024]{2,1,0:T(8,128)(2,1)S(1)}, bf16[1,256,1024]{2,1,0:T(8,128)(2,1)}, u32[]{:S(2)}) copy-start(bf16[1,256,1024]{2,1,0:T(8,128)(2,1)} %param.15) | copy-start | bytes 1572868
  0.6 10.9 %copy-start.1 = (bf16[1,1024,256]{2,1,0:T(8,128)(2,1)S(1)}, bf16[1,1024,256]{2,1,0:T(8,128)(2,1)}, u32[]{:S(2)}) copy-start(bf16[1,1024,256]{2,1,0:T(8,128)(2,1)} %param.17) | copy-start | bytes 1572868
  0.7 1.0 %copy-start.2 = (bf16[2,8,16,256]{3,2,1,0:T(8,128)(2,1)S(1)}, bf16[2,8,16,256]{3,2,1,0:T(8,128)(2,1)}, u32[]{:S(2)}) copy-start(bf16[2,8,16,256]{3,2,1,0:T(8,128)(2,1)} %g_far.1) | copy-start | bytes 393220
  1.7 0.7 copy-start.4
  2.4 9.2 %copy-start.3 = (bf16[1,7,7,256]{3,2,1,0:T(8,128)(2,1)S(1)}, bf16[1,7,7,256]{3,2,1,0:T(8,128)(2,1)}, u32[]{:S(2)}) copy-start(bf16[1,7,7,256]{3,2,1,0:T(8,128)(2,1)} %taps.1) | copy-start | bytes 75268
  2.4 9.2 %copy-start.5 = (f32[1,1024]{1,0:T(1,128)S(1)}, f32[1,1024]{1,0:T(1,128)}, u32[]{:S(2)}) copy-start(f32[1,1024]{1,0:T(1,128)} %refs_3_.1) | copy-start | bytes 12292
  2.4 9.2 %copy-start.6 = (f32[1,256]{1,0:T(1,128)S(1)}, f32[1,256]{1,0:T(1,128)}, u32[]{:S(2)}) copy-start(f32[1,256]{1,0:T(1,128)} %refs_0_.1) | copy-start | bytes 3076
  2.4 9.2 %copy-start.7 = (f32[1,256]{1,0:T(1,128)S(1)}, f32[1,256]{1,0:T(1,128)}, u32[]{:S(2)}) copy-start(f32[1,256]{1,0:T(1,128)} %refs_1_.1) | copy-start | bytes 3076
  4.0 7.5 %collective-permute-start = (bf16[144,256]{1,0:T(8,128)(2,1)S(1)}, bf16[144,256]{1,0:T(8,128)(2,1)S(1)}, u32[]{:S(2)}, u32[]{:S(2)}) collective-permute-start(bf16[144,256]{1,0:T(8,128)(2,1)S(1)} %get-tuple-element.38), channel_id=1, source_target_pairs={{0,12},{2,6},{6,2},{4,8},{8,4},{10,14},{14,10},{12,0},{1,13},{3,7}... | collective-permute-start | bytes 221192 | tf_op jit(solution)/shard_map/ppermute | solution.py:608
  9.2 7.2 %collective-permute-start.3 = (bf16[2,8,16,256]{3,2,1,0:T(8,128)(2,1)}, bf16[2,8,16,256]{3,2,1,0:T(8,128)(2,1)S(1)}, u32[]{:S(2)}, u32[]{:S(2)}) collective-permute-start(bf16[2,8,16,256]{3,2,1,0:T(8,128)(2,1)} %bitcast.3.x_far), channel_id=1, source_target_pairs={{0,2},{2,0},{1,3},{3,1},{4,6},{6,4},{5,7},{7,5},{8,10},{10,8},{9,1... | collective-permute-start | bytes 393224 | tf_op jit(solution)/shard_map/ppermute | solution.py:590
  9.2 7.2 %collective-permute-start.2 = (bf16[144,256]{1,0:T(8,128)(2,1)S(1)}, bf16[144,256]{1,0:T(8,128)(2,1)S(1)}, u32[]{:S(2)}, u32[]{:S(2)}) collective-permute-start(bf16[144,256]{1,0:T(8,128)(2,1)S(1)} %get-tuple-element.41), channel_id=1, source_target_pairs={{0,6},{2,12},{6,8},{4,2},{8,14},{10,4},{14,0},{12,10},{1,7},{3,13}... | collective-permute-start | bytes 221192 | tf_op jit(solution)/shard_map/ppermute | solution.py:609
  11.8 11.6 %collective-permute-start.1 = (bf16[3,8,16,256]{3,2,1,0:T(8,128)(2,1)S(1)}, bf16[3,8,16,256]{3,2,1,0:T(8,128)(2,1)S(1)}, u32[]{:S(2)}, u32[]{:S(2)}) collective-permute-start(bf16[3,8,16,256]{3,2,1,0:T(8,128)(2,1)S(1)} %get-tuple-element.40.refs_0_), channel_id=1, source_target_pairs={{1,3},{3,1},{5,7},{7,5},{9,11},{11,9},{13,15},{15,13},{17,19},{19,... | collective-permute-start | bytes 589832 | tf_op jit(solution)/shard_map/ppermute | solution.py:618
  23.0 1.4 %copy-start.8 = (f32[512,1024]{1,0:T(8,128)}, f32[512,1024]{1,0:T(8,128)S(1)}, u32[]{:S(2)}) copy-start(f32[512,1024]{1,0:T(8,128)S(1)} %get-tuple-element.50.refs_6_.refs_5_) | copy-start | bytes 6291460
  23.1 1.5 %copy-start.10 = (f32[512,256]{1,0:T(8,128)}, f32[512,256]{1,0:T(8,128)S(1)}, u32[]{:S(2)}) copy-start(f32[512,256]{1,0:T(8,128)S(1)} %get-tuple-element.48.refs_4_.refs_3_) | copy-start | bytes 1572868
  23.1 1.5 %copy-start.12 = (f32[512,1]{1,0:T(8,128)}, f32[512,1]{1,0:T(8,128)S(1)}, u32[]{:S(2)}) copy-start(f32[512,1]{1,0:T(8,128)S(1)} %get-tuple-element.49.refs_5_.refs_4_) | copy-start | bytes 6148
  23.1 6.9 %collective-permute-start.6 = (bf16[256,256]{1,0:T(8,128)(2,1)S(1)}, bf16[256,256]{1,0:T(8,128)(2,1)S(1)}, u32[]{:S(2)}, u32[]{:S(2)}) collective-permute-start(bf16[256,256]{1,0:T(8,128)(2,1)S(1)} %get-tuple-element.56.normed), channel_id=1, source_target_pairs={{0,8},{4,12},{8,0},{12,4},{1,9},{5,13},{9,1},{13,5},{2,10},{6,14},... | collective-permute-start | bytes 393224 | tf_op jit(solution)/shard_map/ppermute | solution.py:651
  24.6 6.6 %collective-permute-start.11 = (bf16[2,16,8,256]{3,2,1,0:T(8,128)(2,1)S(1)}, bf16[2,16,8,256]{3,2,1,0:T(8,128)(2,1)S(1)}, u32[]{:S(2)}, u32[]{:S(2)}) collective-permute-start(bf16[2,16,8,256]{3,2,1,0:T(8,128)(2,1)S(1)} %get-tuple-element.60.core1), channel_id=1, source_target_pairs={{1,9},{5,13},{9,1},{13,5},{3,11},{7,15},{11,3},{15,7},{17,25},{21,... | collective-permute-start | bytes 393224 | tf_op jit(solution)/shard_map/ppermute | solution.py:655
  25.3 11.3 %collective-permute-start.12 = (bf16[2,16,8,256]{3,2,1,0:T(8,128)(2,1)S(1)}, bf16[2,16,8,256]{3,2,1,0:T(8,128)(2,1)S(1)}, u32[]{:S(2)}, u32[]{:S(2)}) collective-permute-start(bf16[2,16,8,256]{3,2,1,0:T(8,128)(2,1)S(1)} %get-tuple-element.53), channel_id=1, source_target_pairs={{1,8},{5,12},{9,0},{13,4},{3,10},{7,14},{11,2},{15,6},{17,24},{21,... | collective-permute-start | bytes 393224 | tf_op jit(solution)/shard_map/ppermute | solution.py:655
  26.6 11.3 %collective-permute-start.4 = (bf16[2,16,8,256]{3,2,1,0:T(8,128)(2,1)S(1)}, bf16[2,16,8,256]{3,2,1,0:T(8,128)(2,1)S(1)}, u32[]{:S(2)}, u32[]{:S(2)}) collective-permute-start(bf16[2,16,8,256]{3,2,1,0:T(8,128)(2,1)S(1)} %get-tuple-element.53), channel_id=1, source_target_pairs={{1,0},{3,2},{5,4},{7,6},{9,8},{11,10},{13,12},{15,14},{17,16},{19,... | collective-permute-start | bytes 393224 | tf_op jit(solution)/shard_map/ppermute | solution.py:658
  27.9 16.2 %copy-start.9 = (f32[512,1024]{1,0:T(8,128)S(1)}, f32[512,1024]{1,0:T(8,128)}, u32[]{:S(2)}) copy-start(f32[512,1024]{1,0:T(8,128)} %copy-done.8) | copy-start | bytes 6291460
  27.9 16.2 %copy-start.11 = (f32[512,256]{1,0:T(8,128)S(1)}, f32[512,256]{1,0:T(8,128)}, u32[]{:S(2)}) copy-start(f32[512,256]{1,0:T(8,128)} %copy-done.10) | copy-start | bytes 1572868
  27.9 16.1 %copy-start.13 = (f32[512,1]{1,0:T(8,128)S(1)}, f32[512,1]{1,0:T(8,128)}, u32[]{:S(2)}) copy-start(f32[512,1]{1,0:T(8,128)} %copy-done.12) | copy-start | bytes 6148
  30.0 28.2 %collective-permute-start.9 = (bf16[512,256]{1,0:T(8,128)(2,1)S(1)}, bf16[512,256]{1,0:T(8,128)(2,1)S(1)}, u32[]{:S(2)}, u32[]{:S(2)}) collective-permute-start(bf16[512,256]{1,0:T(8,128)(2,1)S(1)} %get-tuple-element.59.refs_0_), channel_id=1, source_target_pairs={{0,4},{4,0},{8,12},{12,8},{1,5},{5,1},{9,13},{13,9},{2,6},{6,2},{1... | collective-permute-start | bytes 786440 | tf_op jit(solution)/shard_map/ppermute | solution.py:651
  30.1 36.8 %collective-permute-start.15 = (bf16[512,256]{1,0:T(8,128)(2,1)S(1)}, bf16[512,256]{1,0:T(8,128)(2,1)S(1)}, u32[]{:S(2)}, u32[]{:S(2)}) collective-permute-start(bf16[512,256]{1,0:T(8,128)(2,1)S(1)} %get-tuple-element.59.refs_0_), channel_id=1, source_target_pairs={{0,2},{2,0},{1,3},{3,1},{4,6},{6,4},{5,7},{7,5},{8,10},{10,8},{9,1... | collective-permute-start | bytes 786440 | tf_op jit(solution)/shard_map/ppermute | solution.py:691
  31.3 8.8 %collective-permute-start.7 = (bf16[2,16,3,256]{3,2,1,0:T(4,128)(2,1)S(1)}, bf16[2,16,3,256]{3,2,1,0:T(4,128)(2,1)S(1)}, u32[]{:S(2)}, u32[]{:S(2)}) collective-permute-start(bf16[2,16,3,256]{3,2,1,0:T(4,128)(2,1)S(1)} %get-tuple-element.57), channel_id=1, source_target_pairs={{1,12},{3,0},{7,2},{5,6},{9,4},{11,8},{15,10},{13,14},{17,28},{19,... | collective-permute-start | bytes 147464 | tf_op jit(solution)/shard_map/ppermute | solution.py:669
  36.6 7.5 %collective-permute-start.5 = (bf16[2,16,3,256]{3,2,1,0:T(4,128)(2,1)S(1)}, bf16[2,16,3,256]{3,2,1,0:T(4,128)(2,1)S(1)}, u32[]{:S(2)}, u32[]{:S(2)}) collective-permute-start(bf16[2,16,3,256]{3,2,1,0:T(4,128)(2,1)S(1)} %get-tuple-element.54), channel_id=1, source_target_pairs={{1,2},{3,6},{7,4},{5,8},{9,10},{11,14},{15,12},{13,0},{17,18},{19,... | collective-permute-start | bytes 147464 | tf_op jit(solution)/shard_map/ppermute | solution.py:659
  38.4 15.0 %collective-permute-start.13 = (bf16[512,256]{1,0:T(8,128)(2,1)S(1)}, bf16[512,256]{1,0:T(8,128)(2,1)S(1)}, u32[]{:S(2)}, u32[]{:S(2)}) collective-permute-start(bf16[512,256]{1,0:T(8,128)(2,1)S(1)} %shard_map.126.refs_1_), channel_id=1, source_target_pairs={{0,4},{4,0},{8,12},{12,8},{1,5},{5,1},{9,13},{13,9},{2,6},{6,2},{1... | collective-permute-start | bytes 786440 | tf_op jit(solution)/shard_map/ppermute | solution.py:651
  48.5 4.9 %collective-permute-start.8 = (bf16[2,8,8,256]{3,2,1,0:T(8,128)(2,1)S(1)}, bf16[2,8,8,256]{3,2,1,0:T(8,128)(2,1)S(1)}, u32[]{:S(2)}, u32[]{:S(2)}) collective-permute-start(bf16[2,8,8,256]{3,2,1,0:T(8,128)(2,1)S(1)} %constant_dynamic-slice_fusion), channel_id=1, source_target_pairs={{0,2},{2,0},{1,3},{3,1},{4,6},{6,4},{5,7},{7,5},{8,10},{10,8},{9,1... | collective-permute-start | bytes 196616 | tf_op jit(solution)/shard_map/ppermute | solution.py:713
  52.2 14.7 %collective-permute-start.16 = (bf16[512,256]{1,0:T(8,128)(2,1)S(1)}, bf16[512,256]{1,0:T(8,128)(2,1)S(1)}, u32[]{:S(2)}, u32[]{:S(2)}) collective-permute-start(bf16[512,256]{1,0:T(8,128)(2,1)S(1)} %shard_map.126.refs_1_), channel_id=1, source_target_pairs={{0,2},{2,0},{1,3},{3,1},{4,6},{6,4},{5,7},{7,5},{8,10},{10,8},{9,1... | collective-permute-start | bytes 786440 | tf_op jit(solution)/shard_map/ppermute | solution.py:691
  56.6 5.3 %collective-permute-start.17 = (f32[49,256]{1,0:T(8,128)S(1)}, f32[49,256]{1,0:T(8,128)S(1)}, u32[]{:S(2)}, u32[]{:S(2)}) collective-permute-start(f32[49,256]{1,0:T(8,128)S(1)} %shard_map.131), channel_id=1, source_target_pairs={{0,2},{2,0},{1,3},{3,1},{4,6},{6,4},{5,7},{7,5},{8,10},{10,8},{9,1... | collective-permute-start | bytes 150536 | tf_op jit(solution)/shard_map/ppermute | solution.py:240
  58.2 14.3 %collective-permute-start.10 = (bf16[512,256]{1,0:T(8,128)(2,1)S(1)}, bf16[512,256]{1,0:T(8,128)(2,1)S(1)}, u32[]{:S(2)}, u32[]{:S(2)}) collective-permute-start(bf16[512,256]{1,0:T(8,128)(2,1)S(1)} %collective-permute-done.9.refs_0_), channel_id=1, source_target_pairs={{0,2},{2,0},{1,3},{3,1},{4,6},{6,4},{5,7},{7,5},{8,10},{10,8},{9,1... | collective-permute-start | bytes 786440 | tf_op jit(solution)/shard_map/ppermute | solution.py:691
  59.3 13.2 %collective-permute-start.14 = (bf16[512,256]{1,0:T(8,128)(2,1)S(1)}, bf16[512,256]{1,0:T(8,128)(2,1)S(1)}, u32[]{:S(2)}, u32[]{:S(2)}) collective-permute-start(bf16[512,256]{1,0:T(8,128)(2,1)S(1)} %collective-permute-done.13.refs_1_.after), channel_id=1, source_target_pairs={{0,2},{2,0},{1,3},{3,1},{4,6},{6,4},{5,7},{7,5},{8,10},{10,8},{9,1... | collective-permute-start | bytes 786440 | tf_op jit(solution)/shard_map/ppermute | solution.py:691
  61.8 4.2 %collective-permute-start.18 = (f32[49,256]{1,0:T(8,128)S(1)}, f32[49,256]{1,0:T(8,128)S(1)}, u32[]{:S(2)}, u32[]{:S(2)}) collective-permute-start(f32[49,256]{1,0:T(8,128)S(1)} %add.17), channel_id=1, source_target_pairs={{0,4},{4,0},{8,12},{12,8},{1,5},{5,1},{9,13},{13,9},{2,6},{6,2},{1... | collective-permute-start | bytes 150536 | tf_op jit(solution)/shard_map/ppermute | solution.py:240
  66.1 5.8 %collective-permute-start.19 = (f32[49,256]{1,0:T(8,128)S(1)}, f32[49,256]{1,0:T(8,128)S(1)}, u32[]{:S(2)}, u32[]{:S(2)}) collective-permute-start(f32[49,256]{1,0:T(8,128)S(1)} %add.18), channel_id=1, source_target_pairs={{0,8},{4,12},{8,0},{12,4},{1,9},{5,13},{9,1},{13,5},{2,10},{6,14},... | collective-permute-start | bytes 150536 | tf_op jit(solution)/shard_map/ppermute | solution.py:240

commit v3 on v2

--- a/solution.py
+++ b/solution.py
@@ -47,34 +47,40 @@
 
 
 def gelu_both(h):
+    k, c, c3, half, one = (
+        jnp.asarray(v, h.dtype) for v in (gelu_k, gelu_k * gelu_c, 3.0 * gelu_k * gelu_c, 0.5, 1.0)
+    )
     h2 = h * h
-    tval = jnp.tanh(h * (gelu_k + (gelu_k * gelu_c) * h2))
-    half = 0.5 + 0.5 * tval
-    slope = half + (0.5 * h) * (1.0 - tval * tval) * (gelu_k + (3.0 * gelu_k * gelu_c) * h2)
-    return h * half, slope
+    tval = jnp.tanh(h * (k + c * h2))
+    rise = half + half * tval
+    return h * rise, rise + (half * h) * (one - tval * tval) * (k + c3 * h2)
+
+
+def lane_parts(chans):
+    return [slice(at, at + LANES) for at in range(0, chans, LANES)]
 
 
 def widen(dst, own, low, high, left, right):
     rows, cols = own.shape[1], own.shape[2]
-    dst[:, :HALO, SIDE : SIDE + cols, :] = low[...].astype(F32)
-    dst[:, HALO : HALO + rows, SIDE : SIDE + cols, :] = own[...].astype(F32)
-    dst[:, HALO + rows :, SIDE : SIDE + cols, :] = high[...].astype(F32)
-    dst[:, :, SIDE - HALO : SIDE, :] = left[...].astype(F32)
-    dst[:, :, SIDE + cols : SIDE + cols + HALO, :] = right[...].astype(F32)
+    for part, lanes in enumerate(lane_parts(own.shape[3])):
+        to = dst.at[part]
+        to[:, :HALO, SIDE : SIDE + cols, :] = low[:, :, :, lanes].astype(F32)
+        to[:, HALO : HALO + rows, SIDE : SIDE + cols, :] = own[:, :, :, lanes].astype(F32)
+        to[:, HALO + rows :, SIDE : SIDE + cols, :] = high[:, :, :, lanes].astype(F32)
+        to[:, :, SIDE - HALO : SIDE, :] = left[:, :, :, lanes].astype(F32)
+        to[:, :, SIDE + cols : SIDE + cols + HALO, :] = right[:, :, :, lanes].astype(F32)
 
 
 def depthwise(src, kern, rows, cols, begin, flip, emit):
-    micros, chans = src.shape[0], src.shape[3]
     chunk = 8 if cols > 8 else 16
     chunk = chunk if rows % chunk == 0 else rows
-    for part in range(chans // LANES):
-        lanes = slice(part * LANES, (part + 1) * LANES)
-        for micro in range(micros):
+    for part, lanes in enumerate(lane_parts(kern.shape[1])):
+        for micro in range(src.shape[1]):
             for first in range(0, rows, chunk):
                 total = jnp.zeros((chunk, cols, LANES), F32)
                 for kb in range(7):
                     at = slice(begin + kb, begin + kb + cols)
-                    slab = src[micro, first : first + chunk + 2 * HALO, at, lanes]
+                    slab = src[part, micro, first : first + chunk + 2 * HALO, at, :]
                     for ka in range(7):
                         tap = (6 - ka) * 7 + (6 - kb) if flip else ka * 7 + kb
                         total = total + slab[ka : ka + chunk] * kern[tap : tap + 1, lanes]
@@ -126,14 +132,13 @@
 
 def kernel_grad_body(first, wide, dz, grad):
     micros, rows, cols, chans = dz.shape
-    for part in range(chans // LANES):
-        lanes = slice(part * LANES, (part + 1) * LANES)
+    for part, lanes in enumerate(lane_parts(chans)):
         for kb in range(7):
             begin = first + kb
             sums = [None] * 7
             for micro in range(micros):
                 own = dz[micro, :, :, lanes].astype(F32)
-                slab = wide[micro, :, begin : begin + cols, lanes]
+                slab = wide[part, micro, :, begin : begin + cols, :]
                 for ka in range(7):
                     prod = jnp.sum(slab[ka : ka + rows] * own, axis=0)
                     sums[ka] = prod if sums[ka] is None else sums[ka] + prod
@@ -158,7 +163,7 @@
 def weight_grad_body(parts, carried, factor, *refs):
     normed, masked = refs[:parts], refs[parts : 2 * parts]
     w_in, b_in, w_out = refs[2 * parts : 2 * parts + 3]
-    grad_in, grad_out, sum_in, sum_out = refs[-4:]
+    grad_in, grad_out, token, sum_in, sum_out = refs[-5:]
     if carried:
         sum_in[...] = refs[2 * parts + 3][...]
         sum_out[...] = refs[2 * parts + 4][...]
@@ -167,7 +172,7 @@
         sum_out[...] = jnp.zeros_like(sum_out)
     for part in range(parts):
         cells = normed[part].shape[0]
-        step = min(cells, 256)
+        step = min(cells, 512)
 
         @pl.loop(0, cells // step)
         def _(index):
@@ -175,13 +180,14 @@
             n = normed[part][at, :]
             gm = masked[part][at, :]
             h = jnp.dot(n, w_in[...], preferred_element_type=F32) + b_in[...]
-            act, slope = gelu_both(h)
-            dhid = (nt_dot(gm, w_out[...]) * slope).astype(BF16)
+            act, slope = gelu_both(h.astype(BF16))
+            dhid = nt_dot(gm, w_out[...]).astype(BF16) * slope
             sum_in[...] += tn_dot(n, dhid)
-            sum_out[...] += tn_dot(act.astype(BF16), gm)
+            sum_out[...] += tn_dot(act, gm)
 
     grad_in[...] = sum_in[...] * factor
     grad_out[...] = sum_out[...] * factor
+    token[...] = jnp.zeros_like(token)
 
 
 def lat_edges(first, last):
@@ -242,14 +248,17 @@
     return value
 
 
-def weight_grads(normed, masked, factor, w_in, b_in, w_out, carried=()):
+def weight_grads(normed, masked, factor, w_in, b_in, w_out, carried=(), after=()):
     chans, hidden = w_in.shape
+    args = [*normed, *masked, w_in, b_in, w_out, *carried]
+    specs = [pl.BlockSpec(memory_space=pltpu.VMEM)] * len(args)
     return call(
         functools.partial(weight_grad_body, len(normed), bool(carried), factor),
-        [like((chans, hidden), F32), like((hidden, chans), F32)],
+        [like((chans, hidden), F32), like((hidden, chans), F32), like((8, LANES), F32)],
         [pltpu.VMEM((chans, hidden), F32), pltpu.VMEM((hidden, chans), F32)],
-        *normed, *masked, w_in, b_in, w_out, *carried,
-        micros=sum(v.shape[0] for v in normed) / 200.0,
+        *args, *after,
+        micros=0.6,
+        specs=specs + [pl.BlockSpec(memory_space=pl.ANY)] * len(after),
     )
 
 
@@ -260,7 +269,7 @@
     hidden = w_in.shape[2]
     cells = micros * rows * cols
     shape = (micros, rows, cols, chans)
-    wide_shape = (micros, rows + 2 * HALO, SIDE + cols + SIDE, chans)
+    wide_shape = (chans // LANES, micros, rows + 2 * HALO, SIDE + cols + SIDE, LANES)
     flat = (cells, chans)
     tiles = lax.axis_size("lat") * lax.axis_size("lon")
     factor = 1.0 / (cells * tiles) ** 0.5
@@ -327,7 +336,7 @@
     )
     grad_k0, dx0, _ = input_grad(dz0, masked0.reshape(shape))
     grad_k = summed(jnp.where(section == 1, grad_k1, grad_k0)) * factor
-    grad_in, grad_out = weight_grads(
+    grad_in, grad_out, _ = weight_grads(
         normed_all, masked_all, factor, weight_in, b_in, weight_out
     )
     if not gather:
@@ -400,23 +409,18 @@
         own_rows = pl.ds(HALO + at, rows)
         tile_x = tile[...].astype(F32)
         packed[...] = edge[...].astype(F32)
-
-        @pl.when(side == 0)
-        def _():
-            for row in range(micros * rows):
-                micro, to = row // rows, row % rows
-                wide[micro, at + HALO + to, : 2 * HALO, :] = packed[row * 9 : row * 9 + 6, :]
-            wide[:, own_rows, 2 * HALO : 2 * HALO + cols, :] = tile_x
-
-        @pl.when(side == 1)
-        def _():
-            skip = half - 2 * HALO
-            wide[:, own_rows, : cols - skip, :] = tile_x[:, :, skip:]
-            for row in range(micros * rows):
-                micro, to = row // rows, row % rows
-                wide[micro, at + HALO + to, cols - skip : cols - skip + 2 * HALO, :] = packed[
-                    row * 9 : row * 9 + 6, :
-                ]
+        skip = half - 2 * HALO
+        for number, keep, tile_at, edge_at in ((0, 0, 2 * HALO, 0), (1, skip, 0, cols - skip)):
+
+            @pl.when(side == number)
+            def _():
+                for part, lanes in enumerate(lane_parts(chans)):
+                    to_cols = slice(tile_at, tile_at + cols - keep)
+                    wide[part, :, own_rows, to_cols, :] = tile_x[:, :, keep:, lanes]
+                    for row in range(micros * rows):
+                        wide[
+                            part, row // rows, at + HALO + row % rows, edge_at : edge_at + 6, :
+                        ] = packed[row * 9 : row * 9 + 6, lanes]
 
     def emit(micro, first, chunk, lanes, total):
         at = (micro * all_rows + first) * reach
@@ -433,7 +437,7 @@
     core = n.reshape(micros * all_rows, reach, chans)[:, HALO : HALO + half]
     normed[...] = core.reshape(normed.shape).astype(BF16)
     h = jnp.dot(n.astype(BF16), w_in[...], preferred_element_type=F32) + b_in[...]
-    slope[...] = gelu_both(h)[1]
+    slope[...] = gelu_both(h)[1].astype(BF16)
 
 
 def pair_back(gwide, dwide, zhat, rscale, slope, gain, w_in, w_out, kern, dz, emit):
@@ -441,13 +445,14 @@
     half = reach - 8
     masked = gwide[...].reshape(micros * rows * reach, chans).astype(BF16)
     dzval = dense_back(
-        masked, slope[...], zhat[...], rscale[...], gain[...], w_in[...], w_out[...]
+        masked, slope[...].astype(F32), zhat[...], rscale[...], gain[...], w_in[...], w_out[...]
     )
     rounded = dzval.astype(BF16).astype(F32).reshape(micros, rows, reach, chans)
-    nothing = jnp.zeros((micros, HALO, reach, chans), F32)
-    dwide[:, :HALO] = nothing
-    dwide[:, HALO + rows :] = nothing
-    dwide[:, HALO : HALO + rows] = rounded
+    nothing = jnp.zeros((micros, HALO, reach, LANES), F32)
+    for part, lanes in enumerate(lane_parts(chans)):
+        dwide[part, :, :HALO] = nothing
+        dwide[part, :, HALO + rows :] = nothing
+        dwide[part, :, HALO : HALO + rows] = rounded[..., lanes]
     dz[...] = rounded[:, :, HALO : HALO + half].astype(BF16)
 
     def add(micro, first, chunk, lanes, total):
@@ -531,12 +536,11 @@
     target[half:] = second[...]
 
 
-def edge_body(first3, normed, got, sent, pair):
-    sent[...] = first3[...]
-    pair_up(pair, normed, got)
-
-
-def select_join_body(place, core1, got1, core0, got0, pair):
+def pair_body(first, second, left0, right0, pair):
+    pair_up(pair, first, second)
+
+
+def select_join_body(place, core1, got1, core0, got0, left0, right0, pair):
     half = pair.shape[0] // 2
     for number, core, got in ((1, core1, got1), (0, core0, got0)):
 
@@ -546,14 +550,21 @@
             pair[half:] = got[...].reshape(half, pair.shape[1])
 
 
+def add_body(scale, first, second, after, out):
+    total = (first[...] + second[...]) * scale
+    if len(out.shape) == 2:
+        out[...] = total
+    else:
+        for row in range(out.shape[0]):
+            out[row] = total[row : row + 1]
+
+
 def pair_kernel_grad_body(place, wide, dz1, dz0, after, grad, dz):
-    @pl.when(place[2] == 1)
-    def _():
-        dz[...] = dz1[...]
-
-    @pl.when(place[2] == 0)
-    def _():
-        dz[...] = dz0[...]
+    for number, own in ((1, dz1), (0, dz0)):
+
+        @pl.when(place[2] == number)
+        def _():
+            dz[...] = own[...]
 
     kernel_grad_body(HALO, wide, dz, grad)
 
@@ -569,7 +580,7 @@
     many = micros * all_rows * reach
     shape = (micros, all_rows, half, chans)
     edge_shape = (micros, all_rows, HALO, chans)
-    wide_shape = (micros, all_rows + 2 * HALO, reach + 8, chans)
+    wide_shape = (chans // LANES, micros, all_rows + 2 * HALO, reach + 8, LANES)
     reach_shape = (micros, all_rows, reach, chans)
     factor = 1.0 / (cells * 2 * lons) ** 0.5
     section, lat, lon = (lax.axis_index(a) for a in ("section", "lat", "lon"))
@@ -624,7 +635,7 @@
             like((cells, chans), BF16),
             like((many, chans), F32),
             like((many, 1), F32),
-            like((many, hidden), F32),
+            like((many, hidden), BF16),
         ],
         [pltpu.VMEM((many, chans), F32), pltpu.VMEM(packed, F32)],
         place, x_near, xp, near, far, kern, bias, gain, weight_in, bias_in,
@@ -634,7 +645,7 @@
     state = (zhat, rscale, slope, gain, weight_in, weight_out, kern)
     buffers = [
         pltpu.VMEM(reach_shape, F32),
-        pltpu.VMEM((micros, all_rows + 2 * HALO, reach, chans), F32),
+        pltpu.VMEM((chans // LANES, micros, all_rows + 2 * HALO, reach, LANES), F32),
     ]
     dx1, dxm1, first3, last3, dz1, core1 = call(
         last_back_body,
@@ -659,13 +670,6 @@
     left0 = lax.ppermute(
         last3, axes, [(device(p) * 2 + 1, device(p + 1) * 2) for p in range(count)]
     )
-    first3, normed_pair = call(
-        edge_body,
-        [like(edge_shape, BF16), like((2 * cells, chans), BF16)],
-        [],
-        first3, normed, exchanged(normed, "lon", far_step),
-        micros=0.5,
-    )
     right0 = lax.ppermute(
         first3, axes, [(device(p) * 2 + 1, device(p - 1) * 2) for p in range(count)]
     )
@@ -673,9 +677,17 @@
         select_join_body,
         [like((2 * cells, chans), BF16)],
         [],
-        place, core1, across(core1, 1), core0, across(dxm1, 0),
+        place, core1, across(core1, 1), core0, across(dxm1, 0), left0, right0,
         micros=0.5,
-        scalars=1,
+        specs=[smem] + [vmem] * 4 + [anywhere] * 2,
+    )
+    (normed_pair,) = call(
+        pair_body,
+        [like((2 * cells, chans), BF16)],
+        [],
+        normed, exchanged(normed, "lon", far_step), left0, right0,
+        micros=0.5,
+        specs=[vmem] * 2 + [anywhere] * 2,
     )
     dx0, dz0 = call(
         first_back_body,
@@ -685,27 +697,39 @@
         micros=4.5,
         scalars=1,
     )
-    parts = [(normed_pair, masked_pair)]
-    if lons == 4:
-        parts.append((exchanged(normed_pair, "lon", 1), exchanged(masked_pair, "lon", 1)))
-    parts += [tuple(lax.ppermute(v, "lat", swap) for v in part) for part in parts]
+    normed_near, masked_near = exchanged(normed_pair, "lon", 1), exchanged(masked_pair, "lon", 1)
+    normed_far, masked_far = (lax.ppermute(v, "lat", swap) for v in (normed_pair, masked_pair))
+    normed_last = exchanged(normed_far, "lon", 1)
+    masked_last = lax.ppermute(masked_near, "lat", swap)
 
     (grad_k,) = call(
         pair_kernel_grad_body,
         [like((49, chans), F32)],
         [pltpu.VMEM(shape, BF16)],
-        place, wide, dz1, dz0, parts[1][1],
+        place, wide, dz1, dz0, normed_near,
         micros=3.0,
         specs=[smem] + [vmem] * 3 + [anywhere],
     )
-    grad_k = summed(grad_k) * factor
-    sums = ()
-    for index, part in enumerate(parts):
-        scale = factor if index == len(parts) - 1 else 1.0
-        sums = weight_grads(
-            [part[0]], [part[1]], scale, weight_in, bias_in, weight_out, sums
-        )
-    grad_in, grad_out = sums
+    weights = (weight_in, bias_in, weight_out)
+
+    def added(grad, axis, step, scale, shape, after):
+        return call(
+            functools.partial(add_body, scale),
+            [like(shape, F32)],
+            [],
+            grad, exchanged(grad, axis, step), after,
+            micros=0.2,
+            specs=[vmem, vmem, anywhere],
+        )[0]
+
+    taps = grad_k.shape
+    *sums, done = weight_grads([normed_pair], [masked_pair], 1.0, *weights)
+    grad_k = added(grad_k, "lon", far_step, 1.0, taps, done)
+    *sums, done = weight_grads([normed_near], [masked_near], 1.0, *weights, sums)
+    grad_k = added(grad_k, "lon", 1, 1.0, taps, done)
+    *sums, done = weight_grads([normed_far], [masked_far], 1.0, *weights, sums)
+    grad_in, grad_out, done = weight_grads([normed_last], [masked_last], factor, *weights, sums)
+    grad_k = added(grad_k, "lat", 1, factor, (49, 1, chans), done)
 
     result = jnp.where(section == 1, dx1, dx0)
     kept = lax.dynamic_slice_in_dim(result, lat * rows, rows, 1)
@@ -714,12 +738,12 @@
     low = jnp.where(side == 0, kept, got)
     high = jnp.where(side == 0, got, kept)
     result = jnp.concatenate([low, high], axis=2)
-    return result[None], grad_in[None], grad_out[None], grad_k[None]
+    return result[None], grad_in[None], grad_out[None], jnp.transpose(grad_k, (1, 0, 2))
 
 
 def shards(saved_inputs, out_cotangent, *rest):
     lats, lons = lax.axis_size("lat"), lax.axis_size("lon")
-    paired = lats == 2 and lons in (2, 4) and lats * lons <= GATHER_TILES
+    paired = lats == 2 and lons == 4
     rows, cols = out_cotangent.shape[1:3]
     paired = paired and rows % 8 == 0 and cols == 16
     body = pair_shards if paired else tile_shards

time: 76.9 us -> 64.4 us (0.84)
  Pallas kernels: 29.5 us -> 22.7 us
  waiting for transfers between devices: 19.8 us -> 13.4 us
  starting transfers between devices: 22.4 us -> 23.7 us
    pallas_call x12 -> x15, Pallas kernels: 29.5 us -> 22.7 us  [call(): pl.pallas_call(body, out_shape=outs, in_specs=specs, out_specs=[pl.BlockS...]
    ppermute x3 -> x1, waiting for transfers between devices: 4.53 us -> 0.01 us  [pair_shards(): masked_last = lax.ppermute(masked_near, 'lat', swap)]
    ppermute x3 -> x7, starting transfers between devices: 1.98 us -> 6.11 us  [exchanged(): lax.ppermute(value, axis, [(i, i ^ step) for i in range(lax.axis_size(axi...]
    ppermute x2, waiting for transfers between devices: 4.03 us -> 0.01 us  [across(): return lax.ppermute(value, ('lon', 'section'), pairs)]
    ppermute x3 -> x7, waiting for transfers between devices: 2.08 us -> 5.55 us  [exchanged(): lax.ppermute(value, axis, [(i, i ^ step) for i in range(lax.axis_size(axi...]
    ppermute x4 -> x2, starting transfers between devices: 4.37 us -> 2.52 us  [pair_shards(): lax.ppermute(v, 'lat', swap)]
    ppermute x1, waiting for transfers between devices: 3.95 us -> 2.63 us  [pair_shards(): lax.ppermute(last3, axes, [(device(p) * 2 + 1, device(p + 1) * 2) for p i...]
    ppermute x3 -> x1, starting transfers between devices: 2.49 us -> 1.29 us  [pair_shards(): masked_last = lax.ppermute(masked_near, 'lat', swap)]
  transfers between devices with their start and end apart: 20 -> 20, of which waited for: 8 -> 7; matrix products, arithmetic and copies ran while one was open for 2% -> 1% of each run, Pallas kernels for 31% -> 32%
where the time goes in v3:
time: 64.4 us; the launch traced here: 64.1 us
  starting transfers between devices  23.7 us (37%)
  Pallas kernels  22.7 us (35%)
  waiting for transfers between devices  13.4 us (21%)
  local copies, waits for them, and re-layouts  2.6 us (4%)
  between operations  0.95 us (1%)
  other arithmetic  0.78 us (1%)
    pallas_call x15, Pallas kernels, call(): pl.pallas_call(body, out_shape=outs, in_specs=specs, out_specs=[pl.BlockS...  22.7 us
    ppermute x7, starting transfers between devices, exchanged(): lax.ppermute(value, axis, [(i, i ^ step) for i in range(lax.axis_size(axi...  6.11 us
    ppermute x7, waiting for transfers between devices, exchanged(): lax.ppermute(value, axis, [(i, i ^ step) for i in range(lax.axis_size(axi...  5.55 us
    ppermute x1, starting transfers between devices, pair_shards(): near = lax.ppermute(near, ('lon', 'lat'), near_pairs)  5.12 us
    ppermute x1, waiting for transfers between devices, pair_shards(): far = lax.ppermute(far, ('lon', 'lat'), far_pairs)  3.84 us
    ppermute x1, waiting for transfers between devices, pair_shards(): lax.ppermute(last3, axes, [(device(p) * 2 + 1, device(p + 1) * 2) for p i...  2.63 us
    unnamed x28, local copies, waits for them, and re-layouts  2.59 us
    ppermute x2, starting transfers between devices, pair_shards(): lax.ppermute(v, 'lat', swap)  2.52 us
  transfers between devices with their start and end apart: 20, of which 7 were waited for; matrix products, arithmetic and copies ran while one was open for 1% of the time, Pallas kernels for 32%

profile of v3, /device:TPU:0, one launch (start us, length us, event | category | flops | bytes accessed | tf_op | source)
XLA Modules:
  0.0 64.1 jit_solution(17446431583639121066)
XLA Ops:
  0.6 0.1 pad_add_fusion.place
  0.7 0.9 %copy-done.2 = bf16[2,8,16,256]{3,2,1,0:T(8,128)(2,1)S(1)} copy-done((bf16[2,8,16,256]{3,2,1,0:T(8,128)(2,1)S(1)}, bf16[2,8,16,256]{3,2,1,0:T(8,128)(2,1)}, u32[]{:S(2)}) %copy-start.2) | copy-done | bytes 131096
  1.6 0.7 %copy-done.4 = s32[8,16]{1,0:T(8,128)S(1)} copy-done((s32[8,16]{1,0:T(8,128)S(1)}, s32[8,16]{1,0:T(8,128)}, u32[]{:S(2)}) %copy-start.4) | copy-done | bytes 536
  2.3 0.0 copy-start.6
  2.3 0.0 copy-start.7
  2.3 1.6 %shard_map.120 = (bf16[2,8,16,256]{3,2,1,0:T(8,128)(2,1)S(1)}, bf16[3,8,16,256]{3,2,1,0:T(8,128)(2,1)S(1)}, bf16[144,256]{1,0:T(8,128)(2,1)S(1)}, bf16[144,256]{1,0:T(8,128)(2,1)S(1)}) custom-call(s32[3]{0:T(128)S(1)} %pad_add_fusion.place, bf16[2,8,16,256]{3,2,1,0:T(8,128)(2,1)} %bitcast.3.x_far, bf16[2,8,16,256]{3,2,1,0:T(8,128)(2,1)S(1)} %copy-done.2, ...), custom_call_target="tpu_custom_call" | custom-call | flops 1100000000 | bytes 3600000 | tf_op jit(solution)/shard_map/pallas_call | solution.py:24
  4.0 5.1 %collective-permute-start = (bf16[144,256]{1,0:T(8,128)(2,1)S(1)}, bf16[144,256]{1,0:T(8,128)(2,1)S(1)}, u32[]{:S(2)}, u32[]{:S(2)}) collective-permute-start(bf16[144,256]{1,0:T(8,128)(2,1)S(1)} %get-tuple-element.39), channel_id=1, source_target_pairs={{0,12},{2,6},{6,2},{4,8},{8,4},{10,14},{14,10},{12,0},{1,13},{3,7}... | collective-permute-start | bytes 221192 | tf_op jit(solution)/shard_map/ppermute | solution.py:619
  9.1 1.0 %collective-permute-start.2 = (bf16[144,256]{1,0:T(8,128)(2,1)S(1)}, bf16[144,256]{1,0:T(8,128)(2,1)S(1)}, u32[]{:S(2)}, u32[]{:S(2)}) collective-permute-start(bf16[144,256]{1,0:T(8,128)(2,1)S(1)} %get-tuple-element.42), channel_id=1, source_target_pairs={{0,6},{2,12},{6,8},{4,2},{8,14},{10,4},{14,0},{12,10},{1,7},{3,13}... | collective-permute-start | bytes 221192 | tf_op jit(solution)/shard_map/ppermute | solution.py:620
  10.1 1.4 %collective-permute-done.near.refs_2_ = bf16[144,256]{1,0:T(8,128)(2,1)S(1)} collective-permute-done((bf16[144,256]{1,0:T(8,128)(2,1)S(1)}, bf16[144,256]{1,0:T(8,128)(2,1)S(1)}, u32[]{:S(2)}, u32[]{:S(2)}) %collective-permute-start) | collective-permute-done | bytes 73760 | tf_op jit(solution)/shard_map/ppermute | solution.py:619
  11.5 0.2 shard_map.121
  11.7 0.7 %collective-permute-start.1 = (bf16[3,8,16,256]{3,2,1,0:T(8,128)(2,1)S(1)}, bf16[3,8,16,256]{3,2,1,0:T(8,128)(2,1)S(1)}, u32[]{:S(2)}, u32[]{:S(2)}) collective-permute-start(bf16[3,8,16,256]{3,2,1,0:T(8,128)(2,1)S(1)} %get-tuple-element.41.refs_0_), channel_id=1, source_target_pairs={{1,3},{3,1},{5,7},{7,5},{9,11},{11,9},{13,15},{15,13},{17,19},{19,... | collective-permute-start | bytes 589832 | tf_op jit(solution)/shard_map/ppermute | solution.py:629
  12.4 3.8 %collective-permute-done.2.far.refs_3_ = bf16[144,256]{1,0:T(8,128)(2,1)S(1)} collective-permute-done((bf16[144,256]{1,0:T(8,128)(2,1)S(1)}, bf16[144,256]{1,0:T(8,128)(2,1)S(1)}, u32[]{:S(2)}, u32[]{:S(2)}) %collective-permute-start.2) | collective-permute-done | bytes 73760 | tf_op jit(solution)/shard_map/ppermute | solution.py:620
  16.3 6.0 %shard_map.122 = (f32[2,2,22,24,128]{4,3,2,1,0:T(8,128)S(1)}, bf16[256,256]{1,0:T(8,128)(2,1)S(1)}, f32[512,256]{1,0:T(8,128)S(1)}, f32[512,1]{1,0:T(8,128)S(1)}, bf16[512,1024]{1,0:T(8,128)(2,1)S(1)}) custom-call(s32[3]{0:T(128)S(1)} %pad_add_fusion.place, bf16[2,8,16,256]{3,2,1,0:T(8,128)(2,1)S(1)} %get-tuple-element.43.x, ...), custom_call_target="tpu_custom_call" | custom-call | flops 7150000128 | bytes 23400000 | tf_op jit(solution)/shard_map/pallas_call | solution.py:24
  22.3 0.3 collective-permute-start.8
  22.6 0.5 shard_map.123
  23.2 0.1 copy-done.8
  23.3 0.2 copy-done.10
  23.4 0.7 %copy-done.12 = bf16[2,16,8,256]{3,2,1,0:T(8,128)(2,1)} copy-done((bf16[2,16,8,256]{3,2,1,0:T(8,128)(2,1)}, bf16[2,16,8,256]{3,2,1,0:T(8,128)(2,1)S(1)}, u32[]{:S(2)}) %copy-start.12) | copy-done | bytes 131096
  24.1 1.3 %collective-permute-start.4 = (bf16[2,16,8,256]{3,2,1,0:T(8,128)(2,1)S(1)}, bf16[2,16,8,256]{3,2,1,0:T(8,128)(2,1)S(1)}, u32[]{:S(2)}, u32[]{:S(2)}) collective-permute-start(bf16[2,16,8,256]{3,2,1,0:T(8,128)(2,1)S(1)} %get-tuple-element.54), channel_id=1, source_target_pairs={{1,0},{3,2},{5,4},{7,6},{9,8},{11,10},{13,12},{15,14},{17,16},{19,... | collective-permute-start | bytes 393224 | tf_op jit(solution)/shard_map/ppermute | solution.py:669
  25.4 1.3 %collective-permute-start.5 = (bf16[2,16,3,256]{3,2,1,0:T(4,128)(2,1)S(1)}, bf16[2,16,3,256]{3,2,1,0:T(4,128)(2,1)S(1)}, u32[]{:S(2)}, u32[]{:S(2)}) collective-permute-start(bf16[2,16,3,256]{3,2,1,0:T(4,128)(2,1)S(1)} %get-tuple-element.55), channel_id=1, source_target_pairs={{1,2},{3,6},{7,4},{5,8},{9,10},{11,14},{15,12},{13,0},{17,18},{19,... | collective-permute-start | bytes 147464 | tf_op jit(solution)/shard_map/ppermute | solution.py:670
  26.7 1.3 %collective-permute-start.6 = (bf16[2,16,3,256]{3,2,1,0:T(4,128)(2,1)S(1)}, bf16[2,16,3,256]{3,2,1,0:T(4,128)(2,1)S(1)}, u32[]{:S(2)}, u32[]{:S(2)}) collective-permute-start(bf16[2,16,3,256]{3,2,1,0:T(4,128)(2,1)S(1)} %get-tuple-element.56), channel_id=1, source_target_pairs={{1,12},{3,0},{7,2},{5,6},{9,4},{11,8},{15,10},{13,14},{17,28},{19,... | collective-permute-start | bytes 147464 | tf_op jit(solution)/shard_map/ppermute | solution.py:673
  28.0 0.0 copy-start.9
  28.0 0.0 copy-start.11
  28.0 1.4 %collective-permute-start.12 = (bf16[2,16,8,256]{3,2,1,0:T(8,128)(2,1)S(1)}, bf16[2,16,8,256]{3,2,1,0:T(8,128)(2,1)S(1)}, u32[]{:S(2)}, u32[]{:S(2)}) collective-permute-start(bf16[2,16,8,256]{3,2,1,0:T(8,128)(2,1)S(1)} %get-tuple-element.54), channel_id=1, source_target_pairs={{1,8},{5,12},{9,0},{13,4},{3,10},{7,14},{11,2},{15,6},{17,24},{21,... | collective-permute-start | bytes 393224 | tf_op jit(solution)/shard_map/ppermute | solution.py:666
  29.5 0.7 %collective-permute-start.11 = (bf16[2,16,8,256]{3,2,1,0:T(8,128)(2,1)S(1)}, bf16[2,16,8,256]{3,2,1,0:T(8,128)(2,1)S(1)}, u32[]{:S(2)}, u32[]{:S(2)}) collective-permute-start(bf16[2,16,8,256]{3,2,1,0:T(8,128)(2,1)S(1)} %get-tuple-element.59.core1), channel_id=1, source_target_pairs={{1,9},{5,13},{9,1},{13,5},{3,11},{7,15},{11,3},{15,7},{17,25},{21,... | collective-permute-start | bytes 393224 | tf_op jit(solution)/shard_map/ppermute | solution.py:666
  30.1 2.6 %collective-permute-done.5.refs_1_.left0 = bf16[2,16,3,256]{3,2,1,0:T(4,128)(2,1)S(1)} collective-permute-done((bf16[2,16,3,256]{3,2,1,0:T(4,128)(2,1)S(1)}, bf16[2,16,3,256]{3,2,1,0:T(4,128)(2,1)S(1)}, u32[]{:S(2)}, u32[]{:S(2)}) %collective-permute-start.5) | collective-permute-done | bytes 49184 | tf_op jit(solution)/shard_map/ppermute | solution.py:670
  32.8 1.5 %collective-permute-start.16 = (bf16[512,256]{1,0:T(8,128)(2,1)S(1)}, bf16[512,256]{1,0:T(8,128)(2,1)S(1)}, u32[]{:S(2)}, u32[]{:S(2)}) collective-permute-start(bf16[512,256]{1,0:T(8,128)(2,1)S(1)} %shard_map.125.refs_0_), channel_id=1, source_target_pairs={{0,4},{4,0},{8,12},{12,8},{1,5},{5,1},{9,13},{13,9},{2,6},{6,2},{1... | collective-permute-start | bytes 786440 | tf_op jit(solution)/shard_map/ppermute | solution.py:662
  34.3 1.1 %collective-permute-start.9 = (bf16[512,256]{1,0:T(8,128)(2,1)S(1)}, bf16[512,256]{1,0:T(8,128)(2,1)S(1)}, u32[]{:S(2)}, u32[]{:S(2)}) collective-permute-start(bf16[512,256]{1,0:T(8,128)(2,1)S(1)} %shard_map.125.refs_0_), channel_id=1, source_target_pairs={{0,2},{2,0},{1,3},{3,1},{4,6},{6,4},{5,7},{7,5},{8,10},{10,8},{9,1... | collective-permute-start | bytes 786440 | tf_op jit(solution)/shard_map/ppermute | solution.py:701
  35.4 3.0 %shard_map.124 = (bf16[2,16,8,256]{3,2,1,0:T(8,128)(2,1)S(1)}, bf16[2,16,8,256]{3,2,1,0:T(8,128)(2,1)S(1)}) custom-call(s32[3]{0:T(128)S(1)} %pad_add_fusion.place, bf16[2,16,8,256]{3,2,1,0:T(8,128)(2,1)S(1)} %collective-permute-done.4.refs_0_.core0, bf16[2,16,3,256]{3,2,1,0:T(4,128)(2,1)S(1)} %collective-permute-done.5.refs_1_.left0, ...), custom_call_target="tpu_custom_call" | custom-call | flops 4950000128 | bytes 16200000 | tf_op jit(solution)/shard_map/pallas_call | solution.py:24
  38.4 1.0 %collective-permute-start.7 = (bf16[2,8,8,256]{3,2,1,0:T(8,128)(2,1)S(1)}, bf16[2,8,8,256]{3,2,1,0:T(8,128)(2,1)S(1)}, u32[]{:S(2)}, u32[]{:S(2)}) collective-permute-start(bf16[2,8,8,256]{3,2,1,0:T(8,128)(2,1)S(1)} %constant_dynamic-slice_fusion), channel_id=1, source_target_pairs={{0,2},{2,0},{1,3},{3,1},{4,6},{6,4},{5,7},{7,5},{8,10},{10,8},{9,1... | collective-permute-start | bytes 196616 | tf_op jit(solution)/shard_map/ppermute | solution.py:737
  39.4 0.8 %shard_map.126.refs_1_ = bf16[512,256]{1,0:T(8,128)(2,1)S(1)} custom-call(s32[3]{0:T(128)S(1)} %pad_add_fusion.place, bf16[2,16,8,256]{3,2,1,0:T(8,128)(2,1)S(1)} %get-tuple-element.59.core1, bf16[2,16,8,256]{3,2,1,0:T(8,128)(2,1)S(1)} %collective-permute-done.11.got1, bf16[2,16,8,256]{3,2,1,0:T(8,128)(2,1)S(1)} %collective-permute-done.4.refs_0_.core0, ...), custom_call_target="tpu_custom_call" | custom-call | flops 550000000 | bytes 1800000 | tf_op jit(solution)/shard_map/pallas_call | solution.py:24
  40.2 0.7 %collective-permute-start.13 = (bf16[512,256]{1,0:T(8,128)(2,1)S(1)}, bf16[512,256]{1,0:T(8,128)(2,1)S(1)}, u32[]{:S(2)}, u32[]{:S(2)}) collective-permute-start(bf16[512,256]{1,0:T(8,128)(2,1)S(1)} %shard_map.126.refs_1_), channel_id=1, source_target_pairs={{0,4},{4,0},{8,12},{12,8},{1,5},{5,1},{9,13},{13,9},{2,6},{6,2},{1... | collective-permute-start | bytes 786440 | tf_op jit(solution)/shard_map/ppermute | solution.py:662
  40.9 1.4 %collective-permute-start.15 = (bf16[512,256]{1,0:T(8,128)(2,1)S(1)}, bf16[512,256]{1,0:T(8,128)(2,1)S(1)}, u32[]{:S(2)}, u32[]{:S(2)}) collective-permute-start(bf16[512,256]{1,0:T(8,128)(2,1)S(1)} %shard_map.126.refs_1_), channel_id=1, source_target_pairs={{0,2},{2,0},{1,3},{3,1},{4,6},{6,4},{5,7},{7,5},{8,10},{10,8},{9,1... | collective-permute-start | bytes 786440 | tf_op jit(solution)/shard_map/ppermute | solution.py:701
  42.3 1.7 %shard_map.127 = (f32[256,1024]{1,0:T(8,128)S(1)}, f32[1024,256]{1,0:T(8,128)S(1)}, f32[8,128]{1,0:T(8,128)S(1)}) custom-call(bf16[512,256]{1,0:T(8,128)(2,1)S(1)} %shard_map.125.refs_0_, bf16[512,256]{1,0:T(8,128)(2,1)S(1)} %shard_map.126.refs_1_, bf16[256,1024]{1,0:T(8,128)(2,1)S(1)} %get-tuple-element.47.w_in.refs_8_.refs_7_.refs_2_, ...), custom_call_target="tpu_custom_call" | custom-call | flops 660000000 | bytes 2160000 | tf_op jit(solution)/shard_map/pallas_call | solution.py:24
  44.0 1.6 %shard_map.131.first = f32[49,256]{1,0:T(8,128)S(1)} custom-call(s32[3]{0:T(128)S(1)} %pad_add_fusion.place, f32[2,2,22,24,128]{4,3,2,1,0:T(8,128)S(1)} %get-tuple-element.68.wide, bf16[2,16,8,256]{3,2,1,0:T(8,128)(2,1)S(1)} %copy-done.13, bf16[2,16,8,256]{3,2,1,0:T(8,128)(2,1)S(1)} %get-tuple-element.70.dz0, ...), custom_call_target="tpu_custom_call" | custom-call | flops 3300000000 | bytes 10800000 | tf_op jit(solution)/shard_map/pallas_call | solution.py:24
  45.6 3.1 %collective-permute-start.17 = (f32[49,256]{1,0:T(8,128)S(1)}, f32[49,256]{1,0:T(8,128)S(1)}, u32[]{:S(2)}, u32[]{:S(2)}) collective-permute-start(f32[49,256]{1,0:T(8,128)S(1)} %shard_map.131.first), channel_id=1, source_target_pairs={{0,8},{4,12},{8,0},{12,4},{1,9},{5,13},{9,1},{13,5},{2,10},{6,14},... | collective-permute-start | bytes 150536 | tf_op jit(solution)/shard_map/ppermute | solution.py:662
  48.8 0.4 collective-permute-done.13.refs_1_
  49.2 1.3 %collective-permute-start.14 = (bf16[512,256]{1,0:T(8,128)(2,1)S(1)}, bf16[512,256]{1,0:T(8,128)(2,1)S(1)}, u32[]{:S(2)}, u32[]{:S(2)}) collective-permute-start(bf16[512,256]{1,0:T(8,128)(2,1)S(1)} %collective-permute-done.13.refs_1_), channel_id=1, source_target_pairs={{0,2},{2,0},{1,3},{3,1},{4,6},{6,4},{5,7},{7,5},{8,10},{10,8},{9,1... | collective-permute-start | bytes 786440 | tf_op jit(solution)/shard_map/ppermute | solution.py:703
  50.5 0.7 %maximum_bitcast_fusion = bf16[1,2,8,16,256]{4,3,2,1,0:T(8,128)(2,1)} fusion(bf16[2,8,8,256]{3,2,1,0:T(8,128)(2,1)S(1)} %get-tuple-element.75, bf16[2,8,8,256]{3,2,1,0:T(8,128)(2,1)S(1)} %get-tuple-element.74), kind=kLoop, calls=%fused_computation | loop fusion | flops 262144 | bytes 262144 | tf_op jit(solution)/shard_map/broadcast_in_dim | solution.py:741
  51.2 1.6 %collective-permute-done.17.second = f32[49,256]{1,0:T(8,128)S(1)} collective-permute-done((f32[49,256]{1,0:T(8,128)S(1)}, f32[49,256]{1,0:T(8,128)S(1)}, u32[]{:S(2)}, u32[]{:S(2)}) %collective-permute-start.17) | collective-permute-done | bytes 50208 | tf_op jit(solution)/shard_map/ppermute | solution.py:662
  52.7 0.1 collective-permute-start.18
  52.8 1.7 %shard_map.128 = (f32[256,1024]{1,0:T(8,128)S(1)}, f32[1024,256]{1,0:T(8,128)S(1)}, f32[8,128]{1,0:T(8,128)S(1)}) custom-call(bf16[512,256]{1,0:T(8,128)(2,1)S(1)} %collective-permute-done.16.refs_0_.after, bf16[512,256]{1,0:T(8,128)(2,1)S(1)} %collective-permute-done.13.refs_1_, bf16[256,1024]{1,0:T(8,128)(2,1)S(1)} %get-tuple-element.47.w_in.refs_8_.refs_7_.refs_2_, ...), custom_call_target="tpu_custom_call" | custom-call | flops 660000000 | bytes 2160000 | tf_op jit(solution)/shard_map/pallas_call | solution.py:24
  54.5 2.2 %shard_map.129 = (f32[256,1024]{1,0:T(8,128)S(1)}, f32[1024,256]{1,0:T(8,128)S(1)}, f32[8,128]{1,0:T(8,128)}) custom-call(bf16[512,256]{1,0:T(8,128)(2,1)S(1)} %collective-permute-done.9.refs_0_, bf16[512,256]{1,0:T(8,128)(2,1)S(1)} %collective-permute-done.15.refs_1_, bf16[256,1024]{1,0:T(8,128)(2,1)S(1)} %get-tuple-element.47.w_in.refs_8_.refs_7_.refs_2_, ...), custom_call_target="tpu_custom_call" | custom-call | flops 660000000 | bytes 2160000 | tf_op jit(solution)/shard_map/pallas_call | solution.py:24
  56.7 2.5 %collective-permute-done.18.second = f32[49,256]{1,0:T(8,128)S(1)} collective-permute-done((f32[49,256]{1,0:T(8,128)S(1)}, f32[49,256]{1,0:T(8,128)S(1)}, u32[]{:S(2)}, u32[]{:S(2)}) %collective-permute-start.18) | collective-permute-done | bytes 50208 | tf_op jit(solution)/shard_map/ppermute | solution.py:662
  59.2 0.5 collective-permute-start.19
  59.7 2.7 %shard_map.130 = (f32[256,1024]{1,0:T(8,128)}, f32[1024,256]{1,0:T(8,128)}, f32[8,128]{1,0:T(8,128)S(1)}) custom-call(bf16[512,256]{1,0:T(8,128)(2,1)S(1)} %collective-permute-done.10.refs_0_, bf16[512,256]{1,0:T(8,128)(2,1)S(1)} %collective-permute-done.14.refs_1_, bf16[256,1024]{1,0:T(8,128)(2,1)S(1)} %get-tuple-element.47.w_in.refs_8_.refs_7_.refs_2_, ...), custom_call_target="tpu_custom_call" | custom-call | flops 660000000 | bytes 2160000 | tf_op jit(solution)/shard_map/pallas_call | solution.py:24
  62.4 1.0 %collective-permute-done.19.second = f32[49,256]{1,0:T(8,128)S(1)} collective-permute-done((f32[49,256]{1,0:T(8,128)S(1)}, f32[49,256]{1,0:T(8,128)S(1)}, u32[]{:S(2)}, u32[]{:S(2)}) %collective-permute-start.19) | collective-permute-done | bytes 50208 | tf_op jit(solution)/shard_map/ppermute | solution.py:662
  63.5 0.6 %shard_map.134 = f32[49,1,256]{2,1,0:T(1,128)} custom-call(f32[49,256]{1,0:T(8,128)S(1)} %shard_map.133.first, f32[49,256]{1,0:T(8,128)S(1)} %collective-permute-done.19.second, f32[8,128]{1,0:T(8,128)S(1)} %get-tuple-element.73.after), custom_call_target="tpu_custom_call" | custom-call | flops 220000000 | bytes 720000 | tf_op jit(solution)/shard_map/pallas_call | solution.py:24
  (40 shorter events, 0.2 us)
Async XLA Ops:
  0.7 0.9 %copy-start.2 = (bf16[2,8,16,256]{3,2,1,0:T(8,128)(2,1)S(1)}, bf16[2,8,16,256]{3,2,1,0:T(8,128)(2,1)}, u32[]{:S(2)}) copy-start(bf16[2,8,16,256]{3,2,1,0:T(8,128)(2,1)} %g_far.1) | copy-start | bytes 393220
  1.6 0.7 %copy-start.4 = (s32[8,16]{1,0:T(8,128)S(1)}, s32[8,16]{1,0:T(8,128)}, u32[]{:S(2)}) copy-start(s32[8,16]{1,0:T(8,128)} %mask_far.1) | copy-start | bytes 1540
  2.3 9.2 %copy-start = (bf16[1,256,1024]{2,1,0:T(8,128)(2,1)S(1)}, bf16[1,256,1024]{2,1,0:T(8,128)(2,1)}, u32[]{:S(2)}) copy-start(bf16[1,256,1024]{2,1,0:T(8,128)(2,1)} %param.15) | copy-start | bytes 1572868
  2.3 9.2 %copy-start.1 = (bf16[1,1024,256]{2,1,0:T(8,128)(2,1)S(1)}, bf16[1,1024,256]{2,1,0:T(8,128)(2,1)}, u32[]{:S(2)}) copy-start(bf16[1,1024,256]{2,1,0:T(8,128)(2,1)} %param.17) | copy-start | bytes 1572868
  2.3 9.2 %copy-start.3 = (bf16[1,7,7,256]{3,2,1,0:T(8,128)(2,1)S(1)}, bf16[1,7,7,256]{3,2,1,0:T(8,128)(2,1)}, u32[]{:S(2)}) copy-start(bf16[1,7,7,256]{3,2,1,0:T(8,128)(2,1)} %taps.1) | copy-start | bytes 75268
  2.3 9.2 %copy-start.5 = (f32[1,1024]{1,0:T(1,128)S(1)}, f32[1,1024]{1,0:T(1,128)}, u32[]{:S(2)}) copy-start(f32[1,1024]{1,0:T(1,128)} %refs_3_.1) | copy-start | bytes 12292
  2.3 9.2 %copy-start.6 = (f32[1,256]{1,0:T(1,128)S(1)}, f32[1,256]{1,0:T(1,128)}, u32[]{:S(2)}) copy-start(f32[1,256]{1,0:T(1,128)} %refs_0_.1) | copy-start | bytes 3076
  2.3 9.2 %copy-start.7 = (f32[1,256]{1,0:T(1,128)S(1)}, f32[1,256]{1,0:T(1,128)}, u32[]{:S(2)}) copy-start(f32[1,256]{1,0:T(1,128)} %refs_1_.1) | copy-start | bytes 3076
  4.0 7.5 %collective-permute-start = (bf16[144,256]{1,0:T(8,128)(2,1)S(1)}, bf16[144,256]{1,0:T(8,128)(2,1)S(1)}, u32[]{:S(2)}, u32[]{:S(2)}) collective-permute-start(bf16[144,256]{1,0:T(8,128)(2,1)S(1)} %get-tuple-element.39), channel_id=1, source_target_pairs={{0,12},{2,6},{6,2},{4,8},{8,4},{10,14},{14,10},{12,0},{1,13},{3,7}... | collective-permute-start | bytes 221192 | tf_op jit(solution)/shard_map/ppermute | solution.py:619
  9.1 7.2 %collective-permute-start.3 = (bf16[2,8,16,256]{3,2,1,0:T(8,128)(2,1)}, bf16[2,8,16,256]{3,2,1,0:T(8,128)(2,1)S(1)}, u32[]{:S(2)}, u32[]{:S(2)}) collective-permute-start(bf16[2,8,16,256]{3,2,1,0:T(8,128)(2,1)} %bitcast.3.x_far), channel_id=1, source_target_pairs={{0,2},{2,0},{1,3},{3,1},{4,6},{6,4},{5,7},{7,5},{8,10},{10,8},{9,1... | collective-permute-start | bytes 393224 | tf_op jit(solution)/shard_map/ppermute | solution.py:601
  9.1 7.2 %collective-permute-start.2 = (bf16[144,256]{1,0:T(8,128)(2,1)S(1)}, bf16[144,256]{1,0:T(8,128)(2,1)S(1)}, u32[]{:S(2)}, u32[]{:S(2)}) collective-permute-start(bf16[144,256]{1,0:T(8,128)(2,1)S(1)} %get-tuple-element.42), channel_id=1, source_target_pairs={{0,6},{2,12},{6,8},{4,2},{8,14},{10,4},{14,0},{12,10},{1,7},{3,13}... | collective-permute-start | bytes 221192 | tf_op jit(solution)/shard_map/ppermute | solution.py:620
  11.7 10.9 %collective-permute-start.1 = (bf16[3,8,16,256]{3,2,1,0:T(8,128)(2,1)S(1)}, bf16[3,8,16,256]{3,2,1,0:T(8,128)(2,1)S(1)}, u32[]{:S(2)}, u32[]{:S(2)}) collective-permute-start(bf16[3,8,16,256]{3,2,1,0:T(8,128)(2,1)S(1)} %get-tuple-element.41.refs_0_), channel_id=1, source_target_pairs={{1,3},{3,1},{5,7},{7,5},{9,11},{11,9},{13,15},{15,13},{17,19},{19,... | collective-permute-start | bytes 589832 | tf_op jit(solution)/shard_map/ppermute | solution.py:629
  22.3 1.0 %copy-start.8 = (bf16[512,1024]{1,0:T(8,128)(2,1)}, bf16[512,1024]{1,0:T(8,128)(2,1)S(1)}, u32[]{:S(2)}) copy-start(bf16[512,1024]{1,0:T(8,128)(2,1)S(1)} %get-tuple-element.51.refs_6_.refs_5_) | copy-start | bytes 3145732
  22.3 1.1 %copy-start.10 = (f32[512,256]{1,0:T(8,128)}, f32[512,256]{1,0:T(8,128)S(1)}, u32[]{:S(2)}) copy-start(f32[512,256]{1,0:T(8,128)S(1)} %get-tuple-element.49.refs_4_.refs_3_) | copy-start | bytes 1572868
  22.3 7.1 %collective-permute-start.8 = (bf16[256,256]{1,0:T(8,128)(2,1)S(1)}, bf16[256,256]{1,0:T(8,128)(2,1)S(1)}, u32[]{:S(2)}, u32[]{:S(2)}) collective-permute-start(bf16[256,256]{1,0:T(8,128)(2,1)S(1)} %get-tuple-element.58.first), channel_id=1, source_target_pairs={{0,8},{4,12},{8,0},{12,4},{1,9},{5,13},{9,1},{13,5},{2,10},{6,14},... | collective-permute-start | bytes 393224 | tf_op jit(solution)/shard_map/ppermute | solution.py:662
  23.4 0.7 %copy-start.12 = (bf16[2,16,8,256]{3,2,1,0:T(8,128)(2,1)}, bf16[2,16,8,256]{3,2,1,0:T(8,128)(2,1)S(1)}, u32[]{:S(2)}) copy-start(bf16[2,16,8,256]{3,2,1,0:T(8,128)(2,1)S(1)} %get-tuple-element.69.dz1) | copy-start | bytes 393220
  24.1 11.3 %collective-permute-start.4 = (bf16[2,16,8,256]{3,2,1,0:T(8,128)(2,1)S(1)}, bf16[2,16,8,256]{3,2,1,0:T(8,128)(2,1)S(1)}, u32[]{:S(2)}, u32[]{:S(2)}) collective-permute-start(bf16[2,16,8,256]{3,2,1,0:T(8,128)(2,1)S(1)} %get-tuple-element.54), channel_id=1, source_target_pairs={{1,0},{3,2},{5,4},{7,6},{9,8},{11,10},{13,12},{15,14},{17,16},{19,... | collective-permute-start | bytes 393224 | tf_op jit(solution)/shard_map/ppermute | solution.py:669
  25.4 7.4 %collective-permute-start.5 = (bf16[2,16,3,256]{3,2,1,0:T(4,128)(2,1)S(1)}, bf16[2,16,3,256]{3,2,1,0:T(4,128)(2,1)S(1)}, u32[]{:S(2)}, u32[]{:S(2)}) collective-permute-start(bf16[2,16,3,256]{3,2,1,0:T(4,128)(2,1)S(1)} %get-tuple-element.55), channel_id=1, source_target_pairs={{1,2},{3,6},{7,4},{5,8},{9,10},{11,14},{15,12},{13,0},{17,18},{19,... | collective-permute-start | bytes 147464 | tf_op jit(solution)/shard_map/ppermute | solution.py:670
  26.7 6.1 %collective-permute-start.6 = (bf16[2,16,3,256]{3,2,1,0:T(4,128)(2,1)S(1)}, bf16[2,16,3,256]{3,2,1,0:T(4,128)(2,1)S(1)}, u32[]{:S(2)}, u32[]{:S(2)}) collective-permute-start(bf16[2,16,3,256]{3,2,1,0:T(4,128)(2,1)S(1)} %get-tuple-element.56), channel_id=1, source_target_pairs={{1,12},{3,0},{7,2},{5,6},{9,4},{11,8},{15,10},{13,14},{17,28},{19,... | collective-permute-start | bytes 147464 | tf_op jit(solution)/shard_map/ppermute | solution.py:673
  28.0 7.4 %copy-start.9 = (bf16[512,1024]{1,0:T(8,128)(2,1)S(1)}, bf16[512,1024]{1,0:T(8,128)(2,1)}, u32[]{:S(2)}) copy-start(bf16[512,1024]{1,0:T(8,128)(2,1)} %copy-done.8) | copy-start | bytes 3145732
  28.0 7.4 %copy-start.11 = (f32[512,256]{1,0:T(8,128)S(1)}, f32[512,256]{1,0:T(8,128)}, u32[]{:S(2)}) copy-start(f32[512,256]{1,0:T(8,128)} %copy-done.10) | copy-start | bytes 1572868
  28.0 11.4 %collective-permute-start.12 = (bf16[2,16,8,256]{3,2,1,0:T(8,128)(2,1)S(1)}, bf16[2,16,8,256]{3,2,1,0:T(8,128)(2,1)S(1)}, u32[]{:S(2)}, u32[]{:S(2)}) collective-permute-start(bf16[2,16,8,256]{3,2,1,0:T(8,128)(2,1)S(1)} %get-tuple-element.54), channel_id=1, source_target_pairs={{1,8},{5,12},{9,0},{13,4},{3,10},{7,14},{11,2},{15,6},{17,24},{21,... | collective-permute-start | bytes 393224 | tf_op jit(solution)/shard_map/ppermute | solution.py:666
  29.5 10.0 %collective-permute-start.11 = (bf16[2,16,8,256]{3,2,1,0:T(8,128)(2,1)S(1)}, bf16[2,16,8,256]{3,2,1,0:T(8,128)(2,1)S(1)}, u32[]{:S(2)}, u32[]{:S(2)}) collective-permute-start(bf16[2,16,8,256]{3,2,1,0:T(8,128)(2,1)S(1)} %get-tuple-element.59.core1), channel_id=1, source_target_pairs={{1,9},{5,13},{9,1},{13,5},{3,11},{7,15},{11,3},{15,7},{17,25},{21,... | collective-permute-start | bytes 393224 | tf_op jit(solution)/shard_map/ppermute | solution.py:666
  32.8 11.2 %collective-permute-start.16 = (bf16[512,256]{1,0:T(8,128)(2,1)S(1)}, bf16[512,256]{1,0:T(8,128)(2,1)S(1)}, u32[]{:S(2)}, u32[]{:S(2)}) collective-permute-start(bf16[512,256]{1,0:T(8,128)(2,1)S(1)} %shard_map.125.refs_0_), channel_id=1, source_target_pairs={{0,4},{4,0},{8,12},{12,8},{1,5},{5,1},{9,13},{13,9},{2,6},{6,2},{1... | collective-permute-start | bytes 786440 | tf_op jit(solution)/shard_map/ppermute | solution.py:662
  34.3 14.5 %collective-permute-start.9 = (bf16[512,256]{1,0:T(8,128)(2,1)S(1)}, bf16[512,256]{1,0:T(8,128)(2,1)S(1)}, u32[]{:S(2)}, u32[]{:S(2)}) collective-permute-start(bf16[512,256]{1,0:T(8,128)(2,1)S(1)} %shard_map.125.refs_0_), channel_id=1, source_target_pairs={{0,2},{2,0},{1,3},{3,1},{4,6},{6,4},{5,7},{7,5},{8,10},{10,8},{9,1... | collective-permute-start | bytes 786440 | tf_op jit(solution)/shard_map/ppermute | solution.py:701
  38.4 5.5 %collective-permute-start.7 = (bf16[2,8,8,256]{3,2,1,0:T(8,128)(2,1)S(1)}, bf16[2,8,8,256]{3,2,1,0:T(8,128)(2,1)S(1)}, u32[]{:S(2)}, u32[]{:S(2)}) collective-permute-start(bf16[2,8,8,256]{3,2,1,0:T(8,128)(2,1)S(1)} %constant_dynamic-slice_fusion), channel_id=1, source_target_pairs={{0,2},{2,0},{1,3},{3,1},{4,6},{6,4},{5,7},{7,5},{8,10},{10,8},{9,1... | collective-permute-start | bytes 196616 | tf_op jit(solution)/shard_map/ppermute | solution.py:737
  40.2 3.8 %copy-start.13 = (bf16[2,16,8,256]{3,2,1,0:T(8,128)(2,1)S(1)}, bf16[2,16,8,256]{3,2,1,0:T(8,128)(2,1)}, u32[]{:S(2)}) copy-start(bf16[2,16,8,256]{3,2,1,0:T(8,128)(2,1)} %copy-done.12) | copy-start | bytes 393220
  40.2 9.0 %collective-permute-start.13 = (bf16[512,256]{1,0:T(8,128)(2,1)S(1)}, bf16[512,256]{1,0:T(8,128)(2,1)S(1)}, u32[]{:S(2)}, u32[]{:S(2)}) collective-permute-start(bf16[512,256]{1,0:T(8,128)(2,1)S(1)} %shard_map.126.refs_1_), channel_id=1, source_target_pairs={{0,4},{4,0},{8,12},{12,8},{1,5},{5,1},{9,13},{13,9},{2,6},{6,2},{1... | collective-permute-start | bytes 786440 | tf_op jit(solution)/shard_map/ppermute | solution.py:662
  40.9 13.6 %collective-permute-start.15 = (bf16[512,256]{1,0:T(8,128)(2,1)S(1)}, bf16[512,256]{1,0:T(8,128)(2,1)S(1)}, u32[]{:S(2)}, u32[]{:S(2)}) collective-permute-start(bf16[512,256]{1,0:T(8,128)(2,1)S(1)} %shard_map.126.refs_1_), channel_id=1, source_target_pairs={{0,2},{2,0},{1,3},{3,1},{4,6},{6,4},{5,7},{7,5},{8,10},{10,8},{9,1... | collective-permute-start | bytes 786440 | tf_op jit(solution)/shard_map/ppermute | solution.py:701
  45.6 7.1 %collective-permute-start.17 = (f32[49,256]{1,0:T(8,128)S(1)}, f32[49,256]{1,0:T(8,128)S(1)}, u32[]{:S(2)}, u32[]{:S(2)}) collective-permute-start(f32[49,256]{1,0:T(8,128)S(1)} %shard_map.131.first), channel_id=1, source_target_pairs={{0,8},{4,12},{8,0},{12,4},{1,9},{5,13},{9,1},{13,5},{2,10},{6,14},... | collective-permute-start | bytes 150536 | tf_op jit(solution)/shard_map/ppermute | solution.py:662
  48.8 10.9 %collective-permute-start.10 = (bf16[512,256]{1,0:T(8,128)(2,1)S(1)}, bf16[512,256]{1,0:T(8,128)(2,1)S(1)}, u32[]{:S(2)}, u32[]{:S(2)}) collective-permute-start(bf16[512,256]{1,0:T(8,128)(2,1)S(1)} %collective-permute-done.9.refs_0_), channel_id=1, source_target_pairs={{0,4},{4,0},{8,12},{12,8},{1,5},{5,1},{9,13},{13,9},{2,6},{6,2},{1... | collective-permute-start | bytes 786440 | tf_op jit(solution)/shard_map/ppermute | solution.py:662
  49.2 10.5 %collective-permute-start.14 = (bf16[512,256]{1,0:T(8,128)(2,1)S(1)}, bf16[512,256]{1,0:T(8,128)(2,1)S(1)}, u32[]{:S(2)}, u32[]{:S(2)}) collective-permute-start(bf16[512,256]{1,0:T(8,128)(2,1)S(1)} %collective-permute-done.13.refs_1_), channel_id=1, source_target_pairs={{0,2},{2,0},{1,3},{3,1},{4,6},{6,4},{5,7},{7,5},{8,10},{10,8},{9,1... | collective-permute-start | bytes 786440 | tf_op jit(solution)/shard_map/ppermute | solution.py:703
  52.7 6.5 %collective-permute-start.18 = (f32[49,256]{1,0:T(8,128)S(1)}, f32[49,256]{1,0:T(8,128)S(1)}, u32[]{:S(2)}, u32[]{:S(2)}) collective-permute-start(f32[49,256]{1,0:T(8,128)S(1)} %shard_map.132.first), channel_id=1, source_target_pairs={{0,4},{4,0},{8,12},{12,8},{1,5},{5,1},{9,13},{13,9},{2,6},{6,2},{1... | collective-permute-start | bytes 150536 | tf_op jit(solution)/shard_map/ppermute | solution.py:662
  59.2 4.2 %collective-permute-start.19 = (f32[49,256]{1,0:T(8,128)S(1)}, f32[49,256]{1,0:T(8,128)S(1)}, u32[]{:S(2)}, u32[]{:S(2)}) collective-permute-start(f32[49,256]{1,0:T(8,128)S(1)} %shard_map.133.first), channel_id=1, source_target_pairs={{0,2},{2,0},{1,3},{3,1},{4,6},{6,4},{5,7},{7,5},{8,10},{10,8},{9,1... | collective-permute-start | bytes 150536 | tf_op jit(solution)/shard_map/ppermute | solution.py:662

commit v4 on v3

--- a/solution.py
+++ b/solution.py
@@ -678,7 +678,7 @@
         [like((2 * cells, chans), BF16)],
         [],
         place, core1, across(core1, 1), core0, across(dxm1, 0), left0, right0,
-        micros=0.5,
+        micros=1.5,
         specs=[smem] + [vmem] * 4 + [anywhere] * 2,
     )
     (normed_pair,) = call(
@@ -686,7 +686,7 @@
         [like((2 * cells, chans), BF16)],
         [],
         normed, exchanged(normed, "lon", far_step), left0, right0,
-        micros=0.5,
+        micros=1.5,
         specs=[vmem] * 2 + [anywhere] * 2,
     )
     dx0, dz0 = call(
@@ -706,8 +706,8 @@
         pair_kernel_grad_body,
         [like((49, chans), F32)],
         [pltpu.VMEM(shape, BF16)],
-        place, wide, dz1, dz0, normed_near,
-        micros=3.0,
+        place, wide, dz1, dz0, normed_far,
+        micros=1.5,
         specs=[smem] + [vmem] * 3 + [anywhere],
     )
     weights = (weight_in, bias_in, weight_out)

time: 64.4 us -> 61.7 us (0.958)
  waiting for transfers between devices: 13.4 us -> 10.1 us
  starting transfers between devices: 23.7 us -> 25 us
  local copies, waits for them, and re-layouts: 2.6 us -> 1.94 us
    ppermute x1, waiting for transfers between devices: 2.63 us -> 0.77 us  [pair_shards(): lax.ppermute(last3, axes, [(device(p) * 2 + 1, device(p + 1) * 2) for p i...]
    ppermute x7, waiting for transfers between devices: 5.55 us -> 4.08 us  [exchanged(): lax.ppermute(value, axis, [(i, i ^ step) for i in range(lax.axis_size(axi...]
    ppermute x7, starting transfers between devices: 6.11 us -> 7.11 us  [exchanged(): lax.ppermute(value, axis, [(i, i ^ step) for i in range(lax.axis_size(axi...]
    unnamed x28 -> x24, local copies, waits for them, and re-layouts: 2.59 us -> 1.92 us
  transfers between devices with their start and end apart: 20 -> 20, of which waited for: 7 -> 7; matrix products, arithmetic and copies ran while one was open for 1% -> 1% of each run, Pallas kernels for 32% -> 33%
where the time goes in v4:
time: 61.7 us; the launch traced here: 61.4 us
  starting transfers between devices  25 us (41%)
  Pallas kernels  22.7 us (37%)
  waiting for transfers between devices  10.1 us (16%)
  local copies, waits for them, and re-layouts  1.94 us (3%)
  between operations  0.91 us (1%)
  other arithmetic  0.78 us (1%)
    pallas_call x15, Pallas kernels, call(): pl.pallas_call(body, out_shape=outs, in_specs=specs, out_specs=[pl.BlockS...  22.7 us
    ppermute x7, starting transfers between devices, exchanged(): lax.ppermute(value, axis, [(i, i ^ step) for i in range(lax.axis_size(axi...  7.11 us
    ppermute x1, starting transfers between devices, pair_shards(): near = lax.ppermute(near, ('lon', 'lat'), near_pairs)  5.12 us
    ppermute x7, waiting for transfers between devices, exchanged(): lax.ppermute(value, axis, [(i, i ^ step) for i in range(lax.axis_size(axi...  4.08 us
    ppermute x1, waiting for transfers between devices, pair_shards(): far = lax.ppermute(far, ('lon', 'lat'), far_pairs)  3.84 us
    ppermute x2, starting transfers between devices, pair_shards(): lax.ppermute(v, 'lat', swap)  2.94 us
    ppermute x2, starting transfers between devices, across(): return lax.ppermute(value, ('lon', 'section'), pairs)  2.08 us
    unnamed x24, local copies, waits for them, and re-layouts  1.92 us
  transfers between devices with their start and end apart: 20, of which 7 were waited for; matrix products, arithmetic and copies ran while one was open for 1% of the time, Pallas kernels for 33%

profile of v4, /device:TPU:0, one launch (start us, length us, event | category | flops | bytes accessed | tf_op | source)
XLA Modules:
  0.0 61.4 jit_solution(5358949062675940877)
XLA Ops:
  0.6 0.1 pad_add_fusion.place
  0.7 0.9 %copy-done.2 = bf16[2,8,16,256]{3,2,1,0:T(8,128)(2,1)S(1)} copy-done((bf16[2,8,16,256]{3,2,1,0:T(8,128)(2,1)S(1)}, bf16[2,8,16,256]{3,2,1,0:T(8,128)(2,1)}, u32[]{:S(2)}) %copy-start.2) | copy-done | bytes 131096
  1.6 0.7 %copy-done.4 = s32[8,16]{1,0:T(8,128)S(1)} copy-done((s32[8,16]{1,0:T(8,128)S(1)}, s32[8,16]{1,0:T(8,128)}, u32[]{:S(2)}) %copy-start.4) | copy-done | bytes 536
  2.3 0.0 copy-start.6
  2.3 0.0 copy-start.7
  2.3 1.6 %shard_map.120 = (bf16[2,8,16,256]{3,2,1,0:T(8,128)(2,1)S(1)}, bf16[3,8,16,256]{3,2,1,0:T(8,128)(2,1)S(1)}, bf16[144,256]{1,0:T(8,128)(2,1)S(1)}, bf16[144,256]{1,0:T(8,128)(2,1)S(1)}) custom-call(s32[3]{0:T(128)S(1)} %pad_add_fusion.place, bf16[2,8,16,256]{3,2,1,0:T(8,128)(2,1)} %bitcast.3.x_far, bf16[2,8,16,256]{3,2,1,0:T(8,128)(2,1)S(1)} %copy-done.2, ...), custom_call_target="tpu_custom_call" | custom-call | flops 1100000000 | bytes 3600000 | tf_op jit(solution)/shard_map/pallas_call | solution.py:24
  4.0 5.1 %collective-permute-start = (bf16[144,256]{1,0:T(8,128)(2,1)S(1)}, bf16[144,256]{1,0:T(8,128)(2,1)S(1)}, u32[]{:S(2)}, u32[]{:S(2)}) collective-permute-start(bf16[144,256]{1,0:T(8,128)(2,1)S(1)} %get-tuple-element.39), channel_id=1, source_target_pairs={{0,12},{2,6},{6,2},{4,8},{8,4},{10,14},{14,10},{12,0},{1,13},{3,7}... | collective-permute-start | bytes 221192 | tf_op jit(solution)/shard_map/ppermute | solution.py:619
  9.1 1.0 %collective-permute-start.2 = (bf16[144,256]{1,0:T(8,128)(2,1)S(1)}, bf16[144,256]{1,0:T(8,128)(2,1)S(1)}, u32[]{:S(2)}, u32[]{:S(2)}) collective-permute-start(bf16[144,256]{1,0:T(8,128)(2,1)S(1)} %get-tuple-element.42), channel_id=1, source_target_pairs={{0,6},{2,12},{6,8},{4,2},{8,14},{10,4},{14,0},{12,10},{1,7},{3,13}... | collective-permute-start | bytes 221192 | tf_op jit(solution)/shard_map/ppermute | solution.py:620
  10.1 1.4 %collective-permute-done.near.refs_2_ = bf16[144,256]{1,0:T(8,128)(2,1)S(1)} collective-permute-done((bf16[144,256]{1,0:T(8,128)(2,1)S(1)}, bf16[144,256]{1,0:T(8,128)(2,1)S(1)}, u32[]{:S(2)}, u32[]{:S(2)}) %collective-permute-start) | collective-permute-done | bytes 73760 | tf_op jit(solution)/shard_map/ppermute | solution.py:619
  11.5 0.2 shard_map.121
  11.7 0.7 %collective-permute-start.1 = (bf16[3,8,16,256]{3,2,1,0:T(8,128)(2,1)S(1)}, bf16[3,8,16,256]{3,2,1,0:T(8,128)(2,1)S(1)}, u32[]{:S(2)}, u32[]{:S(2)}) collective-permute-start(bf16[3,8,16,256]{3,2,1,0:T(8,128)(2,1)S(1)} %get-tuple-element.41.refs_0_), channel_id=1, source_target_pairs={{1,3},{3,1},{5,7},{7,5},{9,11},{11,9},{13,15},{15,13},{17,19},{19,... | collective-permute-start | bytes 589832 | tf_op jit(solution)/shard_map/ppermute | solution.py:629
  12.4 3.8 %collective-permute-done.2.far.refs_3_ = bf16[144,256]{1,0:T(8,128)(2,1)S(1)} collective-permute-done((bf16[144,256]{1,0:T(8,128)(2,1)S(1)}, bf16[144,256]{1,0:T(8,128)(2,1)S(1)}, u32[]{:S(2)}, u32[]{:S(2)}) %collective-permute-start.2) | collective-permute-done | bytes 73760 | tf_op jit(solution)/shard_map/ppermute | solution.py:620
  16.3 6.0 %shard_map.122 = (f32[2,2,22,24,128]{4,3,2,1,0:T(8,128)S(1)}, bf16[256,256]{1,0:T(8,128)(2,1)S(1)}, f32[512,256]{1,0:T(8,128)S(1)}, f32[512,1]{1,0:T(8,128)S(1)}, bf16[512,1024]{1,0:T(8,128)(2,1)S(1)}) custom-call(s32[3]{0:T(128)S(1)} %pad_add_fusion.place, bf16[2,8,16,256]{3,2,1,0:T(8,128)(2,1)S(1)} %get-tuple-element.43.x, ...), custom_call_target="tpu_custom_call" | custom-call | flops 7150000128 | bytes 23400000 | tf_op jit(solution)/shard_map/pallas_call | solution.py:24
  22.3 0.0 copy-start.8
  22.3 0.0 copy-start.10
  22.3 0.3 collective-permute-start.8
  22.6 0.5 shard_map.123
  23.2 0.1 copy-done.8
  23.3 0.2 copy-done.10
  23.4 1.3 %collective-permute-start.5 = (bf16[2,16,3,256]{3,2,1,0:T(4,128)(2,1)S(1)}, bf16[2,16,3,256]{3,2,1,0:T(4,128)(2,1)S(1)}, u32[]{:S(2)}, u32[]{:S(2)}) collective-permute-start(bf16[2,16,3,256]{3,2,1,0:T(4,128)(2,1)S(1)} %get-tuple-element.55), channel_id=1, source_target_pairs={{1,2},{3,6},{7,4},{5,8},{9,10},{11,14},{15,12},{13,0},{17,18},{19,... | collective-permute-start | bytes 147464 | tf_op jit(solution)/shard_map/ppermute | solution.py:670
  24.7 1.3 %collective-permute-start.6 = (bf16[2,16,3,256]{3,2,1,0:T(4,128)(2,1)S(1)}, bf16[2,16,3,256]{3,2,1,0:T(4,128)(2,1)S(1)}, u32[]{:S(2)}, u32[]{:S(2)}) collective-permute-start(bf16[2,16,3,256]{3,2,1,0:T(4,128)(2,1)S(1)} %get-tuple-element.56), channel_id=1, source_target_pairs={{1,12},{3,0},{7,2},{5,6},{9,4},{11,8},{15,10},{13,14},{17,28},{19,... | collective-permute-start | bytes 147464 | tf_op jit(solution)/shard_map/ppermute | solution.py:673
  26.0 1.3 %collective-permute-start.4 = (bf16[2,16,8,256]{3,2,1,0:T(8,128)(2,1)S(1)}, bf16[2,16,8,256]{3,2,1,0:T(8,128)(2,1)S(1)}, u32[]{:S(2)}, u32[]{:S(2)}) collective-permute-start(bf16[2,16,8,256]{3,2,1,0:T(8,128)(2,1)S(1)} %get-tuple-element.54), channel_id=1, source_target_pairs={{1,0},{3,2},{5,4},{7,6},{9,8},{11,10},{13,12},{15,14},{17,16},{19,... | collective-permute-start | bytes 393224 | tf_op jit(solution)/shard_map/ppermute | solution.py:669
  27.3 1.3 %collective-permute-start.12 = (bf16[2,16,8,256]{3,2,1,0:T(8,128)(2,1)S(1)}, bf16[2,16,8,256]{3,2,1,0:T(8,128)(2,1)S(1)}, u32[]{:S(2)}, u32[]{:S(2)}) collective-permute-start(bf16[2,16,8,256]{3,2,1,0:T(8,128)(2,1)S(1)} %get-tuple-element.54), channel_id=1, source_target_pairs={{1,8},{5,12},{9,0},{13,4},{3,10},{7,14},{11,2},{15,6},{17,24},{21,... | collective-permute-start | bytes 393224 | tf_op jit(solution)/shard_map/ppermute | solution.py:666
  28.6 0.6 collective-permute-done.8.second
  29.2 0.8 %collective-permute-start.11 = (bf16[2,16,8,256]{3,2,1,0:T(8,128)(2,1)S(1)}, bf16[2,16,8,256]{3,2,1,0:T(8,128)(2,1)S(1)}, u32[]{:S(2)}, u32[]{:S(2)}) collective-permute-start(bf16[2,16,8,256]{3,2,1,0:T(8,128)(2,1)S(1)} %get-tuple-element.59.core1), channel_id=1, source_target_pairs={{1,9},{5,13},{9,1},{13,5},{3,11},{7,15},{11,3},{15,7},{17,25},{21,... | collective-permute-start | bytes 393224 | tf_op jit(solution)/shard_map/ppermute | solution.py:666
  30.0 0.8 %collective-permute-done.5.refs_1_.left0 = bf16[2,16,3,256]{3,2,1,0:T(4,128)(2,1)S(1)} collective-permute-done((bf16[2,16,3,256]{3,2,1,0:T(4,128)(2,1)S(1)}, bf16[2,16,3,256]{3,2,1,0:T(4,128)(2,1)S(1)}, u32[]{:S(2)}, u32[]{:S(2)}) %collective-permute-start.5) | collective-permute-done | bytes 49184 | tf_op jit(solution)/shard_map/ppermute | solution.py:670
  30.8 1.5 %collective-permute-start.9 = (bf16[512,256]{1,0:T(8,128)(2,1)S(1)}, bf16[512,256]{1,0:T(8,128)(2,1)S(1)}, u32[]{:S(2)}, u32[]{:S(2)}) collective-permute-start(bf16[512,256]{1,0:T(8,128)(2,1)S(1)} %shard_map.125.refs_0_), channel_id=1, source_target_pairs={{0,2},{2,0},{1,3},{3,1},{4,6},{6,4},{5,7},{7,5},{8,10},{10,8},{9,1... | collective-permute-start | bytes 786440 | tf_op jit(solution)/shard_map/ppermute | solution.py:701
  32.3 1.1 %collective-permute-start.16 = (bf16[512,256]{1,0:T(8,128)(2,1)S(1)}, bf16[512,256]{1,0:T(8,128)(2,1)S(1)}, u32[]{:S(2)}, u32[]{:S(2)}) collective-permute-start(bf16[512,256]{1,0:T(8,128)(2,1)S(1)} %shard_map.125.refs_0_), channel_id=1, source_target_pairs={{0,4},{4,0},{8,12},{12,8},{1,5},{5,1},{9,13},{13,9},{2,6},{6,2},{1... | collective-permute-start | bytes 786440 | tf_op jit(solution)/shard_map/ppermute | solution.py:662
  33.4 3.0 %shard_map.124 = (bf16[2,16,8,256]{3,2,1,0:T(8,128)(2,1)S(1)}, bf16[2,16,8,256]{3,2,1,0:T(8,128)(2,1)S(1)}) custom-call(s32[3]{0:T(128)S(1)} %pad_add_fusion.place, bf16[2,16,8,256]{3,2,1,0:T(8,128)(2,1)S(1)} %collective-permute-done.4.refs_0_.core0, bf16[2,16,3,256]{3,2,1,0:T(4,128)(2,1)S(1)} %collective-permute-done.5.refs_1_.left0, ...), custom_call_target="tpu_custom_call" | custom-call | flops 4950000128 | bytes 16200000 | tf_op jit(solution)/shard_map/pallas_call | solution.py:24
  36.5 1.0 %collective-permute-start.7 = (bf16[2,8,8,256]{3,2,1,0:T(8,128)(2,1)S(1)}, bf16[2,8,8,256]{3,2,1,0:T(8,128)(2,1)S(1)}, u32[]{:S(2)}, u32[]{:S(2)}) collective-permute-start(bf16[2,8,8,256]{3,2,1,0:T(8,128)(2,1)S(1)} %constant_dynamic-slice_fusion), channel_id=1, source_target_pairs={{0,2},{2,0},{1,3},{3,1},{4,6},{6,4},{5,7},{7,5},{8,10},{10,8},{9,1... | collective-permute-start | bytes 196616 | tf_op jit(solution)/shard_map/ppermute | solution.py:737
  37.5 0.8 %shard_map.126.refs_1_ = bf16[512,256]{1,0:T(8,128)(2,1)S(1)} custom-call(s32[3]{0:T(128)S(1)} %pad_add_fusion.place, bf16[2,16,8,256]{3,2,1,0:T(8,128)(2,1)S(1)} %get-tuple-element.59.core1, bf16[2,16,8,256]{3,2,1,0:T(8,128)(2,1)S(1)} %collective-permute-done.11.got1, bf16[2,16,8,256]{3,2,1,0:T(8,128)(2,1)S(1)} %collective-permute-done.4.refs_0_.core0, ...), custom_call_target="tpu_custom_call" | custom-call | flops 1650000000 | bytes 5400000 | tf_op jit(solution)/shard_map/pallas_call | solution.py:24
  38.2 0.7 %collective-permute-start.13 = (bf16[512,256]{1,0:T(8,128)(2,1)S(1)}, bf16[512,256]{1,0:T(8,128)(2,1)S(1)}, u32[]{:S(2)}, u32[]{:S(2)}) collective-permute-start(bf16[512,256]{1,0:T(8,128)(2,1)S(1)} %shard_map.126.refs_1_), channel_id=1, source_target_pairs={{0,4},{4,0},{8,12},{12,8},{1,5},{5,1},{9,13},{13,9},{2,6},{6,2},{1... | collective-permute-start | bytes 786440 | tf_op jit(solution)/shard_map/ppermute | solution.py:662
  38.9 1.4 %collective-permute-start.15 = (bf16[512,256]{1,0:T(8,128)(2,1)S(1)}, bf16[512,256]{1,0:T(8,128)(2,1)S(1)}, u32[]{:S(2)}, u32[]{:S(2)}) collective-permute-start(bf16[512,256]{1,0:T(8,128)(2,1)S(1)} %shard_map.126.refs_1_), channel_id=1, source_target_pairs={{0,2},{2,0},{1,3},{3,1},{4,6},{6,4},{5,7},{7,5},{8,10},{10,8},{9,1... | collective-permute-start | bytes 786440 | tf_op jit(solution)/shard_map/ppermute | solution.py:701
  40.3 1.6 %shard_map.127 = (f32[256,1024]{1,0:T(8,128)S(1)}, f32[1024,256]{1,0:T(8,128)S(1)}, f32[8,128]{1,0:T(8,128)S(1)}) custom-call(bf16[512,256]{1,0:T(8,128)(2,1)S(1)} %shard_map.125.refs_0_, bf16[512,256]{1,0:T(8,128)(2,1)S(1)} %shard_map.126.refs_1_, bf16[256,1024]{1,0:T(8,128)(2,1)S(1)} %get-tuple-element.47.w_in.refs_8_.refs_7_.refs_2_, ...), custom_call_target="tpu_custom_call" | custom-call | flops 660000000 | bytes 2160000 | tf_op jit(solution)/shard_map/pallas_call | solution.py:24
  42.0 1.6 %shard_map.131.first = f32[49,256]{1,0:T(8,128)S(1)} custom-call(s32[3]{0:T(128)S(1)} %pad_add_fusion.place, f32[2,2,22,24,128]{4,3,2,1,0:T(8,128)S(1)} %get-tuple-element.68.wide, bf16[2,16,8,256]{3,2,1,0:T(8,128)(2,1)S(1)} %get-tuple-element.69.dz1, bf16[2,16,8,256]{3,2,1,0:T(8,128)(2,1)S(1)} %get-tuple-element.70.dz0, ...), custom_call_target="tpu_custom_call" | custom-call | flops 1650000000 | bytes 5400000 | tf_op jit(solution)/shard_map/pallas_call | solution.py:24
  43.7 1.0 %collective-permute-start.17 = (f32[49,256]{1,0:T(8,128)S(1)}, f32[49,256]{1,0:T(8,128)S(1)}, u32[]{:S(2)}, u32[]{:S(2)}) collective-permute-start(f32[49,256]{1,0:T(8,128)S(1)} %shard_map.131.first), channel_id=1, source_target_pairs={{0,8},{4,12},{8,0},{12,4},{1,9},{5,13},{9,1},{13,5},{2,10},{6,14},... | collective-permute-start | bytes 150536 | tf_op jit(solution)/shard_map/ppermute | solution.py:662
  44.6 1.5 %collective-permute-start.10 = (bf16[512,256]{1,0:T(8,128)(2,1)S(1)}, bf16[512,256]{1,0:T(8,128)(2,1)S(1)}, u32[]{:S(2)}, u32[]{:S(2)}) collective-permute-start(bf16[512,256]{1,0:T(8,128)(2,1)S(1)} %collective-permute-done.9.refs_0_.after), channel_id=1, source_target_pairs={{0,4},{4,0},{8,12},{12,8},{1,5},{5,1},{9,13},{13,9},{2,6},{6,2},{1... | collective-permute-start | bytes 786440 | tf_op jit(solution)/shard_map/ppermute | solution.py:662
  46.2 1.4 %collective-permute-done.13.refs_1_ = bf16[512,256]{1,0:T(8,128)(2,1)S(1)} collective-permute-done((bf16[512,256]{1,0:T(8,128)(2,1)S(1)}, bf16[512,256]{1,0:T(8,128)(2,1)S(1)}, u32[]{:S(2)}, u32[]{:S(2)}) %collective-permute-start.13) | collective-permute-done | bytes 262176 | tf_op jit(solution)/shard_map/ppermute | solution.py:662
  47.6 1.2 %collective-permute-start.14 = (bf16[512,256]{1,0:T(8,128)(2,1)S(1)}, bf16[512,256]{1,0:T(8,128)(2,1)S(1)}, u32[]{:S(2)}, u32[]{:S(2)}) collective-permute-start(bf16[512,256]{1,0:T(8,128)(2,1)S(1)} %collective-permute-done.13.refs_1_), channel_id=1, source_target_pairs={{0,2},{2,0},{1,3},{3,1},{4,6},{6,4},{5,7},{7,5},{8,10},{10,8},{9,1... | collective-permute-start | bytes 786440 | tf_op jit(solution)/shard_map/ppermute | solution.py:703
  48.8 0.7 %maximum_bitcast_fusion = bf16[1,2,8,16,256]{4,3,2,1,0:T(8,128)(2,1)} fusion(bf16[2,8,8,256]{3,2,1,0:T(8,128)(2,1)S(1)} %get-tuple-element.75, bf16[2,8,8,256]{3,2,1,0:T(8,128)(2,1)S(1)} %get-tuple-element.74), kind=kLoop, calls=%fused_computation | loop fusion | flops 262144 | bytes 262144 | tf_op jit(solution)/shard_map/broadcast_in_dim | solution.py:741
  49.5 1.5 %collective-permute-start.18 = (f32[49,256]{1,0:T(8,128)S(1)}, f32[49,256]{1,0:T(8,128)S(1)}, u32[]{:S(2)}, u32[]{:S(2)}) collective-permute-start(f32[49,256]{1,0:T(8,128)S(1)} %shard_map.132.first), channel_id=1, source_target_pairs={{0,4},{4,0},{8,12},{12,8},{1,5},{5,1},{9,13},{13,9},{2,6},{6,2},{1... | collective-permute-start | bytes 150536 | tf_op jit(solution)/shard_map/ppermute | solution.py:662
  51.0 1.7 %shard_map.128 = (f32[256,1024]{1,0:T(8,128)S(1)}, f32[1024,256]{1,0:T(8,128)S(1)}, f32[8,128]{1,0:T(8,128)S(1)}) custom-call(bf16[512,256]{1,0:T(8,128)(2,1)S(1)} %collective-permute-done.16.refs_0_, bf16[512,256]{1,0:T(8,128)(2,1)S(1)} %collective-permute-done.13.refs_1_, bf16[256,1024]{1,0:T(8,128)(2,1)S(1)} %get-tuple-element.47.w_in.refs_8_.refs_7_.refs_2_, ...), custom_call_target="tpu_custom_call" | custom-call | flops 660000000 | bytes 2160000 | tf_op jit(solution)/shard_map/pallas_call | solution.py:24
  52.7 2.2 %shard_map.129 = (f32[256,1024]{1,0:T(8,128)S(1)}, f32[1024,256]{1,0:T(8,128)S(1)}, f32[8,128]{1,0:T(8,128)}) custom-call(bf16[512,256]{1,0:T(8,128)(2,1)S(1)} %collective-permute-done.9.refs_0_.after, bf16[512,256]{1,0:T(8,128)(2,1)S(1)} %collective-permute-done.15.refs_1_, bf16[256,1024]{1,0:T(8,128)(2,1)S(1)} %get-tuple-element.47.w_in.refs_8_.refs_7_.refs_2_, ...), custom_call_target="tpu_custom_call" | custom-call | flops 660000000 | bytes 2160000 | tf_op jit(solution)/shard_map/pallas_call | solution.py:24
  54.9 1.5 %collective-permute-done.18.second = f32[49,256]{1,0:T(8,128)S(1)} collective-permute-done((f32[49,256]{1,0:T(8,128)S(1)}, f32[49,256]{1,0:T(8,128)S(1)}, u32[]{:S(2)}, u32[]{:S(2)}) %collective-permute-start.18) | collective-permute-done | bytes 50208 | tf_op jit(solution)/shard_map/ppermute | solution.py:662
  56.4 1.1 %collective-permute-start.19 = (f32[49,256]{1,0:T(8,128)S(1)}, f32[49,256]{1,0:T(8,128)S(1)}, u32[]{:S(2)}, u32[]{:S(2)}) collective-permute-start(f32[49,256]{1,0:T(8,128)S(1)} %shard_map.133.first), channel_id=1, source_target_pairs={{0,2},{2,0},{1,3},{3,1},{4,6},{6,4},{5,7},{7,5},{8,10},{10,8},{9,1... | collective-permute-start | bytes 150536 | tf_op jit(solution)/shard_map/ppermute | solution.py:662
  57.4 2.7 %shard_map.130 = (f32[256,1024]{1,0:T(8,128)}, f32[1024,256]{1,0:T(8,128)}, f32[8,128]{1,0:T(8,128)S(1)}) custom-call(bf16[512,256]{1,0:T(8,128)(2,1)S(1)} %collective-permute-done.10.refs_0_, bf16[512,256]{1,0:T(8,128)(2,1)S(1)} %collective-permute-done.14.refs_1_, bf16[256,1024]{1,0:T(8,128)(2,1)S(1)} %get-tuple-element.47.w_in.refs_8_.refs_7_.refs_2_, ...), custom_call_target="tpu_custom_call" | custom-call | flops 660000000 | bytes 2160000 | tf_op jit(solution)/shard_map/pallas_call | solution.py:24
  60.1 0.6 %collective-permute-done.19.second = f32[49,256]{1,0:T(8,128)S(1)} collective-permute-done((f32[49,256]{1,0:T(8,128)S(1)}, f32[49,256]{1,0:T(8,128)S(1)}, u32[]{:S(2)}, u32[]{:S(2)}) %collective-permute-start.19) | collective-permute-done | bytes 50208 | tf_op jit(solution)/shard_map/ppermute | solution.py:662
  60.8 0.6 %shard_map.134 = f32[49,1,256]{2,1,0:T(1,128)} custom-call(f32[49,256]{1,0:T(8,128)S(1)} %shard_map.133.first, f32[49,256]{1,0:T(8,128)S(1)} %collective-permute-done.19.second, f32[8,128]{1,0:T(8,128)S(1)} %get-tuple-element.73.after), custom_call_target="tpu_custom_call" | custom-call | flops 220000000 | bytes 720000 | tf_op jit(solution)/shard_map/pallas_call | solution.py:24
  (36 shorter events, 0.2 us)
Async XLA Ops:
  0.7 0.9 %copy-start.2 = (bf16[2,8,16,256]{3,2,1,0:T(8,128)(2,1)S(1)}, bf16[2,8,16,256]{3,2,1,0:T(8,128)(2,1)}, u32[]{:S(2)}) copy-start(bf16[2,8,16,256]{3,2,1,0:T(8,128)(2,1)} %g_far.1) | copy-start | bytes 393220
  1.6 0.7 %copy-start.4 = (s32[8,16]{1,0:T(8,128)S(1)}, s32[8,16]{1,0:T(8,128)}, u32[]{:S(2)}) copy-start(s32[8,16]{1,0:T(8,128)} %mask_far.1) | copy-start | bytes 1540
  2.3 9.2 %copy-start = (bf16[1,256,1024]{2,1,0:T(8,128)(2,1)S(1)}, bf16[1,256,1024]{2,1,0:T(8,128)(2,1)}, u32[]{:S(2)}) copy-start(bf16[1,256,1024]{2,1,0:T(8,128)(2,1)} %param.15) | copy-start | bytes 1572868
  2.3 9.2 %copy-start.1 = (bf16[1,1024,256]{2,1,0:T(8,128)(2,1)S(1)}, bf16[1,1024,256]{2,1,0:T(8,128)(2,1)}, u32[]{:S(2)}) copy-start(bf16[1,1024,256]{2,1,0:T(8,128)(2,1)} %param.17) | copy-start | bytes 1572868
  2.3 9.2 %copy-start.3 = (bf16[1,7,7,256]{3,2,1,0:T(8,128)(2,1)S(1)}, bf16[1,7,7,256]{3,2,1,0:T(8,128)(2,1)}, u32[]{:S(2)}) copy-start(bf16[1,7,7,256]{3,2,1,0:T(8,128)(2,1)} %taps.1) | copy-start | bytes 75268
  2.3 9.2 %copy-start.5 = (f32[1,1024]{1,0:T(1,128)S(1)}, f32[1,1024]{1,0:T(1,128)}, u32[]{:S(2)}) copy-start(f32[1,1024]{1,0:T(1,128)} %refs_3_.1) | copy-start | bytes 12292
  2.3 9.2 %copy-start.6 = (f32[1,256]{1,0:T(1,128)S(1)}, f32[1,256]{1,0:T(1,128)}, u32[]{:S(2)}) copy-start(f32[1,256]{1,0:T(1,128)} %refs_0_.1) | copy-start | bytes 3076
  2.3 9.2 %copy-start.7 = (f32[1,256]{1,0:T(1,128)S(1)}, f32[1,256]{1,0:T(1,128)}, u32[]{:S(2)}) copy-start(f32[1,256]{1,0:T(1,128)} %refs_1_.1) | copy-start | bytes 3076
  4.0 7.5 %collective-permute-start = (bf16[144,256]{1,0:T(8,128)(2,1)S(1)}, bf16[144,256]{1,0:T(8,128)(2,1)S(1)}, u32[]{:S(2)}, u32[]{:S(2)}) collective-permute-start(bf16[144,256]{1,0:T(8,128)(2,1)S(1)} %get-tuple-element.39), channel_id=1, source_target_pairs={{0,12},{2,6},{6,2},{4,8},{8,4},{10,14},{14,10},{12,0},{1,13},{3,7}... | collective-permute-start | bytes 221192 | tf_op jit(solution)/shard_map/ppermute | solution.py:619
  9.1 7.2 %collective-permute-start.3 = (bf16[2,8,16,256]{3,2,1,0:T(8,128)(2,1)}, bf16[2,8,16,256]{3,2,1,0:T(8,128)(2,1)S(1)}, u32[]{:S(2)}, u32[]{:S(2)}) collective-permute-start(bf16[2,8,16,256]{3,2,1,0:T(8,128)(2,1)} %bitcast.3.x_far), channel_id=1, source_target_pairs={{0,2},{2,0},{1,3},{3,1},{4,6},{6,4},{5,7},{7,5},{8,10},{10,8},{9,1... | collective-permute-start | bytes 393224 | tf_op jit(solution)/shard_map/ppermute | solution.py:601
  9.1 7.2 %collective-permute-start.2 = (bf16[144,256]{1,0:T(8,128)(2,1)S(1)}, bf16[144,256]{1,0:T(8,128)(2,1)S(1)}, u32[]{:S(2)}, u32[]{:S(2)}) collective-permute-start(bf16[144,256]{1,0:T(8,128)(2,1)S(1)} %get-tuple-element.42), channel_id=1, source_target_pairs={{0,6},{2,12},{6,8},{4,2},{8,14},{10,4},{14,0},{12,10},{1,7},{3,13}... | collective-permute-start | bytes 221192 | tf_op jit(solution)/shard_map/ppermute | solution.py:620
  11.7 10.9 %collective-permute-start.1 = (bf16[3,8,16,256]{3,2,1,0:T(8,128)(2,1)S(1)}, bf16[3,8,16,256]{3,2,1,0:T(8,128)(2,1)S(1)}, u32[]{:S(2)}, u32[]{:S(2)}) collective-permute-start(bf16[3,8,16,256]{3,2,1,0:T(8,128)(2,1)S(1)} %get-tuple-element.41.refs_0_), channel_id=1, source_target_pairs={{1,3},{3,1},{5,7},{7,5},{9,11},{11,9},{13,15},{15,13},{17,19},{19,... | collective-permute-start | bytes 589832 | tf_op jit(solution)/shard_map/ppermute | solution.py:629
  22.3 1.0 %copy-start.8 = (bf16[512,1024]{1,0:T(8,128)(2,1)}, bf16[512,1024]{1,0:T(8,128)(2,1)S(1)}, u32[]{:S(2)}) copy-start(bf16[512,1024]{1,0:T(8,128)(2,1)S(1)} %get-tuple-element.51.refs_6_.refs_5_) | copy-start | bytes 3145732
  22.3 1.1 %copy-start.10 = (f32[512,256]{1,0:T(8,128)}, f32[512,256]{1,0:T(8,128)S(1)}, u32[]{:S(2)}) copy-start(f32[512,256]{1,0:T(8,128)S(1)} %get-tuple-element.49.refs_4_.refs_3_) | copy-start | bytes 1572868
  22.3 6.9 %collective-permute-start.8 = (bf16[256,256]{1,0:T(8,128)(2,1)S(1)}, bf16[256,256]{1,0:T(8,128)(2,1)S(1)}, u32[]{:S(2)}, u32[]{:S(2)}) collective-permute-start(bf16[256,256]{1,0:T(8,128)(2,1)S(1)} %get-tuple-element.58.first), channel_id=1, source_target_pairs={{0,8},{4,12},{8,0},{12,4},{1,9},{5,13},{9,1},{13,5},{2,10},{6,14},... | collective-permute-start | bytes 393224 | tf_op jit(solution)/shard_map/ppermute | solution.py:662
  23.4 7.4 %collective-permute-start.5 = (bf16[2,16,3,256]{3,2,1,0:T(4,128)(2,1)S(1)}, bf16[2,16,3,256]{3,2,1,0:T(4,128)(2,1)S(1)}, u32[]{:S(2)}, u32[]{:S(2)}) collective-permute-start(bf16[2,16,3,256]{3,2,1,0:T(4,128)(2,1)S(1)} %get-tuple-element.55), channel_id=1, source_target_pairs={{1,2},{3,6},{7,4},{5,8},{9,10},{11,14},{15,12},{13,0},{17,18},{19,... | collective-permute-start | bytes 147464 | tf_op jit(solution)/shard_map/ppermute | solution.py:670
  24.7 6.1 %collective-permute-start.6 = (bf16[2,16,3,256]{3,2,1,0:T(4,128)(2,1)S(1)}, bf16[2,16,3,256]{3,2,1,0:T(4,128)(2,1)S(1)}, u32[]{:S(2)}, u32[]{:S(2)}) collective-permute-start(bf16[2,16,3,256]{3,2,1,0:T(4,128)(2,1)S(1)} %get-tuple-element.56), channel_id=1, source_target_pairs={{1,12},{3,0},{7,2},{5,6},{9,4},{11,8},{15,10},{13,14},{17,28},{19,... | collective-permute-start | bytes 147464 | tf_op jit(solution)/shard_map/ppermute | solution.py:673
  26.0 7.4 %collective-permute-start.4 = (bf16[2,16,8,256]{3,2,1,0:T(8,128)(2,1)S(1)}, bf16[2,16,8,256]{3,2,1,0:T(8,128)(2,1)S(1)}, u32[]{:S(2)}, u32[]{:S(2)}) collective-permute-start(bf16[2,16,8,256]{3,2,1,0:T(8,128)(2,1)S(1)} %get-tuple-element.54), channel_id=1, source_target_pairs={{1,0},{3,2},{5,4},{7,6},{9,8},{11,10},{13,12},{15,14},{17,16},{19,... | collective-permute-start | bytes 393224 | tf_op jit(solution)/shard_map/ppermute | solution.py:669
  27.3 10.1 %collective-permute-start.12 = (bf16[2,16,8,256]{3,2,1,0:T(8,128)(2,1)S(1)}, bf16[2,16,8,256]{3,2,1,0:T(8,128)(2,1)S(1)}, u32[]{:S(2)}, u32[]{:S(2)}) collective-permute-start(bf16[2,16,8,256]{3,2,1,0:T(8,128)(2,1)S(1)} %get-tuple-element.54), channel_id=1, source_target_pairs={{1,8},{5,12},{9,0},{13,4},{3,10},{7,14},{11,2},{15,6},{17,24},{21,... | collective-permute-start | bytes 393224 | tf_op jit(solution)/shard_map/ppermute | solution.py:666
  29.2 4.2 %copy-start.9 = (bf16[512,1024]{1,0:T(8,128)(2,1)S(1)}, bf16[512,1024]{1,0:T(8,128)(2,1)}, u32[]{:S(2)}) copy-start(bf16[512,1024]{1,0:T(8,128)(2,1)} %copy-done.8) | copy-start | bytes 3145732
  29.2 4.2 %copy-start.11 = (f32[512,256]{1,0:T(8,128)S(1)}, f32[512,256]{1,0:T(8,128)}, u32[]{:S(2)}) copy-start(f32[512,256]{1,0:T(8,128)} %copy-done.10) | copy-start | bytes 1572868
  29.2 8.2 %collective-permute-start.11 = (bf16[2,16,8,256]{3,2,1,0:T(8,128)(2,1)S(1)}, bf16[2,16,8,256]{3,2,1,0:T(8,128)(2,1)S(1)}, u32[]{:S(2)}, u32[]{:S(2)}) collective-permute-start(bf16[2,16,8,256]{3,2,1,0:T(8,128)(2,1)S(1)} %get-tuple-element.59.core1), channel_id=1, source_target_pairs={{1,9},{5,13},{9,1},{13,5},{3,11},{7,15},{11,3},{15,7},{17,25},{21,... | collective-permute-start | bytes 393224 | tf_op jit(solution)/shard_map/ppermute | solution.py:666
  30.8 11.2 %collective-permute-start.9 = (bf16[512,256]{1,0:T(8,128)(2,1)S(1)}, bf16[512,256]{1,0:T(8,128)(2,1)S(1)}, u32[]{:S(2)}, u32[]{:S(2)}) collective-permute-start(bf16[512,256]{1,0:T(8,128)(2,1)S(1)} %shard_map.125.refs_0_), channel_id=1, source_target_pairs={{0,2},{2,0},{1,3},{3,1},{4,6},{6,4},{5,7},{7,5},{8,10},{10,8},{9,1... | collective-permute-start | bytes 786440 | tf_op jit(solution)/shard_map/ppermute | solution.py:701
  32.3 18.6 %collective-permute-start.16 = (bf16[512,256]{1,0:T(8,128)(2,1)S(1)}, bf16[512,256]{1,0:T(8,128)(2,1)S(1)}, u32[]{:S(2)}, u32[]{:S(2)}) collective-permute-start(bf16[512,256]{1,0:T(8,128)(2,1)S(1)} %shard_map.125.refs_0_), channel_id=1, source_target_pairs={{0,4},{4,0},{8,12},{12,8},{1,5},{5,1},{9,13},{13,9},{2,6},{6,2},{1... | collective-permute-start | bytes 786440 | tf_op jit(solution)/shard_map/ppermute | solution.py:662
  36.5 5.5 %collective-permute-start.7 = (bf16[2,8,8,256]{3,2,1,0:T(8,128)(2,1)S(1)}, bf16[2,8,8,256]{3,2,1,0:T(8,128)(2,1)S(1)}, u32[]{:S(2)}, u32[]{:S(2)}) collective-permute-start(bf16[2,8,8,256]{3,2,1,0:T(8,128)(2,1)S(1)} %constant_dynamic-slice_fusion), channel_id=1, source_target_pairs={{0,2},{2,0},{1,3},{3,1},{4,6},{6,4},{5,7},{7,5},{8,10},{10,8},{9,1... | collective-permute-start | bytes 196616 | tf_op jit(solution)/shard_map/ppermute | solution.py:737
  38.2 9.3 %collective-permute-start.13 = (bf16[512,256]{1,0:T(8,128)(2,1)S(1)}, bf16[512,256]{1,0:T(8,128)(2,1)S(1)}, u32[]{:S(2)}, u32[]{:S(2)}) collective-permute-start(bf16[512,256]{1,0:T(8,128)(2,1)S(1)} %shard_map.126.refs_1_), channel_id=1, source_target_pairs={{0,4},{4,0},{8,12},{12,8},{1,5},{5,1},{9,13},{13,9},{2,6},{6,2},{1... | collective-permute-start | bytes 786440 | tf_op jit(solution)/shard_map/ppermute | solution.py:662
  38.9 13.8 %collective-permute-start.15 = (bf16[512,256]{1,0:T(8,128)(2,1)S(1)}, bf16[512,256]{1,0:T(8,128)(2,1)S(1)}, u32[]{:S(2)}, u32[]{:S(2)}) collective-permute-start(bf16[512,256]{1,0:T(8,128)(2,1)S(1)} %shard_map.126.refs_1_), channel_id=1, source_target_pairs={{0,2},{2,0},{1,3},{3,1},{4,6},{6,4},{5,7},{7,5},{8,10},{10,8},{9,1... | collective-permute-start | bytes 786440 | tf_op jit(solution)/shard_map/ppermute | solution.py:701
  43.7 5.8 %collective-permute-start.17 = (f32[49,256]{1,0:T(8,128)S(1)}, f32[49,256]{1,0:T(8,128)S(1)}, u32[]{:S(2)}, u32[]{:S(2)}) collective-permute-start(f32[49,256]{1,0:T(8,128)S(1)} %shard_map.131.first), channel_id=1, source_target_pairs={{0,8},{4,12},{8,0},{12,4},{1,9},{5,13},{9,1},{13,5},{2,10},{6,14},... | collective-permute-start | bytes 150536 | tf_op jit(solution)/shard_map/ppermute | solution.py:662
  44.6 12.8 %collective-permute-start.10 = (bf16[512,256]{1,0:T(8,128)(2,1)S(1)}, bf16[512,256]{1,0:T(8,128)(2,1)S(1)}, u32[]{:S(2)}, u32[]{:S(2)}) collective-permute-start(bf16[512,256]{1,0:T(8,128)(2,1)S(1)} %collective-permute-done.9.refs_0_.after), channel_id=1, source_target_pairs={{0,4},{4,0},{8,12},{12,8},{1,5},{5,1},{9,13},{13,9},{2,6},{6,2},{1... | collective-permute-start | bytes 786440 | tf_op jit(solution)/shard_map/ppermute | solution.py:662
  47.6 9.9 %collective-permute-start.14 = (bf16[512,256]{1,0:T(8,128)(2,1)S(1)}, bf16[512,256]{1,0:T(8,128)(2,1)S(1)}, u32[]{:S(2)}, u32[]{:S(2)}) collective-permute-start(bf16[512,256]{1,0:T(8,128)(2,1)S(1)} %collective-permute-done.13.refs_1_), channel_id=1, source_target_pairs={{0,2},{2,0},{1,3},{3,1},{4,6},{6,4},{5,7},{7,5},{8,10},{10,8},{9,1... | collective-permute-start | bytes 786440 | tf_op jit(solution)/shard_map/ppermute | solution.py:703
  49.5 6.9 %collective-permute-start.18 = (f32[49,256]{1,0:T(8,128)S(1)}, f32[49,256]{1,0:T(8,128)S(1)}, u32[]{:S(2)}, u32[]{:S(2)}) collective-permute-start(f32[49,256]{1,0:T(8,128)S(1)} %shard_map.132.first), channel_id=1, source_target_pairs={{0,4},{4,0},{8,12},{12,8},{1,5},{5,1},{9,13},{13,9},{2,6},{6,2},{1... | collective-permute-start | bytes 150536 | tf_op jit(solution)/shard_map/ppermute | solution.py:662
  56.4 4.4 %collective-permute-start.19 = (f32[49,256]{1,0:T(8,128)S(1)}, f32[49,256]{1,0:T(8,128)S(1)}, u32[]{:S(2)}, u32[]{:S(2)}) collective-permute-start(f32[49,256]{1,0:T(8,128)S(1)} %shard_map.133.first), channel_id=1, source_target_pairs={{0,2},{2,0},{1,3},{3,1},{4,6},{6,4},{5,7},{7,5},{8,10},{10,8},{9,1... | collective-permute-start | bytes 150536 | tf_op jit(solution)/shard_map/ppermute | solution.py:662

commit v5 on v4

--- a/solution.py
+++ b/solution.py
@@ -437,7 +437,7 @@
     core = n.reshape(micros * all_rows, reach, chans)[:, HALO : HALO + half]
     normed[...] = core.reshape(normed.shape).astype(BF16)
     h = jnp.dot(n.astype(BF16), w_in[...], preferred_element_type=F32) + b_in[...]
-    slope[...] = gelu_both(h)[1].astype(BF16)
+    slope[...] = gelu_both(h.astype(BF16))[1]
 
 
 def pair_back(gwide, dwide, zhat, rscale, slope, gain, w_in, w_out, kern, dz, emit):

time: 61.7 us -> 61.2 us (level)
  no operation moved by 1% of the time
where the time goes in v5:
time: 61.2 us; the launch traced here: 60.9 us
  starting transfers between devices  25 us (41%)
  Pallas kernels  22.2 us (36%)
  waiting for transfers between devices  10.1 us (17%)
  local copies, waits for them, and re-layouts  1.94 us (3%)
  between operations  0.9 us (1%)
  other arithmetic  0.78 us (1%)
    pallas_call x15, Pallas kernels, call(): pl.pallas_call(body, out_shape=outs, in_specs=specs, out_specs=[pl.BlockS...  22.2 us
    ppermute x7, starting transfers between devices, exchanged(): lax.ppermute(value, axis, [(i, i ^ step) for i in range(lax.axis_size(axi...  7.08 us
    ppermute x1, starting transfers between devices, pair_shards(): near = lax.ppermute(near, ('lon', 'lat'), near_pairs)  5.12 us
    ppermute x7, waiting for transfers between devices, exchanged(): lax.ppermute(value, axis, [(i, i ^ step) for i in range(lax.axis_size(axi...  4.06 us
    ppermute x1, waiting for transfers between devices, pair_shards(): far = lax.ppermute(far, ('lon', 'lat'), far_pairs)  3.84 us
    ppermute x2, starting transfers between devices, pair_shards(): lax.ppermute(v, 'lat', swap)  2.93 us
    ppermute x2, starting transfers between devices, across(): return lax.ppermute(value, ('lon', 'section'), pairs)  2.08 us
    unnamed x24, local copies, waits for them, and re-layouts  1.93 us
  transfers between devices with their start and end apart: 20, of which 7 were waited for; matrix products, arithmetic and copies ran while one was open for 1% of the time, Pallas kernels for 33%

profile of v5, /device:TPU:0, one launch (start us, length us, event | category | flops | bytes accessed | tf_op | source)
XLA Modules:
  0.0 60.9 jit_solution(14912092360153438784)
XLA Ops:
  0.6 0.1 pad_add_fusion.place
  0.7 0.9 %copy-done.2 = bf16[2,8,16,256]{3,2,1,0:T(8,128)(2,1)S(1)} copy-done((bf16[2,8,16,256]{3,2,1,0:T(8,128)(2,1)S(1)}, bf16[2,8,16,256]{3,2,1,0:T(8,128)(2,1)}, u32[]{:S(2)}) %copy-start.2) | copy-done | bytes 131096
  1.6 0.7 %copy-done.4 = s32[8,16]{1,0:T(8,128)S(1)} copy-done((s32[8,16]{1,0:T(8,128)S(1)}, s32[8,16]{1,0:T(8,128)}, u32[]{:S(2)}) %copy-start.4) | copy-done | bytes 536
  2.3 0.0 copy-start.6
  2.3 0.0 copy-start.7
  2.3 1.6 %shard_map.120 = (bf16[2,8,16,256]{3,2,1,0:T(8,128)(2,1)S(1)}, bf16[3,8,16,256]{3,2,1,0:T(8,128)(2,1)S(1)}, bf16[144,256]{1,0:T(8,128)(2,1)S(1)}, bf16[144,256]{1,0:T(8,128)(2,1)S(1)}) custom-call(s32[3]{0:T(128)S(1)} %pad_add_fusion.place, bf16[2,8,16,256]{3,2,1,0:T(8,128)(2,1)} %bitcast.3.x_far, bf16[2,8,16,256]{3,2,1,0:T(8,128)(2,1)S(1)} %copy-done.2, ...), custom_call_target="tpu_custom_call" | custom-call | flops 1100000000 | bytes 3600000 | tf_op jit(solution)/shard_map/pallas_call | solution.py:24
  4.0 5.1 %collective-permute-start = (bf16[144,256]{1,0:T(8,128)(2,1)S(1)}, bf16[144,256]{1,0:T(8,128)(2,1)S(1)}, u32[]{:S(2)}, u32[]{:S(2)}) collective-permute-start(bf16[144,256]{1,0:T(8,128)(2,1)S(1)} %get-tuple-element.39), channel_id=1, source_target_pairs={{0,12},{2,6},{6,2},{4,8},{8,4},{10,14},{14,10},{12,0},{1,13},{3,7}... | collective-permute-start | bytes 221192 | tf_op jit(solution)/shard_map/ppermute | solution.py:619
  9.1 1.0 %collective-permute-start.2 = (bf16[144,256]{1,0:T(8,128)(2,1)S(1)}, bf16[144,256]{1,0:T(8,128)(2,1)S(1)}, u32[]{:S(2)}, u32[]{:S(2)}) collective-permute-start(bf16[144,256]{1,0:T(8,128)(2,1)S(1)} %get-tuple-element.42), channel_id=1, source_target_pairs={{0,6},{2,12},{6,8},{4,2},{8,14},{10,4},{14,0},{12,10},{1,7},{3,13}... | collective-permute-start | bytes 221192 | tf_op jit(solution)/shard_map/ppermute | solution.py:620
  10.1 1.4 %collective-permute-done.near.refs_2_ = bf16[144,256]{1,0:T(8,128)(2,1)S(1)} collective-permute-done((bf16[144,256]{1,0:T(8,128)(2,1)S(1)}, bf16[144,256]{1,0:T(8,128)(2,1)S(1)}, u32[]{:S(2)}, u32[]{:S(2)}) %collective-permute-start) | collective-permute-done | bytes 73760 | tf_op jit(solution)/shard_map/ppermute | solution.py:619
  11.5 0.2 shard_map.121
  11.7 0.7 %collective-permute-start.1 = (bf16[3,8,16,256]{3,2,1,0:T(8,128)(2,1)S(1)}, bf16[3,8,16,256]{3,2,1,0:T(8,128)(2,1)S(1)}, u32[]{:S(2)}, u32[]{:S(2)}) collective-permute-start(bf16[3,8,16,256]{3,2,1,0:T(8,128)(2,1)S(1)} %get-tuple-element.41.refs_0_), channel_id=1, source_target_pairs={{1,3},{3,1},{5,7},{7,5},{9,11},{11,9},{13,15},{15,13},{17,19},{19,... | collective-permute-start | bytes 589832 | tf_op jit(solution)/shard_map/ppermute | solution.py:629
  12.4 3.8 %collective-permute-done.2.far.refs_3_ = bf16[144,256]{1,0:T(8,128)(2,1)S(1)} collective-permute-done((bf16[144,256]{1,0:T(8,128)(2,1)S(1)}, bf16[144,256]{1,0:T(8,128)(2,1)S(1)}, u32[]{:S(2)}, u32[]{:S(2)}) %collective-permute-start.2) | collective-permute-done | bytes 73760 | tf_op jit(solution)/shard_map/ppermute | solution.py:620
  16.3 5.6 %shard_map.122 = (f32[2,2,22,24,128]{4,3,2,1,0:T(8,128)S(1)}, bf16[256,256]{1,0:T(8,128)(2,1)S(1)}, f32[512,256]{1,0:T(8,128)S(1)}, f32[512,1]{1,0:T(8,128)S(1)}, bf16[512,1024]{1,0:T(8,128)(2,1)S(1)}) custom-call(s32[3]{0:T(128)S(1)} %pad_add_fusion.place, bf16[2,8,16,256]{3,2,1,0:T(8,128)(2,1)S(1)} %get-tuple-element.43.x, ...), custom_call_target="tpu_custom_call" | custom-call | flops 7150000128 | bytes 23400000 | tf_op jit(solution)/shard_map/pallas_call | solution.py:24
  21.9 0.0 copy-start.8
  21.9 0.0 copy-start.10
  21.9 0.3 collective-permute-start.8
  22.1 0.5 shard_map.123
  22.7 0.1 copy-done.8
  22.8 0.2 copy-done.10
  23.0 1.3 %collective-permute-start.5 = (bf16[2,16,3,256]{3,2,1,0:T(4,128)(2,1)S(1)}, bf16[2,16,3,256]{3,2,1,0:T(4,128)(2,1)S(1)}, u32[]{:S(2)}, u32[]{:S(2)}) collective-permute-start(bf16[2,16,3,256]{3,2,1,0:T(4,128)(2,1)S(1)} %get-tuple-element.55), channel_id=1, source_target_pairs={{1,2},{3,6},{7,4},{5,8},{9,10},{11,14},{15,12},{13,0},{17,18},{19,... | collective-permute-start | bytes 147464 | tf_op jit(solution)/shard_map/ppermute | solution.py:670
  24.3 1.3 %collective-permute-start.6 = (bf16[2,16,3,256]{3,2,1,0:T(4,128)(2,1)S(1)}, bf16[2,16,3,256]{3,2,1,0:T(4,128)(2,1)S(1)}, u32[]{:S(2)}, u32[]{:S(2)}) collective-permute-start(bf16[2,16,3,256]{3,2,1,0:T(4,128)(2,1)S(1)} %get-tuple-element.56), channel_id=1, source_target_pairs={{1,12},{3,0},{7,2},{5,6},{9,4},{11,8},{15,10},{13,14},{17,28},{19,... | collective-permute-start | bytes 147464 | tf_op jit(solution)/shard_map/ppermute | solution.py:673
  25.6 1.3 %collective-permute-start.4 = (bf16[2,16,8,256]{3,2,1,0:T(8,128)(2,1)S(1)}, bf16[2,16,8,256]{3,2,1,0:T(8,128)(2,1)S(1)}, u32[]{:S(2)}, u32[]{:S(2)}) collective-permute-start(bf16[2,16,8,256]{3,2,1,0:T(8,128)(2,1)S(1)} %get-tuple-element.54), channel_id=1, source_target_pairs={{1,0},{3,2},{5,4},{7,6},{9,8},{11,10},{13,12},{15,14},{17,16},{19,... | collective-permute-start | bytes 393224 | tf_op jit(solution)/shard_map/ppermute | solution.py:669
  26.9 1.3 %collective-permute-start.12 = (bf16[2,16,8,256]{3,2,1,0:T(8,128)(2,1)S(1)}, bf16[2,16,8,256]{3,2,1,0:T(8,128)(2,1)S(1)}, u32[]{:S(2)}, u32[]{:S(2)}) collective-permute-start(bf16[2,16,8,256]{3,2,1,0:T(8,128)(2,1)S(1)} %get-tuple-element.54), channel_id=1, source_target_pairs={{1,8},{5,12},{9,0},{13,4},{3,10},{7,14},{11,2},{15,6},{17,24},{21,... | collective-permute-start | bytes 393224 | tf_op jit(solution)/shard_map/ppermute | solution.py:666
  28.2 0.6 collective-permute-done.8.second
  28.8 0.8 %collective-permute-start.11 = (bf16[2,16,8,256]{3,2,1,0:T(8,128)(2,1)S(1)}, bf16[2,16,8,256]{3,2,1,0:T(8,128)(2,1)S(1)}, u32[]{:S(2)}, u32[]{:S(2)}) collective-permute-start(bf16[2,16,8,256]{3,2,1,0:T(8,128)(2,1)S(1)} %get-tuple-element.59.core1), channel_id=1, source_target_pairs={{1,9},{5,13},{9,1},{13,5},{3,11},{7,15},{11,3},{15,7},{17,25},{21,... | collective-permute-start | bytes 393224 | tf_op jit(solution)/shard_map/ppermute | solution.py:666
  29.6 0.8 %collective-permute-done.5.refs_1_.left0 = bf16[2,16,3,256]{3,2,1,0:T(4,128)(2,1)S(1)} collective-permute-done((bf16[2,16,3,256]{3,2,1,0:T(4,128)(2,1)S(1)}, bf16[2,16,3,256]{3,2,1,0:T(4,128)(2,1)S(1)}, u32[]{:S(2)}, u32[]{:S(2)}) %collective-permute-start.5) | collective-permute-done | bytes 49184 | tf_op jit(solution)/shard_map/ppermute | solution.py:670
  30.4 1.5 %collective-permute-start.9 = (bf16[512,256]{1,0:T(8,128)(2,1)S(1)}, bf16[512,256]{1,0:T(8,128)(2,1)S(1)}, u32[]{:S(2)}, u32[]{:S(2)}) collective-permute-start(bf16[512,256]{1,0:T(8,128)(2,1)S(1)} %shard_map.125.refs_0_), channel_id=1, source_target_pairs={{0,2},{2,0},{1,3},{3,1},{4,6},{6,4},{5,7},{7,5},{8,10},{10,8},{9,1... | collective-permute-start | bytes 786440 | tf_op jit(solution)/shard_map/ppermute | solution.py:701
  31.9 1.1 %collective-permute-start.16 = (bf16[512,256]{1,0:T(8,128)(2,1)S(1)}, bf16[512,256]{1,0:T(8,128)(2,1)S(1)}, u32[]{:S(2)}, u32[]{:S(2)}) collective-permute-start(bf16[512,256]{1,0:T(8,128)(2,1)S(1)} %shard_map.125.refs_0_), channel_id=1, source_target_pairs={{0,4},{4,0},{8,12},{12,8},{1,5},{5,1},{9,13},{13,9},{2,6},{6,2},{1... | collective-permute-start | bytes 786440 | tf_op jit(solution)/shard_map/ppermute | solution.py:662
  33.0 3.0 %shard_map.124 = (bf16[2,16,8,256]{3,2,1,0:T(8,128)(2,1)S(1)}, bf16[2,16,8,256]{3,2,1,0:T(8,128)(2,1)S(1)}) custom-call(s32[3]{0:T(128)S(1)} %pad_add_fusion.place, bf16[2,16,8,256]{3,2,1,0:T(8,128)(2,1)S(1)} %collective-permute-done.4.refs_0_.core0, bf16[2,16,3,256]{3,2,1,0:T(4,128)(2,1)S(1)} %collective-permute-done.5.refs_1_.left0, ...), custom_call_target="tpu_custom_call" | custom-call | flops 4950000128 | bytes 16200000 | tf_op jit(solution)/shard_map/pallas_call | solution.py:24
  36.0 1.0 %collective-permute-start.7 = (bf16[2,8,8,256]{3,2,1,0:T(8,128)(2,1)S(1)}, bf16[2,8,8,256]{3,2,1,0:T(8,128)(2,1)S(1)}, u32[]{:S(2)}, u32[]{:S(2)}) collective-permute-start(bf16[2,8,8,256]{3,2,1,0:T(8,128)(2,1)S(1)} %constant_dynamic-slice_fusion), channel_id=1, source_target_pairs={{0,2},{2,0},{1,3},{3,1},{4,6},{6,4},{5,7},{7,5},{8,10},{10,8},{9,1... | collective-permute-start | bytes 196616 | tf_op jit(solution)/shard_map/ppermute | solution.py:737
  37.0 0.8 %shard_map.126.refs_1_ = bf16[512,256]{1,0:T(8,128)(2,1)S(1)} custom-call(s32[3]{0:T(128)S(1)} %pad_add_fusion.place, bf16[2,16,8,256]{3,2,1,0:T(8,128)(2,1)S(1)} %get-tuple-element.59.core1, bf16[2,16,8,256]{3,2,1,0:T(8,128)(2,1)S(1)} %collective-permute-done.11.got1, bf16[2,16,8,256]{3,2,1,0:T(8,128)(2,1)S(1)} %collective-permute-done.4.refs_0_.core0, ...), custom_call_target="tpu_custom_call" | custom-call | flops 1650000000 | bytes 5400000 | tf_op jit(solution)/shard_map/pallas_call | solution.py:24
  37.8 0.7 %collective-permute-start.13 = (bf16[512,256]{1,0:T(8,128)(2,1)S(1)}, bf16[512,256]{1,0:T(8,128)(2,1)S(1)}, u32[]{:S(2)}, u32[]{:S(2)}) collective-permute-start(bf16[512,256]{1,0:T(8,128)(2,1)S(1)} %shard_map.126.refs_1_), channel_id=1, source_target_pairs={{0,4},{4,0},{8,12},{12,8},{1,5},{5,1},{9,13},{13,9},{2,6},{6,2},{1... | collective-permute-start | bytes 786440 | tf_op jit(solution)/shard_map/ppermute | solution.py:662
  38.5 1.4 %collective-permute-start.15 = (bf16[512,256]{1,0:T(8,128)(2,1)S(1)}, bf16[512,256]{1,0:T(8,128)(2,1)S(1)}, u32[]{:S(2)}, u32[]{:S(2)}) collective-permute-start(bf16[512,256]{1,0:T(8,128)(2,1)S(1)} %shard_map.126.refs_1_), channel_id=1, source_target_pairs={{0,2},{2,0},{1,3},{3,1},{4,6},{6,4},{5,7},{7,5},{8,10},{10,8},{9,1... | collective-permute-start | bytes 786440 | tf_op jit(solution)/shard_map/ppermute | solution.py:701
  39.9 1.7 %shard_map.127 = (f32[256,1024]{1,0:T(8,128)S(1)}, f32[1024,256]{1,0:T(8,128)S(1)}, f32[8,128]{1,0:T(8,128)S(1)}) custom-call(bf16[512,256]{1,0:T(8,128)(2,1)S(1)} %shard_map.125.refs_0_, bf16[512,256]{1,0:T(8,128)(2,1)S(1)} %shard_map.126.refs_1_, bf16[256,1024]{1,0:T(8,128)(2,1)S(1)} %get-tuple-element.47.w_in.refs_8_.refs_7_.refs_2_, ...), custom_call_target="tpu_custom_call" | custom-call | flops 660000000 | bytes 2160000 | tf_op jit(solution)/shard_map/pallas_call | solution.py:24
  41.6 1.6 %shard_map.131.first = f32[49,256]{1,0:T(8,128)S(1)} custom-call(s32[3]{0:T(128)S(1)} %pad_add_fusion.place, f32[2,2,22,24,128]{4,3,2,1,0:T(8,128)S(1)} %get-tuple-element.68.wide, bf16[2,16,8,256]{3,2,1,0:T(8,128)(2,1)S(1)} %get-tuple-element.69.dz1, bf16[2,16,8,256]{3,2,1,0:T(8,128)(2,1)S(1)} %get-tuple-element.70.dz0, ...), custom_call_target="tpu_custom_call" | custom-call | flops 1650000000 | bytes 5400000 | tf_op jit(solution)/shard_map/pallas_call | solution.py:24
  43.2 1.0 %collective-permute-start.17 = (f32[49,256]{1,0:T(8,128)S(1)}, f32[49,256]{1,0:T(8,128)S(1)}, u32[]{:S(2)}, u32[]{:S(2)}) collective-permute-start(f32[49,256]{1,0:T(8,128)S(1)} %shard_map.131.first), channel_id=1, source_target_pairs={{0,8},{4,12},{8,0},{12,4},{1,9},{5,13},{9,1},{13,5},{2,10},{6,14},... | collective-permute-start | bytes 150536 | tf_op jit(solution)/shard_map/ppermute | solution.py:662
  44.2 1.5 %collective-permute-start.10 = (bf16[512,256]{1,0:T(8,128)(2,1)S(1)}, bf16[512,256]{1,0:T(8,128)(2,1)S(1)}, u32[]{:S(2)}, u32[]{:S(2)}) collective-permute-start(bf16[512,256]{1,0:T(8,128)(2,1)S(1)} %collective-permute-done.9.refs_0_.after), channel_id=1, source_target_pairs={{0,4},{4,0},{8,12},{12,8},{1,5},{5,1},{9,13},{13,9},{2,6},{6,2},{1... | collective-permute-start | bytes 786440 | tf_op jit(solution)/shard_map/ppermute | solution.py:662
  45.7 1.4 %collective-permute-done.13.refs_1_ = bf16[512,256]{1,0:T(8,128)(2,1)S(1)} collective-permute-done((bf16[512,256]{1,0:T(8,128)(2,1)S(1)}, bf16[512,256]{1,0:T(8,128)(2,1)S(1)}, u32[]{:S(2)}, u32[]{:S(2)}) %collective-permute-start.13) | collective-permute-done | bytes 262176 | tf_op jit(solution)/shard_map/ppermute | solution.py:662
  47.1 1.3 %collective-permute-start.14 = (bf16[512,256]{1,0:T(8,128)(2,1)S(1)}, bf16[512,256]{1,0:T(8,128)(2,1)S(1)}, u32[]{:S(2)}, u32[]{:S(2)}) collective-permute-start(bf16[512,256]{1,0:T(8,128)(2,1)S(1)} %collective-permute-done.13.refs_1_), channel_id=1, source_target_pairs={{0,2},{2,0},{1,3},{3,1},{4,6},{6,4},{5,7},{7,5},{8,10},{10,8},{9,1... | collective-permute-start | bytes 786440 | tf_op jit(solution)/shard_map/ppermute | solution.py:703
  48.4 0.7 %maximum_bitcast_fusion = bf16[1,2,8,16,256]{4,3,2,1,0:T(8,128)(2,1)} fusion(bf16[2,8,8,256]{3,2,1,0:T(8,128)(2,1)S(1)} %get-tuple-element.75, bf16[2,8,8,256]{3,2,1,0:T(8,128)(2,1)S(1)} %get-tuple-element.74), kind=kLoop, calls=%fused_computation | loop fusion | flops 262144 | bytes 262144 | tf_op jit(solution)/shard_map/broadcast_in_dim | solution.py:741
  49.0 1.5 %collective-permute-start.18 = (f32[49,256]{1,0:T(8,128)S(1)}, f32[49,256]{1,0:T(8,128)S(1)}, u32[]{:S(2)}, u32[]{:S(2)}) collective-permute-start(f32[49,256]{1,0:T(8,128)S(1)} %shard_map.132.first), channel_id=1, source_target_pairs={{0,4},{4,0},{8,12},{12,8},{1,5},{5,1},{9,13},{13,9},{2,6},{6,2},{1... | collective-permute-start | bytes 150536 | tf_op jit(solution)/shard_map/ppermute | solution.py:662
  50.5 1.7 %shard_map.128 = (f32[256,1024]{1,0:T(8,128)S(1)}, f32[1024,256]{1,0:T(8,128)S(1)}, f32[8,128]{1,0:T(8,128)S(1)}) custom-call(bf16[512,256]{1,0:T(8,128)(2,1)S(1)} %collective-permute-done.16.refs_0_, bf16[512,256]{1,0:T(8,128)(2,1)S(1)} %collective-permute-done.13.refs_1_, bf16[256,1024]{1,0:T(8,128)(2,1)S(1)} %get-tuple-element.47.w_in.refs_8_.refs_7_.refs_2_, ...), custom_call_target="tpu_custom_call" | custom-call | flops 660000000 | bytes 2160000 | tf_op jit(solution)/shard_map/pallas_call | solution.py:24
  52.2 2.2 %shard_map.129 = (f32[256,1024]{1,0:T(8,128)S(1)}, f32[1024,256]{1,0:T(8,128)S(1)}, f32[8,128]{1,0:T(8,128)}) custom-call(bf16[512,256]{1,0:T(8,128)(2,1)S(1)} %collective-permute-done.9.refs_0_.after, bf16[512,256]{1,0:T(8,128)(2,1)S(1)} %collective-permute-done.15.refs_1_, bf16[256,1024]{1,0:T(8,128)(2,1)S(1)} %get-tuple-element.47.w_in.refs_8_.refs_7_.refs_2_, ...), custom_call_target="tpu_custom_call" | custom-call | flops 660000000 | bytes 2160000 | tf_op jit(solution)/shard_map/pallas_call | solution.py:24
  54.4 1.5 %collective-permute-done.18.second = f32[49,256]{1,0:T(8,128)S(1)} collective-permute-done((f32[49,256]{1,0:T(8,128)S(1)}, f32[49,256]{1,0:T(8,128)S(1)}, u32[]{:S(2)}, u32[]{:S(2)}) %collective-permute-start.18) | collective-permute-done | bytes 50208 | tf_op jit(solution)/shard_map/ppermute | solution.py:662
  55.9 1.0 %collective-permute-start.19 = (f32[49,256]{1,0:T(8,128)S(1)}, f32[49,256]{1,0:T(8,128)S(1)}, u32[]{:S(2)}, u32[]{:S(2)}) collective-permute-start(f32[49,256]{1,0:T(8,128)S(1)} %shard_map.133.first), channel_id=1, source_target_pairs={{0,2},{2,0},{1,3},{3,1},{4,6},{6,4},{5,7},{7,5},{8,10},{10,8},{9,1... | collective-permute-start | bytes 150536 | tf_op jit(solution)/shard_map/ppermute | solution.py:662
  57.0 2.7 %shard_map.130 = (f32[256,1024]{1,0:T(8,128)}, f32[1024,256]{1,0:T(8,128)}, f32[8,128]{1,0:T(8,128)S(1)}) custom-call(bf16[512,256]{1,0:T(8,128)(2,1)S(1)} %collective-permute-done.10.refs_0_, bf16[512,256]{1,0:T(8,128)(2,1)S(1)} %collective-permute-done.14.refs_1_, bf16[256,1024]{1,0:T(8,128)(2,1)S(1)} %get-tuple-element.47.w_in.refs_8_.refs_7_.refs_2_, ...), custom_call_target="tpu_custom_call" | custom-call | flops 660000000 | bytes 2160000 | tf_op jit(solution)/shard_map/pallas_call | solution.py:24
  59.7 0.6 %collective-permute-done.19.second = f32[49,256]{1,0:T(8,128)S(1)} collective-permute-done((f32[49,256]{1,0:T(8,128)S(1)}, f32[49,256]{1,0:T(8,128)S(1)}, u32[]{:S(2)}, u32[]{:S(2)}) %collective-permute-start.19) | collective-permute-done | bytes 50208 | tf_op jit(solution)/shard_map/ppermute | solution.py:662
  60.3 0.6 %shard_map.134 = f32[49,1,256]{2,1,0:T(1,128)} custom-call(f32[49,256]{1,0:T(8,128)S(1)} %shard_map.133.first, f32[49,256]{1,0:T(8,128)S(1)} %collective-permute-done.19.second, f32[8,128]{1,0:T(8,128)S(1)} %get-tuple-element.73.after), custom_call_target="tpu_custom_call" | custom-call | flops 220000000 | bytes 720000 | tf_op jit(solution)/shard_map/pallas_call | solution.py:24
  (36 shorter events, 0.2 us)
Async XLA Ops:
  0.7 0.9 %copy-start.2 = (bf16[2,8,16,256]{3,2,1,0:T(8,128)(2,1)S(1)}, bf16[2,8,16,256]{3,2,1,0:T(8,128)(2,1)}, u32[]{:S(2)}) copy-start(bf16[2,8,16,256]{3,2,1,0:T(8,128)(2,1)} %g_far.1) | copy-start | bytes 393220
  1.6 0.7 %copy-start.4 = (s32[8,16]{1,0:T(8,128)S(1)}, s32[8,16]{1,0:T(8,128)}, u32[]{:S(2)}) copy-start(s32[8,16]{1,0:T(8,128)} %mask_far.1) | copy-start | bytes 1540
  2.3 9.2 %copy-start = (bf16[1,256,1024]{2,1,0:T(8,128)(2,1)S(1)}, bf16[1,256,1024]{2,1,0:T(8,128)(2,1)}, u32[]{:S(2)}) copy-start(bf16[1,256,1024]{2,1,0:T(8,128)(2,1)} %param.15) | copy-start | bytes 1572868
  2.3 9.2 %copy-start.1 = (bf16[1,1024,256]{2,1,0:T(8,128)(2,1)S(1)}, bf16[1,1024,256]{2,1,0:T(8,128)(2,1)}, u32[]{:S(2)}) copy-start(bf16[1,1024,256]{2,1,0:T(8,128)(2,1)} %param.17) | copy-start | bytes 1572868
  2.3 9.2 %copy-start.3 = (bf16[1,7,7,256]{3,2,1,0:T(8,128)(2,1)S(1)}, bf16[1,7,7,256]{3,2,1,0:T(8,128)(2,1)}, u32[]{:S(2)}) copy-start(bf16[1,7,7,256]{3,2,1,0:T(8,128)(2,1)} %taps.1) | copy-start | bytes 75268
  2.3 9.2 %copy-start.5 = (f32[1,1024]{1,0:T(1,128)S(1)}, f32[1,1024]{1,0:T(1,128)}, u32[]{:S(2)}) copy-start(f32[1,1024]{1,0:T(1,128)} %refs_3_.1) | copy-start | bytes 12292
  2.3 9.2 %copy-start.6 = (f32[1,256]{1,0:T(1,128)S(1)}, f32[1,256]{1,0:T(1,128)}, u32[]{:S(2)}) copy-start(f32[1,256]{1,0:T(1,128)} %refs_0_.1) | copy-start | bytes 3076
  2.3 9.2 %copy-start.7 = (f32[1,256]{1,0:T(1,128)S(1)}, f32[1,256]{1,0:T(1,128)}, u32[]{:S(2)}) copy-start(f32[1,256]{1,0:T(1,128)} %refs_1_.1) | copy-start | bytes 3076
  4.0 7.5 %collective-permute-start = (bf16[144,256]{1,0:T(8,128)(2,1)S(1)}, bf16[144,256]{1,0:T(8,128)(2,1)S(1)}, u32[]{:S(2)}, u32[]{:S(2)}) collective-permute-start(bf16[144,256]{1,0:T(8,128)(2,1)S(1)} %get-tuple-element.39), channel_id=1, source_target_pairs={{0,12},{2,6},{6,2},{4,8},{8,4},{10,14},{14,10},{12,0},{1,13},{3,7}... | collective-permute-start | bytes 221192 | tf_op jit(solution)/shard_map/ppermute | solution.py:619
  9.1 7.2 %collective-permute-start.3 = (bf16[2,8,16,256]{3,2,1,0:T(8,128)(2,1)}, bf16[2,8,16,256]{3,2,1,0:T(8,128)(2,1)S(1)}, u32[]{:S(2)}, u32[]{:S(2)}) collective-permute-start(bf16[2,8,16,256]{3,2,1,0:T(8,128)(2,1)} %bitcast.3.x_far), channel_id=1, source_target_pairs={{0,2},{2,0},{1,3},{3,1},{4,6},{6,4},{5,7},{7,5},{8,10},{10,8},{9,1... | collective-permute-start | bytes 393224 | tf_op jit(solution)/shard_map/ppermute | solution.py:601
  9.1 7.2 %collective-permute-start.2 = (bf16[144,256]{1,0:T(8,128)(2,1)S(1)}, bf16[144,256]{1,0:T(8,128)(2,1)S(1)}, u32[]{:S(2)}, u32[]{:S(2)}) collective-permute-start(bf16[144,256]{1,0:T(8,128)(2,1)S(1)} %get-tuple-element.42), channel_id=1, source_target_pairs={{0,6},{2,12},{6,8},{4,2},{8,14},{10,4},{14,0},{12,10},{1,7},{3,13}... | collective-permute-start | bytes 221192 | tf_op jit(solution)/shard_map/ppermute | solution.py:620
  11.7 10.4 %collective-permute-start.1 = (bf16[3,8,16,256]{3,2,1,0:T(8,128)(2,1)S(1)}, bf16[3,8,16,256]{3,2,1,0:T(8,128)(2,1)S(1)}, u32[]{:S(2)}, u32[]{:S(2)}) collective-permute-start(bf16[3,8,16,256]{3,2,1,0:T(8,128)(2,1)S(1)} %get-tuple-element.41.refs_0_), channel_id=1, source_target_pairs={{1,3},{3,1},{5,7},{7,5},{9,11},{11,9},{13,15},{15,13},{17,19},{19,... | collective-permute-start | bytes 589832 | tf_op jit(solution)/shard_map/ppermute | solution.py:629
  21.9 1.0 %copy-start.8 = (bf16[512,1024]{1,0:T(8,128)(2,1)}, bf16[512,1024]{1,0:T(8,128)(2,1)S(1)}, u32[]{:S(2)}) copy-start(bf16[512,1024]{1,0:T(8,128)(2,1)S(1)} %get-tuple-element.51.refs_6_.refs_5_) | copy-start | bytes 3145732
  21.9 1.1 %copy-start.10 = (f32[512,256]{1,0:T(8,128)}, f32[512,256]{1,0:T(8,128)S(1)}, u32[]{:S(2)}) copy-start(f32[512,256]{1,0:T(8,128)S(1)} %get-tuple-element.49.refs_4_.refs_3_) | copy-start | bytes 1572868
  21.9 6.9 %collective-permute-start.8 = (bf16[256,256]{1,0:T(8,128)(2,1)S(1)}, bf16[256,256]{1,0:T(8,128)(2,1)S(1)}, u32[]{:S(2)}, u32[]{:S(2)}) collective-permute-start(bf16[256,256]{1,0:T(8,128)(2,1)S(1)} %get-tuple-element.58.first), channel_id=1, source_target_pairs={{0,8},{4,12},{8,0},{12,4},{1,9},{5,13},{9,1},{13,5},{2,10},{6,14},... | collective-permute-start | bytes 393224 | tf_op jit(solution)/shard_map/ppermute | solution.py:662
  23.0 7.4 %collective-permute-start.5 = (bf16[2,16,3,256]{3,2,1,0:T(4,128)(2,1)S(1)}, bf16[2,16,3,256]{3,2,1,0:T(4,128)(2,1)S(1)}, u32[]{:S(2)}, u32[]{:S(2)}) collective-permute-start(bf16[2,16,3,256]{3,2,1,0:T(4,128)(2,1)S(1)} %get-tuple-element.55), channel_id=1, source_target_pairs={{1,2},{3,6},{7,4},{5,8},{9,10},{11,14},{15,12},{13,0},{17,18},{19,... | collective-permute-start | bytes 147464 | tf_op jit(solution)/shard_map/ppermute | solution.py:670
  24.3 6.1 %collective-permute-start.6 = (bf16[2,16,3,256]{3,2,1,0:T(4,128)(2,1)S(1)}, bf16[2,16,3,256]{3,2,1,0:T(4,128)(2,1)S(1)}, u32[]{:S(2)}, u32[]{:S(2)}) collective-permute-start(bf16[2,16,3,256]{3,2,1,0:T(4,128)(2,1)S(1)} %get-tuple-element.56), channel_id=1, source_target_pairs={{1,12},{3,0},{7,2},{5,6},{9,4},{11,8},{15,10},{13,14},{17,28},{19,... | collective-permute-start | bytes 147464 | tf_op jit(solution)/shard_map/ppermute | solution.py:673
  25.6 7.4 %collective-permute-start.4 = (bf16[2,16,8,256]{3,2,1,0:T(8,128)(2,1)S(1)}, bf16[2,16,8,256]{3,2,1,0:T(8,128)(2,1)S(1)}, u32[]{:S(2)}, u32[]{:S(2)}) collective-permute-start(bf16[2,16,8,256]{3,2,1,0:T(8,128)(2,1)S(1)} %get-tuple-element.54), channel_id=1, source_target_pairs={{1,0},{3,2},{5,4},{7,6},{9,8},{11,10},{13,12},{15,14},{17,16},{19,... | collective-permute-start | bytes 393224 | tf_op jit(solution)/shard_map/ppermute | solution.py:669
  26.9 10.1 %collective-permute-start.12 = (bf16[2,16,8,256]{3,2,1,0:T(8,128)(2,1)S(1)}, bf16[2,16,8,256]{3,2,1,0:T(8,128)(2,1)S(1)}, u32[]{:S(2)}, u32[]{:S(2)}) collective-permute-start(bf16[2,16,8,256]{3,2,1,0:T(8,128)(2,1)S(1)} %get-tuple-element.54), channel_id=1, source_target_pairs={{1,8},{5,12},{9,0},{13,4},{3,10},{7,14},{11,2},{15,6},{17,24},{21,... | collective-permute-start | bytes 393224 | tf_op jit(solution)/shard_map/ppermute | solution.py:666
  28.8 4.2 %copy-start.9 = (bf16[512,1024]{1,0:T(8,128)(2,1)S(1)}, bf16[512,1024]{1,0:T(8,128)(2,1)}, u32[]{:S(2)}) copy-start(bf16[512,1024]{1,0:T(8,128)(2,1)} %copy-done.8) | copy-start | bytes 3145732
  28.8 4.2 %copy-start.11 = (f32[512,256]{1,0:T(8,128)S(1)}, f32[512,256]{1,0:T(8,128)}, u32[]{:S(2)}) copy-start(f32[512,256]{1,0:T(8,128)} %copy-done.10) | copy-start | bytes 1572868
  28.8 8.3 %collective-permute-start.11 = (bf16[2,16,8,256]{3,2,1,0:T(8,128)(2,1)S(1)}, bf16[2,16,8,256]{3,2,1,0:T(8,128)(2,1)S(1)}, u32[]{:S(2)}, u32[]{:S(2)}) collective-permute-start(bf16[2,16,8,256]{3,2,1,0:T(8,128)(2,1)S(1)} %get-tuple-element.59.core1), channel_id=1, source_target_pairs={{1,9},{5,13},{9,1},{13,5},{3,11},{7,15},{11,3},{15,7},{17,25},{21,... | collective-permute-start | bytes 393224 | tf_op jit(solution)/shard_map/ppermute | solution.py:666
  30.4 11.2 %collective-permute-start.9 = (bf16[512,256]{1,0:T(8,128)(2,1)S(1)}, bf16[512,256]{1,0:T(8,128)(2,1)S(1)}, u32[]{:S(2)}, u32[]{:S(2)}) collective-permute-start(bf16[512,256]{1,0:T(8,128)(2,1)S(1)} %shard_map.125.refs_0_), channel_id=1, source_target_pairs={{0,2},{2,0},{1,3},{3,1},{4,6},{6,4},{5,7},{7,5},{8,10},{10,8},{9,1... | collective-permute-start | bytes 786440 | tf_op jit(solution)/shard_map/ppermute | solution.py:701
  31.9 18.6 %collective-permute-start.16 = (bf16[512,256]{1,0:T(8,128)(2,1)S(1)}, bf16[512,256]{1,0:T(8,128)(2,1)S(1)}, u32[]{:S(2)}, u32[]{:S(2)}) collective-permute-start(bf16[512,256]{1,0:T(8,128)(2,1)S(1)} %shard_map.125.refs_0_), channel_id=1, source_target_pairs={{0,4},{4,0},{8,12},{12,8},{1,5},{5,1},{9,13},{13,9},{2,6},{6,2},{1... | collective-permute-start | bytes 786440 | tf_op jit(solution)/shard_map/ppermute | solution.py:662
  36.0 5.5 %collective-permute-start.7 = (bf16[2,8,8,256]{3,2,1,0:T(8,128)(2,1)S(1)}, bf16[2,8,8,256]{3,2,1,0:T(8,128)(2,1)S(1)}, u32[]{:S(2)}, u32[]{:S(2)}) collective-permute-start(bf16[2,8,8,256]{3,2,1,0:T(8,128)(2,1)S(1)} %constant_dynamic-slice_fusion), channel_id=1, source_target_pairs={{0,2},{2,0},{1,3},{3,1},{4,6},{6,4},{5,7},{7,5},{8,10},{10,8},{9,1... | collective-permute-start | bytes 196616 | tf_op jit(solution)/shard_map/ppermute | solution.py:737
  37.8 9.3 %collective-permute-start.13 = (bf16[512,256]{1,0:T(8,128)(2,1)S(1)}, bf16[512,256]{1,0:T(8,128)(2,1)S(1)}, u32[]{:S(2)}, u32[]{:S(2)}) collective-permute-start(bf16[512,256]{1,0:T(8,128)(2,1)S(1)} %shard_map.126.refs_1_), channel_id=1, source_target_pairs={{0,4},{4,0},{8,12},{12,8},{1,5},{5,1},{9,13},{13,9},{2,6},{6,2},{1... | collective-permute-start | bytes 786440 | tf_op jit(solution)/shard_map/ppermute | solution.py:662
  38.5 13.8 %collective-permute-start.15 = (bf16[512,256]{1,0:T(8,128)(2,1)S(1)}, bf16[512,256]{1,0:T(8,128)(2,1)S(1)}, u32[]{:S(2)}, u32[]{:S(2)}) collective-permute-start(bf16[512,256]{1,0:T(8,128)(2,1)S(1)} %shard_map.126.refs_1_), channel_id=1, source_target_pairs={{0,2},{2,0},{1,3},{3,1},{4,6},{6,4},{5,7},{7,5},{8,10},{10,8},{9,1... | collective-permute-start | bytes 786440 | tf_op jit(solution)/shard_map/ppermute | solution.py:701
  43.2 5.8 %collective-permute-start.17 = (f32[49,256]{1,0:T(8,128)S(1)}, f32[49,256]{1,0:T(8,128)S(1)}, u32[]{:S(2)}, u32[]{:S(2)}) collective-permute-start(f32[49,256]{1,0:T(8,128)S(1)} %shard_map.131.first), channel_id=1, source_target_pairs={{0,8},{4,12},{8,0},{12,4},{1,9},{5,13},{9,1},{13,5},{2,10},{6,14},... | collective-permute-start | bytes 150536 | tf_op jit(solution)/shard_map/ppermute | solution.py:662
  44.2 12.8 %collective-permute-start.10 = (bf16[512,256]{1,0:T(8,128)(2,1)S(1)}, bf16[512,256]{1,0:T(8,128)(2,1)S(1)}, u32[]{:S(2)}, u32[]{:S(2)}) collective-permute-start(bf16[512,256]{1,0:T(8,128)(2,1)S(1)} %collective-permute-done.9.refs_0_.after), channel_id=1, source_target_pairs={{0,4},{4,0},{8,12},{12,8},{1,5},{5,1},{9,13},{13,9},{2,6},{6,2},{1... | collective-permute-start | bytes 786440 | tf_op jit(solution)/shard_map/ppermute | solution.py:662
  47.1 9.9 %collective-permute-start.14 = (bf16[512,256]{1,0:T(8,128)(2,1)S(1)}, bf16[512,256]{1,0:T(8,128)(2,1)S(1)}, u32[]{:S(2)}, u32[]{:S(2)}) collective-permute-start(bf16[512,256]{1,0:T(8,128)(2,1)S(1)} %collective-permute-done.13.refs_1_), channel_id=1, source_target_pairs={{0,2},{2,0},{1,3},{3,1},{4,6},{6,4},{5,7},{7,5},{8,10},{10,8},{9,1... | collective-permute-start | bytes 786440 | tf_op jit(solution)/shard_map/ppermute | solution.py:703
  49.0 6.9 %collective-permute-start.18 = (f32[49,256]{1,0:T(8,128)S(1)}, f32[49,256]{1,0:T(8,128)S(1)}, u32[]{:S(2)}, u32[]{:S(2)}) collective-permute-start(f32[49,256]{1,0:T(8,128)S(1)} %shard_map.132.first), channel_id=1, source_target_pairs={{0,4},{4,0},{8,12},{12,8},{1,5},{5,1},{9,13},{13,9},{2,6},{6,2},{1... | collective-permute-start | bytes 150536 | tf_op jit(solution)/shard_map/ppermute | solution.py:662
  55.9 4.4 %collective-permute-start.19 = (f32[49,256]{1,0:T(8,128)S(1)}, f32[49,256]{1,0:T(8,128)S(1)}, u32[]{:S(2)}, u32[]{:S(2)}) collective-permute-start(f32[49,256]{1,0:T(8,128)S(1)} %shard_map.133.first), channel_id=1, source_target_pairs={{0,2},{2,0},{1,3},{3,1},{4,6},{6,4},{5,7},{7,5},{8,10},{10,8},{9,1... | collective-permute-start | bytes 150536 | tf_op jit(solution)/shard_map/ppermute | solution.py:662
